TPU v7x, 32 devices: a whole 2x2x4 slice. The times are simulated.
32 devices in a mesh: rows: 8 (over y, x, core), cols: 4 (over z).
Axes of the slice: x: 2, y: 2, z: 4, core: 2. Of those that a mesh axis runs over, the one named last changes fastest.
Arguments:
- inputs: bfloat16 [8, 64, 512, 77], P(None, 'rows', 'cols'), may hold values from -6 to 6
- targets: bfloat16 [8, 64, 512, 77], P(None, 'rows', 'cols'), may hold values from -6 to 6
- land_mask: int32 [64, 512], P('rows', 'cols'), may hold values 0 or 1
- volume: float32 [64, 512], P('rows', 'cols'), as said below
- date_index: int32 [2], replicated, may hold values from 0 to 7
- perm_narrow: int32 [800], replicated, may hold values from 0 to 799, each once
- perm_wide: int32 [3200], replicated, may hold values from 0 to 3199, each once
- w_in: bfloat16 [693, 200], replicated, may hold values from -0.21875 to 0.21875
- w_down: bfloat16 [800, 800], replicated, may hold values from -0.21875 to 0.21875
- w_dw: bfloat16 [49, 800], replicated, may hold values from -0.875 to 0.875
- w_hidden: bfloat16 [800, 3200], replicated, may hold values from -0.21875 to 0.21875
- w_out: bfloat16 [3200, 800], replicated, may hold values from -0.15625 to 0.15625
- w_up: bfloat16 [800, 800], replicated, may hold values from -0.21875 to 0.21875
- w_head: bfloat16 [200, 77], replicated, may hold values from -0.4375 to 0.4375
- biases_gains: float32 [7677], replicated
- moment_first: float32 [6602752], P(('rows', 'cols')), may hold values from -0.00061035156 to 0.00061035156
- moment_second: float32 [6602752], P(('rows', 'cols')), may hold values from 1.5300997e-09 to 6.120399e-09
Outputs:
- new_w_in: float32 [693, 200], replicated
- new_w_down: float32 [800, 800], replicated
- new_w_dw: float32 [49, 800], replicated
- new_w_hidden: float32 [800, 3200], replicated
- new_w_out: float32 [3200, 800], replicated
- new_w_up: float32 [800, 800], replicated
- new_w_head: float32 [200, 77], replicated
- new_biases_gains: float32 [7677], replicated
- first_moment: float32 [6602752], P(('rows', 'cols'))
- second_moment: float32 [6602752], P(('rows', 'cols'))
- loss_sum: float32 [], replicated
- loss_weight: float32 [], replicated
- grad_norm: float32 [], replicated
Inputs may be any that keep to these rules, and one draw needn't show every extreme that they name: `perm_narrow`: each value once. `perm_wide`: each value once. `volume`: positive.
All inputs are finite; a program needn't handle non-finite values. No bound on the sum of `land_mask` on one device may be relied on, other than what follows from the above.
Results may differ from a plain program's by a relative error of at most 0.0017.
Values may be sent and summed in bfloat16 or wider, within the bound.
A program may use at most 256 MiB of HBM per device.

v0:
```python
import jax
import jax.numpy as jnp
from jax import lax
from jax.sharding import PartitionSpec as P

CI = 77
C0 = 200
C1 = 800
CH = 3200
MB = 2
STEP = 5


decay_first = 0.9
decay_second = 0.99
epsilon = 1e-08
learn_rate = 0.02
weight_decay = 0.1
clip_limit = 1.0


def padded_2(cells, sides, width):
    for axis, dim in sides:
        count = lax.axis_size(axis)
        head = lax.slice_in_dim(cells, 0, width, axis=dim)
        tail = lax.slice_in_dim(cells, cells.shape[dim] - width, cells.shape[dim], axis=dim)
        cells = jnp.concatenate(
            [
                lax.ppermute(tail, axis, [(i, (i + 1) % count) for i in range(count)]),
                cells,
                lax.ppermute(head, axis, [((i + 1) % count, i) for i in range(count)]),
            ],
            axis=dim,
        )
    return cells


def split_vector(vector):
    lengths = [C0, C1, C1, C1, C1, CH, C1, C0, CI]
    pieces = []
    start = 0
    for length in lengths:
        pieces.append(vector[start : start + length])
        start = start + length
    return pieces


def product(left, right):
    return jnp.dot(left, right, preferred_element_type=jnp.float32)


def inner_rows(left, right):
    return jnp.einsum("nk,nd->kd", left, right, preferred_element_type=jnp.float32)


def outer_cols(left, right):
    return jnp.einsum("nd,kd->nk", left, right, preferred_element_type=jnp.float32)


def column_sum(values):
    return jnp.sum(values, axis=0, dtype=jnp.float32)


def clear_edges(padded, width):
    place = lax.axis_index("rows")
    count = lax.axis_size("rows")
    line = jnp.arange(padded.shape[0])[:, None, None]
    top = (place == 0) & (line < width)
    bottom = (place == count - 1) & (line >= padded.shape[0] - width)
    return jnp.where(top | bottom, jnp.zeros((), padded.dtype), padded)


def to_coarse(field, height, breadth):
    chans = field.shape[-1]
    return (
        field.reshape(height // 2, 2, breadth // 2, 2, chans)
        .transpose(0, 2, 1, 3, 4)
        .reshape(-1, 4 * chans)
    )


def to_fine(field, height, breadth):
    chans = field.shape[-1] // 4
    return (
        field.reshape(height // 2, breadth // 2, 2, 2, chans)
        .transpose(0, 2, 1, 3, 4)
        .reshape(-1, chans)
    )


def layer_norm(values, gain, shift):
    mean = jnp.mean(values, -1, keepdims=True)
    centered = values - mean
    var = jnp.mean(centered * centered, -1, keepdims=True)
    return centered * lax.rsqrt(var + 1e-06) * gain + shift


def depthwise(padded, w_dw, height, breadth):
    total = jnp.zeros((height, breadth, padded.shape[-1]), jnp.float32)
    for shift_y in range(7):
        for shift_x in range(7):
            window = padded[shift_y : shift_y + height, shift_x : shift_x + breadth].astype(
                jnp.float32
            )
            total = total + window * w_dw[shift_y * 7 + shift_x].astype(jnp.float32)
    return total


def depthwise_kernel_grad(padded, grad_map, height, breadth):
    rows_out = []
    grad_float = grad_map.astype(jnp.float32)
    for shift_y in range(7):
        for shift_x in range(7):
            window = padded[shift_y : shift_y + height, shift_x : shift_x + breadth].astype(
                jnp.float32
            )
            rows_out.append(jnp.sum(window * grad_float, axis=(0, 1)))
    return jnp.stack(rows_out)


def depthwise_input_grad(grad_padded, w_dw, height, breadth):
    total = jnp.zeros((height, breadth, grad_padded.shape[-1]), jnp.float32)
    for shift_y in range(7):
        for shift_x in range(7):
            window = grad_padded[
                6 - shift_y : 6 - shift_y + height, 6 - shift_x : 6 - shift_x + breadth
            ].astype(jnp.float32)
            total = total + window * w_dw[shift_y * 7 + shift_x].astype(jnp.float32)
    return total


def on_device(
    inputs,
    targets,
    land_mask,
    volume,
    date_index,
    perm_narrow,
    perm_wide,
    w_in,
    w_down,
    w_dw,
    w_hidden,
    w_out,
    w_up,
    w_head,
    biases_gains,
    moment_first,
    moment_second,
):
    b_in, b_down, b_dw, gain, shift, b_hidden, b_out, b_up, b_head = split_vector(biases_gains)
    weight = land_mask.astype(jnp.float32) * volume
    height, breadth = weight.shape
    half_h, half_w = (height // 2, breadth // 2)
    weight_col = weight.reshape(-1, 1)
    matrices = (w_in, w_down, w_dw, w_hidden, w_out, w_up, w_head)

    def one_batch(carry, date):
        sums, loss = carry
        state = lax.dynamic_index_in_dim(inputs, date, 0, keepdims=False)
        target = lax.dynamic_index_in_dim(targets, date, 0, keepdims=False)
        state_pad = clear_edges(padded_2(state, (("rows", 0), ("cols", 1)), 1), 1)
        taps = jnp.concatenate(
            [state_pad[y : y + height, x : x + breadth] for y in range(3) for x in range(3)], -1
        ).reshape(-1, 9 * CI)
        a_zero = product(taps, w_in) + b_in
        h_zero, gelu_zero = jax.vjp(jax.nn.gelu, a_zero)
        h_low = h_zero.astype(jnp.bfloat16)
        patches = to_coarse(h_low.reshape(height, breadth, C0), height, breadth)
        coarse = product(patches, w_down) + b_down
        coarse_low = coarse.astype(jnp.bfloat16).reshape(half_h, half_w, C1)
        coarse_pad = clear_edges(padded_2(coarse_low, (("rows", 0), ("cols", 1)), 3), 3)
        conv_out = depthwise(coarse_pad, w_dw, half_h, half_w).reshape(-1, C1) + b_dw
        normed, norm_pull = jax.vjp(layer_norm, conv_out, gain, shift)
        normed_low = normed.astype(jnp.bfloat16)
        pre = product(normed_low, w_hidden) + b_hidden
        act, act_pull = jax.vjp(jax.nn.gelu, pre)
        act_low = act.astype(jnp.bfloat16)
        branch = product(act_low, w_out) + b_out
        mixed_low = (coarse + branch).astype(jnp.bfloat16)
        upper = product(mixed_low, w_up) + jnp.tile(b_up, 4)
        summed_low = (to_fine(upper, height, breadth) + h_zero).astype(jnp.bfloat16)
        output = product(summed_low, w_head) + b_head
        error = output - target.reshape(-1, CI).astype(jnp.float32)
        loss_here = jnp.sum(weight_col * error * error)
        grad_out = (2.0 * weight_col * error).astype(jnp.bfloat16)
        d_head = inner_rows(summed_low, grad_out)
        grad_summed = outer_cols(grad_out, w_head)
        grad_upper = to_coarse(
            grad_summed.astype(jnp.bfloat16).reshape(height, breadth, C0), height, breadth
        )
        d_up = inner_rows(mixed_low, grad_upper)
        grad_mixed = outer_cols(grad_upper, w_up)
        grad_branch = grad_mixed.astype(jnp.bfloat16)
        d_out = inner_rows(act_low, grad_branch)
        grad_act = outer_cols(grad_branch, w_out)
        grad_pre = act_pull(grad_act)[0].astype(jnp.bfloat16)
        d_hidden = inner_rows(normed_low, grad_pre)
        grad_normed = outer_cols(grad_pre, w_hidden)
        grad_conv, d_gain, d_shift = norm_pull(grad_normed)
        grad_conv = grad_conv.astype(jnp.bfloat16)
        d_dw = depthwise_kernel_grad(
            coarse_pad, grad_conv.reshape(half_h, half_w, C1), half_h, half_w
        )
        grad_pad = clear_edges(
            padded_2(grad_conv.reshape(half_h, half_w, C1), (("rows", 0), ("cols", 1)), 3), 3
        )
        grad_coarse_low = depthwise_input_grad(grad_pad, w_dw, half_h, half_w).reshape(-1, C1)
        grad_coarse = (grad_coarse_low + grad_mixed).astype(jnp.bfloat16)
        d_down = inner_rows(patches, grad_coarse)
        grad_h = to_fine(outer_cols(grad_coarse, w_down), height, breadth) + grad_summed
        grad_a = gelu_zero(grad_h)[0].astype(jnp.bfloat16)
        d_in = inner_rows(taps, grad_a)
        d_vector = jnp.concatenate(
            [
                column_sum(grad_a),
                column_sum(grad_coarse),
                column_sum(grad_conv),
                d_gain,
                d_shift,
                column_sum(grad_pre),
                column_sum(grad_branch),
                jnp.sum(column_sum(grad_upper).reshape(4, C0), 0),
                column_sum(grad_out),
            ]
        )
        terms = (d_in, d_down, d_dw, d_hidden, d_out, d_up, d_head, d_vector)
        sums = tuple((a + b for a, b in zip(sums, terms)))
        return ((sums, loss + loss_here), None)

    zeros = tuple((jnp.zeros(m.shape, jnp.float32) for m in matrices)) + (
        jnp.zeros(biases_gains.shape, jnp.float32),
    )
    (sums, loss_local), unused = lax.scan(
        one_batch, (zeros, jnp.zeros((), jnp.float32)), date_index
    )
    rotated = list(sums)
    rotated[3] = sums[3][perm_narrow][:, perm_wide]
    rotated[4] = sums[4][perm_wide][:, perm_narrow]
    flat = jnp.concatenate([g.reshape(-1) for g in rotated])
    devices = lax.axis_size(("rows", "cols"))
    share_len = moment_first.shape[0]
    lead = share_len * devices - flat.shape[0]
    flat = jnp.pad(flat, (lead, 0))
    weight_local = jnp.sum(weight)
    summed_all, loss_all, weight_all = lax.psum((flat, loss_local, weight_local), ("rows", "cols"))
    square = jnp.sum(summed_all * summed_all)
    share = lax.dynamic_slice_in_dim(
        summed_all, lax.axis_index(("rows", "cols")) * share_len, share_len
    )
    grad_norm = jnp.sqrt(square)
    clipped = share * jnp.minimum(1.0, clip_limit / grad_norm)
    first = decay_first * moment_first + (1.0 - decay_first) * clipped
    second = decay_second * moment_second + (1.0 - decay_second) * clipped * clipped
    direction = (
        first
        / (1.0 - decay_first**STEP)
        / (jnp.sqrt(second / (1.0 - decay_second**STEP)) + epsilon)
    )
    full = lax.all_gather(
        direction.astype(jnp.bfloat16), ("rows", "cols"), axis=0, tiled=True
    ).astype(direction.dtype)
    back_narrow = jnp.zeros((C1,), jnp.int32).at[perm_narrow].set(jnp.arange(C1, dtype=jnp.int32))
    back_wide = jnp.zeros((CH,), jnp.int32).at[perm_wide].set(jnp.arange(CH, dtype=jnp.int32))
    olds = matrices + (biases_gains,)
    news = []
    start = lead
    for index, old in enumerate(olds):
        count = old.size
        piece = full[start : start + count].reshape(old.shape)
        start = start + count
        if index == 3:
            piece = piece[back_narrow][:, back_wide]
        if index == 4:
            piece = piece[back_wide][:, back_narrow]
        if index < 7:
            news.append(
                old.astype(jnp.float32) * (1.0 - learn_rate * weight_decay) - learn_rate * piece
            )
        else:
            news.append(old - learn_rate * piece)
    loss_weight = MB * CI * weight_all
    return (
        news[0],
        news[1],
        news[2],
        news[3],
        news[4],
        news[5],
        news[6],
        news[7],
        first,
        second,
        loss_all,
        loss_weight,
        grad_norm,
    )


def solution(mesh):
    return jax.shard_map(
        on_device,
        mesh=mesh,
        in_specs=(
            P(None, "rows", "cols", None),
            P(None, "rows", "cols", None),
            P("rows", "cols"),
            P("rows", "cols"),
            P(),
            P(),
            P(),
            P(),
            P(),
            P(),
            P(),
            P(),
            P(),
            P(),
            P(),
            P(("rows", "cols")),
            P(("rows", "cols")),
        ),
        out_specs=(
            P(),
            P(),
            P(),
            P(),
            P(),
            P(),
            P(),
            P(),
            P(("rows", "cols")),
            P(("rows", "cols")),
            P(),
            P(),
            P(),
        ),
        check_vma=False,
    )
```

profile of v0, /device:TPU:0, one launch (start us, length us, event | category | flops | bytes accessed | tf_op | source)
XLA Modules:
  0.0 1663.2 jit_solution(4036975861214311386)
XLA Ops:
  17.9 420.4 %while.30 = (s32[]{:T(128)}, f32[693,200]{0,1:T(8,128)}, f32[800,800]{1,0:T(8,128)}, f32[49,800]{1,0:T(8,128)}, f32[800,3200]{1,0:T(8,128)}, /*index=5*/f32[3200...) while((s32[]{:T(128)}, f32[693,200]{0,1:T(8,128)}, ...), condition=%wide.region_64.65_spmd.clone, body=%wide.region_0.64_spmd.clone.sunk | while | flops 10665886720 | bytes 364747488 | solution.py:234
  33.2 4.4 collective-permute-start.2
  37.6 7.9 collective-permute-done.2
  45.5 5.6 collective-permute-done.3
  66.8 5.1 collective-permute-done.5
  81.5 8.4 add_reduce_fusion.2
  90.7 4.6 convolution_add_fusion.12
  95.4 5.4 fusion.245
  121.4 7.8 convert_reduce_fusion.69
  177.7 6.2 select_add_fusion.15
  184.1 6.0 select_add_fusion.14
  190.3 3.9 stack.499
  203.9 7.3 multiply_add_fusion.7
  238.8 12.0 collective-permute-done.2
  266.5 4.8 collective-permute-done.5
  279.5 8.4 add_reduce_fusion.2
  288.7 4.6 convolution_add_fusion.12
  293.5 5.4 fusion.245
  319.4 8.0 convert_reduce_fusion.69
  372.5 4.2 select_add_fusion.16
  376.8 10.2 select_add_fusion.15
  387.2 7.8 select_add_fusion.14
  395.2 3.9 stack.499
  410.6 7.2 multiply_add_fusion.7
  423.8 4.2 select_add_fusion.12
  444.8 4.8 reshape.862
  449.6 4.8 reshape.866
  454.3 15.7 gather_fusion
  470.1 12.3 copy.172
  482.3 17.9 %gather_fusion.1 = f32[3200,800]{1,0:T(8,128)} fusion(f32[800,3200]{0,1:T(8,128)} %copy.172, s32[4096]{0:T(1024)S(1)} %copy-done.129), kind=kCustom, calls=%fused_computation.1 | custom fusion | bytes 20492800 | tf_op jit(solution)/shard_map/gather | solution.py:238
  500.2 12.2 copy.173
  512.4 11.2 reshape.864
  523.6 12.2 copy.174
  535.9 17.9 %gather_fusion.2 = f32[3200,800]{1,0:T(8,128)} fusion(f32[3200,800]{1,0:T(8,128)} %copy.174, s32[4096]{0:T(1024)S(1)} %copy-done.129), kind=kCustom, calls=%fused_computation.2 | custom fusion | bytes 20492800 | tf_op jit(solution)/shard_map/gather | solution.py:239
  553.8 12.2 copy.175
  566.0 15.9 gather_fusion.3
  581.8 12.2 copy.176
  594.1 14.2 reshape.865
  608.3 220.4 %concatenate.59 = f32[6600877]{0:T(1024)} concatenate(f32[138600]{0:T(1024)S(1)} %copy-done.35, f32[640000]{0:T(1024)} %reshape.862, f32[39200]{0:T(1024)S(1)} %copy-done.97, f32[2560000]{0:T(1024)} %reshape.864, f32[2560000]{0:T(1024)} %reshape.865, f32[640000]{0:T(1024)} %reshape.866, f32[15400]{0:T(1024)S(1)} %copy-done.125, f32[7677]{0:T(1024)S(1)} %copy-done.40), dimensions={0} | concatenate | bytes 52807016 | tf_op jit(solution)/shard_map/concatenate | solution.py:240
  828.7 23.0 %pad.4 = f32[6602752]{0:T(1024)} pad(f32[6600877]{0:T(1024)} %concatenate.59, f32[]{:T(128)} %constant.196.clone.1), padding=1875_0 | pad | bytes 52814520 | tf_op jit(solution)/shard_map/jit(_pad)/pad | solution.py:244
  851.8 405.0 %all-reduce.4.cloned.1.call-done = f32[6602752]{0:T(1024)} async-done(((f32[6602752]{0:T(1024)}), f32[6602752]{0:T(1024)}) %all-reduce.4.cloned.1.call-update) | async-done | bytes 26411024 | tf_op jit(solution)/shard_map/psum | solution.py:246
  1256.9 10.4 multiply_reduce_fusion.3
  1271.2 5.4 reshape.1010
  1276.6 41.2 %all-reduce.1 = (f32[]{:T(128)}, f32[]{:T(128)}) all-reduce(f32[]{:T(128)} %get-tuple-element.460, f32[]{:T(128)} %get-tuple-element.914), channel_id=1, replica_groups=mesh['rows'=8,'cols'=4] {'rows','cols'}, use_global_device_ids=true, to_apply=%region_69.70 | all-reduce | flops 2 | bytes 16 | tf_op jit(solution)/shard_map/psum | solution.py:246
  1318.2 8.7 copy.178
  1326.9 5.4 scatter_custom_fusion
  1332.3 16.0 scatter_custom_fusion.1
  1349.0 88.7 %all-gather.3.cloned.1.call-done = bf16[32,1,206336]{2,1,0:T(2,128)(2,1)} async-done(((bf16[1,1,206336]{2,1,0:T(2,128)(2,1)}), bf16[32,1,206336]{2,1,0:T(2,128)(2,1)}) %all-gather.3.cloned.1.call-update) | async-done | bytes 13205520 | tf_op jit(solution)/shard_map/all_gather | solution.py:260
  1437.7 30.1 %convert_element_type.1720 = f32[32,1,206336]{2,1,0:T(1,128)S(1)} convert(bf16[32,1,206336]{2,1,0:T(2,128)(2,1)} %all-gather.3.cloned.1.call-done) | non-fusion elementwise | flops 6602752 | bytes 39616512 | tf_op jit(solution)/shard_map/convert_element_type | solution.py:262
  1472.6 9.3 fusion.137
  1486.0 4.6 mul.2188
  1490.5 13.5 reshape.869
  1504.0 17.9 %gather_fusion.6 = f32[3200,800]{1,0:T(8,128)} fusion(f32[3200,800]{1,0:T(8,128)} %reshape.869, s32[4096]{0:T(1024)S(1)} %pad_clamp_fusion), kind=kCustom, calls=%fused_computation.6 | custom fusion | bytes 20492800 | tf_op jit(solution)/shard_map/gather | solution.py:275
  1521.9 12.2 copy.180
  1534.1 16.0 gather_fusion.7
  1550.1 10.9 bitcast_subtract_fusion.1
  1561.0 4.6 mul.2172
  1565.6 11.7 reshape.868
  1577.3 15.7 gather_fusion.4
  1593.0 12.2 copy.179
  1605.3 17.9 %gather_fusion.5 = f32[3200,800]{1,0:T(8,128)} fusion(f32[800,3200]{0,1:T(8,128)} %copy.179, s32[4096]{0:T(1024)S(1)} %pad_clamp_fusion), kind=kCustom, calls=%fused_computation.5 | custom fusion | bytes 20492800 | tf_op jit(solution)/shard_map/gather | solution.py:273
  1623.2 11.8 bitcast_subtract_fusion
  1635.0 12.3 copy.183
  1647.3 6.4 multiply_subtract_fusion
  (920 shorter events, 278.9 us)
Async XLA Ops:
  7.2 1249.7 %all-reduce.4.cloned.1.call-start = ((), (), s32[]{:S(2)}) async-start(), calls=%async_computation | async-start | bytes 52822016 | tf_op jit(solution)/shard_map/psum | solution.py:246
  18.1 72.6 %copy-start.28 = (f32[800]{0:T(1024)}, f32[800]{0:T(1024)S(1)}, u32[]{:S(2)}) copy-start(f32[800]{0:T(1024)S(1)} %get-tuple-element.1505) | copy-start | bytes 9604 | tf_op jit(solution)/shard_map/while
  18.1 72.6 %copy-start.31 = (f32[800]{0:T(1024)}, f32[800]{0:T(1024)S(1)}, u32[]{:S(2)}) copy-start(f32[800]{0:T(1024)S(1)} %get-tuple-element.1506) | copy-start | bytes 9604 | tf_op jit(solution)/shard_map/while
  22.4 10.4 collective-permute-start.1
  22.9 9.9 collective-permute-start
  29.6 51.5 %copy-start.47 = (f32[800]{0:T(1024)}, f32[800]{0:T(1024)S(1)}, u32[]{:S(2)}) copy-start(f32[800]{0:T(1024)S(1)} %get-tuple-element.1330) | copy-start | bytes 9604 | tf_op jit(solution)/shard_map/while
  29.6 51.5 %copy-start.48 = (f32[800]{0:T(1024)}, f32[800]{0:T(1024)S(1)}, u32[]{:S(2)}) copy-start(f32[800]{0:T(1024)S(1)} %get-tuple-element.1301) | copy-start | bytes 9604 | tf_op jit(solution)/shard_map/while
  29.6 51.5 %copy-start.49 = (f32[800]{0:T(1024)}, f32[800]{0:T(1024)S(1)}, u32[]{:S(2)}) copy-start(f32[800]{0:T(1024)S(1)} %get-tuple-element.1302) | copy-start | bytes 9604 | tf_op jit(solution)/shard_map/while
  29.6 51.5 %copy-start.50 = (f32[800]{0:T(1024)}, f32[800]{0:T(1024)S(1)}, u32[]{:S(2)}) copy-start(f32[800]{0:T(1024)S(1)} %get-tuple-element.1303) | copy-start | bytes 9604 | tf_op jit(solution)/shard_map/while
  29.6 51.5 %copy-start.51 = (f32[800]{0:T(1024)}, f32[800]{0:T(1024)S(1)}, u32[]{:S(2)}) copy-start(f32[800]{0:T(1024)S(1)} %get-tuple-element.1304) | copy-start | bytes 9604 | tf_op jit(solution)/shard_map/while
  29.6 51.5 %copy-start.52 = (f32[800]{0:T(1024)}, f32[800]{0:T(1024)S(1)}, u32[]{:S(2)}) copy-start(f32[800]{0:T(1024)S(1)} %get-tuple-element.1305) | copy-start | bytes 9604 | tf_op jit(solution)/shard_map/while
  29.6 51.5 %copy-start.53 = (f32[800]{0:T(1024)}, f32[800]{0:T(1024)S(1)}, u32[]{:S(2)}) copy-start(f32[800]{0:T(1024)S(1)} %get-tuple-element.1306) | copy-start | bytes 9604 | tf_op jit(solution)/shard_map/while
  29.6 51.5 %copy-start.54 = (f32[800]{0:T(1024)}, f32[800]{0:T(1024)S(1)}, u32[]{:S(2)}) copy-start(f32[800]{0:T(1024)S(1)} %get-tuple-element.1307) | copy-start | bytes 9604 | tf_op jit(solution)/shard_map/while
  29.6 51.5 %copy-start.55 = (f32[800]{0:T(1024)}, f32[800]{0:T(1024)S(1)}, u32[]{:S(2)}) copy-start(f32[800]{0:T(1024)S(1)} %get-tuple-element.1308) | copy-start | bytes 9604 | tf_op jit(solution)/shard_map/while
  29.6 51.5 %copy-start.56 = (f32[800]{0:T(1024)}, f32[800]{0:T(1024)S(1)}, u32[]{:S(2)}) copy-start(f32[800]{0:T(1024)S(1)} %get-tuple-element.1309) | copy-start | bytes 9604 | tf_op jit(solution)/shard_map/while
  29.7 51.5 %copy-start.57 = (f32[800]{0:T(1024)}, f32[800]{0:T(1024)S(1)}, u32[]{:S(2)}) copy-start(f32[800]{0:T(1024)S(1)} %get-tuple-element.1310) | copy-start | bytes 9604 | tf_op jit(solution)/shard_map/while
  29.7 51.5 %copy-start.58 = (f32[800]{0:T(1024)}, f32[800]{0:T(1024)S(1)}, u32[]{:S(2)}) copy-start(f32[800]{0:T(1024)S(1)} %get-tuple-element.1311) | copy-start | bytes 9604 | tf_op jit(solution)/shard_map/while
  29.7 51.5 %copy-start.59 = (f32[800]{0:T(1024)}, f32[800]{0:T(1024)S(1)}, u32[]{:S(2)}) copy-start(f32[800]{0:T(1024)S(1)} %get-tuple-element.1312) | copy-start | bytes 9604 | tf_op jit(solution)/shard_map/while
  29.7 51.5 %copy-start.60 = (f32[800]{0:T(1024)}, f32[800]{0:T(1024)S(1)}, u32[]{:S(2)}) copy-start(f32[800]{0:T(1024)S(1)} %get-tuple-element.1313) | copy-start | bytes 9604 | tf_op jit(solution)/shard_map/while
  29.7 51.5 %copy-start.61 = (f32[800]{0:T(1024)}, f32[800]{0:T(1024)S(1)}, u32[]{:S(2)}) copy-start(f32[800]{0:T(1024)S(1)} %get-tuple-element.1314) | copy-start | bytes 9604 | tf_op jit(solution)/shard_map/while
  29.7 51.5 %copy-start.62 = (f32[800]{0:T(1024)}, f32[800]{0:T(1024)S(1)}, u32[]{:S(2)}) copy-start(f32[800]{0:T(1024)S(1)} %get-tuple-element.1315) | copy-start | bytes 9604 | tf_op jit(solution)/shard_map/while
  29.7 51.5 %copy-start.63 = (f32[800]{0:T(1024)}, f32[800]{0:T(1024)S(1)}, u32[]{:S(2)}) copy-start(f32[800]{0:T(1024)S(1)} %get-tuple-element.1316) | copy-start | bytes 9604 | tf_op jit(solution)/shard_map/while
  29.7 51.5 %copy-start.64 = (f32[800]{0:T(1024)}, f32[800]{0:T(1024)S(1)}, u32[]{:S(2)}) copy-start(f32[800]{0:T(1024)S(1)} %get-tuple-element.1317) | copy-start | bytes 9604 | tf_op jit(solution)/shard_map/while
  33.2 12.3 collective-permute-start.2
  37.6 13.5 collective-permute-start.3
  61.3 10.5 collective-permute-start.5
  61.4 10.4 collective-permute-start.4
  71.9 4.9 collective-permute-start.6
  73.7 6.8 collective-permute-start.7
  171.7 23.5 %collective-permute-start.9 = (bf16[3,64,800]{2,1,0:T(8,128)(2,1)}, bf16[3,64,800]{2,1,0:T(8,128)(2,1)S(1)}, u32[]{:S(2)}, u32[]{:S(2)}) collective-permute-start(bf16[3,64,800]{2,1,0:T(8,128)(2,1)} %bitcast.227), channel_id=1, source_target_pairs={{0,4},{4,8},{8,12},{12,16},{16,20},{20,24},{24,28},{28,0},{1,5},{5... | collective-permute-start | bytes 921608 | tf_op jit(solution)/shard_map/while/body/eval_jaxpr/ppermute | solution.py:29
  171.7 23.6 %collective-permute-start.8 = (bf16[3,64,800]{2,1,0:T(8,128)(2,1)}, bf16[3,64,800]{2,1,0:T(8,128)(2,1)S(1)}, u32[]{:S(2)}, u32[]{:S(2)}) collective-permute-start(bf16[3,64,800]{2,1,0:T(8,128)(2,1)} %bitcast.257), channel_id=1, source_target_pairs={{4,0},{8,4},{12,8},{16,12},{20,16},{24,20},{28,24},{0,28},{5,1},{9... | collective-permute-start | bytes 921608 | tf_op jit(solution)/shard_map/while/body/eval_jaxpr/ppermute | solution.py:31
  195.3 4.5 collective-permute-start.10
  196.1 6.1 collective-permute-start.11
  222.3 66.4 %copy-start.28 = (f32[800]{0:T(1024)}, f32[800]{0:T(1024)S(1)}, u32[]{:S(2)}) copy-start(f32[800]{0:T(1024)S(1)} %get-tuple-element.1505) | copy-start | bytes 9604 | tf_op jit(solution)/shard_map/while
  222.3 66.4 %copy-start.31 = (f32[800]{0:T(1024)}, f32[800]{0:T(1024)S(1)}, u32[]{:S(2)}) copy-start(f32[800]{0:T(1024)S(1)} %get-tuple-element.1506) | copy-start | bytes 9604 | tf_op jit(solution)/shard_map/while
  226.6 9.7 collective-permute-start.1
  226.7 9.6 collective-permute-start
  233.1 46.0 %copy-start.52 = (f32[800]{0:T(1024)}, f32[800]{0:T(1024)S(1)}, u32[]{:S(2)}) copy-start(f32[800]{0:T(1024)S(1)} %get-tuple-element.1305) | copy-start | bytes 9604 | tf_op jit(solution)/shard_map/while
  233.1 46.0 %copy-start.53 = (f32[800]{0:T(1024)}, f32[800]{0:T(1024)S(1)}, u32[]{:S(2)}) copy-start(f32[800]{0:T(1024)S(1)} %get-tuple-element.1306) | copy-start | bytes 9604 | tf_op jit(solution)/shard_map/while
  233.2 46.0 %copy-start.54 = (f32[800]{0:T(1024)}, f32[800]{0:T(1024)S(1)}, u32[]{:S(2)}) copy-start(f32[800]{0:T(1024)S(1)} %get-tuple-element.1307) | copy-start | bytes 9604 | tf_op jit(solution)/shard_map/while
  233.2 46.0 %copy-start.55 = (f32[800]{0:T(1024)}, f32[800]{0:T(1024)S(1)}, u32[]{:S(2)}) copy-start(f32[800]{0:T(1024)S(1)} %get-tuple-element.1308) | copy-start | bytes 9604 | tf_op jit(solution)/shard_map/while
  233.2 46.0 %copy-start.56 = (f32[800]{0:T(1024)}, f32[800]{0:T(1024)S(1)}, u32[]{:S(2)}) copy-start(f32[800]{0:T(1024)S(1)} %get-tuple-element.1309) | copy-start | bytes 9604 | tf_op jit(solution)/shard_map/while
  233.2 46.0 %copy-start.57 = (f32[800]{0:T(1024)}, f32[800]{0:T(1024)S(1)}, u32[]{:S(2)}) copy-start(f32[800]{0:T(1024)S(1)} %get-tuple-element.1310) | copy-start | bytes 9604 | tf_op jit(solution)/shard_map/while
  233.2 46.0 %copy-start.58 = (f32[800]{0:T(1024)}, f32[800]{0:T(1024)S(1)}, u32[]{:S(2)}) copy-start(f32[800]{0:T(1024)S(1)} %get-tuple-element.1311) | copy-start | bytes 9604 | tf_op jit(solution)/shard_map/while
  233.2 46.0 %copy-start.59 = (f32[800]{0:T(1024)}, f32[800]{0:T(1024)S(1)}, u32[]{:S(2)}) copy-start(f32[800]{0:T(1024)S(1)} %get-tuple-element.1312) | copy-start | bytes 9604 | tf_op jit(solution)/shard_map/while
  233.2 46.0 %copy-start.60 = (f32[800]{0:T(1024)}, f32[800]{0:T(1024)S(1)}, u32[]{:S(2)}) copy-start(f32[800]{0:T(1024)S(1)} %get-tuple-element.1313) | copy-start | bytes 9604 | tf_op jit(solution)/shard_map/while
  233.2 46.0 %copy-start.61 = (f32[800]{0:T(1024)}, f32[800]{0:T(1024)S(1)}, u32[]{:S(2)}) copy-start(f32[800]{0:T(1024)S(1)} %get-tuple-element.1314) | copy-start | bytes 9604 | tf_op jit(solution)/shard_map/while
  233.2 46.0 %copy-start.62 = (f32[800]{0:T(1024)}, f32[800]{0:T(1024)S(1)}, u32[]{:S(2)}) copy-start(f32[800]{0:T(1024)S(1)} %get-tuple-element.1315) | copy-start | bytes 9604 | tf_op jit(solution)/shard_map/while
  236.7 14.1 collective-permute-start.2
  236.9 13.8 collective-permute-start.3
  261.0 10.3 collective-permute-start.5
  261.1 10.2 collective-permute-start.4
  271.4 4.4 collective-permute-start.6
  272.0 6.5 collective-permute-start.7
  369.9 31.2 %collective-permute-start.9 = (bf16[3,64,800]{2,1,0:T(8,128)(2,1)}, bf16[3,64,800]{2,1,0:T(8,128)(2,1)S(1)}, u32[]{:S(2)}, u32[]{:S(2)}) collective-permute-start(bf16[3,64,800]{2,1,0:T(8,128)(2,1)} %bitcast.227), channel_id=1, source_target_pairs={{0,4},{4,8},{8,12},{12,16},{16,20},{20,24},{24,28},{28,0},{1,5},{5... | collective-permute-start | bytes 921608 | tf_op jit(solution)/shard_map/while/body/eval_jaxpr/ppermute | solution.py:29
  369.9 31.2 %collective-permute-start.8 = (bf16[3,64,800]{2,1,0:T(8,128)(2,1)}, bf16[3,64,800]{2,1,0:T(8,128)(2,1)S(1)}, u32[]{:S(2)}, u32[]{:S(2)}) collective-permute-start(bf16[3,64,800]{2,1,0:T(8,128)(2,1)} %bitcast.257), channel_id=1, source_target_pairs={{4,0},{8,4},{12,8},{16,12},{20,16},{24,20},{28,24},{0,28},{5,1},{9... | collective-permute-start | bytes 921608 | tf_op jit(solution)/shard_map/while/body/eval_jaxpr/ppermute | solution.py:31
  401.2 5.2 collective-permute-start.10
  402.8 6.1 collective-permute-start.11
  851.8 585.9 %all-gather.3.cloned.1.call-start = ((), (), s32[]{:S(2)}) async-start(), calls=%async_computation.1 | async-start | bytes 27236352 | tf_op jit(solution)/shard_map/all_gather | solution.py:260
  851.8 416.2 %copy-start.95 = (f32[206336]{0:T(1024)S(1)}, f32[206336]{0:T(1024)}, u32[]{:S(2)}) copy-start(f32[206336]{0:T(1024)} %param.34) | copy-start | bytes 2476036
  851.8 416.2 %copy-start.96 = (f32[206336]{0:T(1024)S(1)}, f32[206336]{0:T(1024)}, u32[]{:S(2)}) copy-start(f32[206336]{0:T(1024)} %param.35) | copy-start | bytes 2476036
  1268.1 49.8 %copy-start.37 = (bf16[200,77]{0,1:T(8,128)(2,1)S(1)}, bf16[200,77]{0,1:T(8,128)(2,1)}, u32[]{:S(2)}) copy-start(bf16[200,77]{0,1:T(8,128)(2,1)} %get-tuple-element.1558) | copy-start | bytes 92404
  1268.1 49.9 %copy-start.124 = (bf16[693,200]{0,1:T(8,128)(2,1)S(1)}, bf16[693,200]{0,1:T(8,128)(2,1)}, u32[]{:S(2)}) copy-start(bf16[693,200]{0,1:T(8,128)(2,1)} %get-tuple-element.1562) | copy-start | bytes 831604
  1349.0 118.7 %copy-start.128 = (f32[7677]{0:T(1024)S(1)}, f32[7677]{0:T(1024)}, u32[]{:S(2)}) copy-start(f32[7677]{0:T(1024)} %param.33) | copy-start | bytes 92128
  (233 other events, 2311.2 us)
Sparse Core Ops, SparseCore 0:
  851.9 404.9 all-reduce.3
  1276.7 160.9 all-gather.2
where the time goes:
time: 1690 us; the launch traced here: 1660 us
  local copies, waits for them, and re-layouts  729 us (43%)
  waiting for transfers between devices  545 us (32%)
  other arithmetic  163 us (10%)
  matrix products  116 us (7%)
  blocking collectives  41.2 us (2%)
  starting transfers between devices  32.4 us (2%)
  between operations  18.4 us (1%)
  loops' own time  17.6 us (1%)
    psum x1, waiting for transfers between devices, on_device(): lax.psum((flat, loss_local, weight_local), ('rows', 'cols'))  405 us
    concatenate x1, local copies, waits for them, and re-layouts, on_device(): flat = jnp.concatenate([g.reshape(-1) for g in rotated])  220 us
    all_gather x1, waiting for transfers between devices, on_device(): lax.all_gather(direction.astype(jnp.bfloat16), ('rows', 'cols'), axis=0,...  88.7 us
    another operation x100, local copies, waits for them, and re-layouts, depthwise_kernel_grad(): return jnp.stack(rows_out)  62 us
    gather x4, local copies, waits for them, and re-layouts, on_device(): rotated[4] = sums[4][perm_wide][:, perm_narrow]  58.2 us
    gather x4, local copies, waits for them, and re-layouts, on_device(): rotated[3] = sums[3][perm_narrow][:, perm_wide]  58.1 us
    dot_general x12, matrix products, inner_rows(): jnp.einsum('nk,nd->kd', left, right, preferred_element_type=jnp.float32)  46.4 us
    gather x3, local copies, waits for them, and re-layouts, on_device(): piece = piece[back_wide][:, back_narrow]  46.1 us
  transfers between devices with their start and end apart: 26, of which 15 were waited for; matrix products, arithmetic and copies ran while one was open for 6% of the time, Pallas kernels for 0%

commit v1 on v0

v1 whole, which is shorter than its diff:
```python
import functools

import jax
import jax.numpy as jnp
from jax import lax
from jax.experimental import pallas as pl
from jax.experimental.pallas import tpu as pltpu
from jax.sharding import PartitionSpec as P

CI = 77
C0 = 200
C1 = 800
CH = 3200
MB = 2
STEP = 5
LANES = 128
MESH = pl.DeviceIdType.MESH
ROUNDER = 12582912.0

decay_first = 0.9
decay_second = 0.99
epsilon = 1e-08
learn_rate = 0.02
weight_decay = 0.1
clip_limit = 1.0

VEC = 4 * C1 + CH + C1 + 2 * C0 + CI
SIZES = (9 * CI * C0, 4 * C0 * C1, 49 * C1, C1 * CH, CH * C1, C1 * 4 * C0, C0 * CI, VEC)
PADDED = 6602752
FLAT_AT = []
ROW_AT = []
for size in SIZES:
    flat_here = FLAT_AT[-1] + SIZES[len(FLAT_AT) - 1] if FLAT_AT else PADDED - sum(SIZES)
    row_here = ROW_AT[-1] + -(-SIZES[len(ROW_AT) - 1] // 1024) * 8 if ROW_AT else 0
    row_here = max(row_here, -(-flat_here // 1024) * 8)
    FLAT_AT.append(flat_here)
    ROW_AT.append(row_here)
SHIFTS = []
for flat_here, row_here, size in zip(FLAT_AT, ROW_AT, SIZES):
    moved = divmod(row_here * LANES - flat_here, LANES)
    if SHIFTS and SHIFTS[-1][:2] == moved:
        SHIFTS[-1] = moved + (SHIFTS[-1][2], flat_here + size)
    else:
        SHIFTS.append(moved + (flat_here, flat_here + size))
MAX_SHIFT = max(s[0] for s in SHIFTS) + 1


def bit_masks(bits):
    masks = [()]
    for bit in bits:
        masks = masks + [m + (bit,) for m in masks]
    return sorted(masks, key=lambda m: -len(m))


class Plan:
    def __init__(self, rows, cols, total):
        self.rows, self.cols, self.count = rows, cols, rows * cols
        self.share = total // LANES // self.count
        self.bits = rows.bit_length() - 1
        need = 7 + self.share + MAX_SHIFT + 1
        self.block = 64 if need > 1024 else 32
        self.window = -(-need // (2 * self.block)) * 2 * self.block
        self.part = self.window // 2
        self.blocks = self.part // self.block
        self.scales = self.blocks
        upper = list(range(1, self.bits))
        self.orders = [upper, upper[1:] + upper[:1]]
        self.stages = len(upper)
        self.space = (self.share * (self.count - 1)) // 8 * 8 + self.window
        self.padded = -(-self.share // 16) * 16
        cut = -(-self.padded // 32) * 16
        self.cuts = [(0, cut), (cut, self.padded - cut)]
        self.local = self.count // 2


def exchange_kernel(
    plan, grad, m_first, m_second, extra, full, first, second, totals,
    acc, near, q_send, q_recv, s_send, s_recv, z_send, z_recv, zs_send, zs_recv,
    rolled, step, low, stats,
    sem_load, sem_near_s, sem_near_r, sem_qs, sem_qr, sem_ss, sem_sr,
    sem_zs, sem_zr, sem_zss, sem_zsr, sem_ts, sem_tr, sem_own,
    sem_gs, sem_gr, sem_hs, sem_hr, sem_cs, sem_cr,
):
    nr, nc, n = plan.rows, plan.cols, plan.count
    r = lax.axis_index("rows")
    c = lax.axis_index("cols")
    me = r * nc + c
    part, window, share = plan.part, plan.window, plan.share

    def flipped(mask):
        out = r
        for bit in mask:
            here = (r // (1 << bit)) % 2
            out = out + (1 - 2 * here) * (1 << bit)
        return out

    def remote(src, dst, send, recv, row, col):
        return pltpu.make_async_remote_copy(
            src_ref=src, dst_ref=dst, send_sem=send, recv_sem=recv,
            device_id=(row, col), device_id_type=MESH,
        )

    barrier = pltpu.get_barrier_semaphore()

    def greet(d, carry):
        k = lax.rem(me + d, n)
        pl.semaphore_signal(barrier, inc=1, device_id=(k // nc, k % nc), device_id_type=MESH)
        return carry

    lax.fori_loop(1, n, greet, 0)
    pl.semaphore_wait(barrier, n - 1)

    upper = list(range(1, plan.bits))
    masks = bit_masks(upper)

    def local_index(mask, col):
        return (flipped(mask) // 2) * nc + col

    def window_start(row, col):
        return pl.multiple_of((share * (row * nc + col)) // 8 * 8, 8)

    def near_copy(mask, col):
        row = flipped(mask + (0,))
        return remote(
            grad.at[pl.ds(window_start(row, col), window)],
            near.at[local_index(mask, col)],
            sem_near_s.at[local_index(mask, col)], sem_near_r.at[local_index(mask, col)],
            flipped((0,)), c,
        )

    def load_copy(mask, col):
        index = local_index(mask, col)
        return pltpu.make_async_copy(
            grad.at[pl.ds(window_start(flipped(mask), col), window)], acc.at[index], sem_load.at[index]
        )

    for mask in masks:
        def begin(col, carry, mask=mask):
            near_copy(mask, col).start()
            load_copy(mask, col).start()
            return carry

        lax.fori_loop(0, nc, begin, 0)

    def encode(index, p, q_ref, s_ref):
        def body(b, carry):
            at = pl.ds(pl.multiple_of(b * plan.block, plan.block), plan.block)
            rows_at = pl.ds(pl.multiple_of(p * part + b * plan.block, 8), plan.block)
            values = acc[index, rows_at, :]
            top = jnp.maximum(jnp.max(jnp.abs(values), axis=0, keepdims=True), 1e-30)
            scaled = values * (32766.0 / top)
            scaled = (scaled + ROUNDER) - ROUNDER
            q_ref[at, :] = scaled.astype(jnp.int32).astype(jnp.int16)
            s_ref[pl.ds(b, 1), :] = top * (1.0 / 32766.0)
            return carry

        lax.fori_loop(0, plan.blocks, body, 0)

    def decode(index, p, q_ref, s_ref):
        def body(b, carry):
            at = pl.ds(pl.multiple_of(b * plan.block, plan.block), plan.block)
            rows_at = pl.ds(pl.multiple_of(p * part + b * plan.block, 8), plan.block)
            acc[index, rows_at, :] += q_ref[at, :].astype(jnp.float32) * s_ref[pl.ds(b, 1), :]
            return carry

        lax.fori_loop(0, plan.blocks, body, 0)

    def stage_base(stage):
        return sum((1 << (plan.stages - 1 - s)) for s in range(stage)) * nc

    def hop(p, stage, slot):
        row = flipped((plan.orders[p][stage],))
        at = stage_base(stage) + slot
        return (
            remote(q_send.at[p, at], q_recv.at[p, at], sem_qs.at[p, at], sem_qr.at[p, at], row, c),
            remote(s_send.at[p, at], s_recv.at[p, at], sem_ss.at[p, at], sem_sr.at[p, at], row, c),
        )

    def send_stage(p, stage, number, mask, col):
        bit = plan.orders[p][stage]
        index = local_index(mask + (bit,), col)
        slot = number * nc + col
        at = stage_base(stage) + slot
        encode(index, p, q_send.at[p, at], s_send.at[p, at])
        for copy in hop(p, stage, slot):
            copy.start()

    def take_stage(p, stage, number, mask, col):
        slot = number * nc + col
        for copy in hop(p, stage, slot):
            copy.wait_recv()
        at = stage_base(stage) + slot
        decode(local_index(mask, col), p, q_recv.at[p, at], s_recv.at[p, at])

    def free_masks(p, stage):
        rest = plan.orders[p][stage + 1 :]
        found = bit_masks(rest)
        if rest:
            found = [m for m in found if rest[0] in m] + [m for m in found if rest[0] not in m]
        return found

    for mask in masks:
        def join(col, carry, mask=mask):
            index = local_index(mask, col)
            near_copy(mask, col).wait_recv()
            load_copy(mask, col).wait()

            def body(b, inner):
                at = pl.ds(pl.multiple_of(b * plan.block, plan.block), plan.block)
                acc[index, at, :] += near[index, at, :]
                return inner

            lax.fori_loop(0, 2 * plan.blocks, body, 0)
            for p in range(2):
                bit = plan.orders[p][0]
                if bit in mask:
                    rest = tuple(b for b in mask if b != bit)
                    options = free_masks(p, 0)
                    number = [sorted(o) for o in options].index(sorted(rest))
                    send_stage(p, 0, number, rest, col)
            return carry

        lax.fori_loop(0, nc, join, 0)

    def far_copy(p, d):
        col = lax.rem(c + d, nc)
        return (
            remote(z_send.at[p, d - 1], z_recv.at[p, d - 1], sem_zs.at[p, d - 1], sem_zr.at[p, d - 1], r, col),
            remote(zs_send.at[p, d - 1], zs_recv.at[p, d - 1], sem_zss.at[p, d - 1], sem_zsr.at[p, d - 1], r, col),
        )

    for stage in range(plan.stages):
        for number in range(1 << (plan.stages - 1 - stage)):
            def take(d, carry, stage=stage, number=number):
                col = lax.rem(c + d, nc)
                for p in range(2):
                    mask = free_masks(p, stage)[number]
                    take_stage(p, stage, number, mask, col)
                    if stage + 1 < plan.stages:
                        bit = plan.orders[p][stage + 1]
                        if bit in mask:
                            rest = tuple(b for b in mask if b != bit)
                            options = free_masks(p, stage + 1)
                            following = [sorted(o) for o in options].index(sorted(rest))
                            send_stage(p, stage + 1, following, rest, col)
                return carry

            if stage + 1 < plan.stages:
                lax.fori_loop(1, nc + 1, take, 0)
            else:
                def take_last(d, carry, take=take):
                    take(d, 0)
                    col = lax.rem(c + d, nc)
                    for p in range(2):
                        encode(local_index((), col), p, z_send.at[p, d - 1], zs_send.at[p, d - 1])
                        for copy in far_copy(p, d):
                            copy.start()
                    return carry

                lax.fori_loop(1, nc, take_last, 0)
                take(nc, 0)

    mine = local_index((), c)

    def gather_far(d, carry):
        for p in range(2):
            for copy in far_copy(p, d):
                copy.wait_recv()
            decode(mine, p, z_recv.at[p, d - 1], zs_recv.at[p, d - 1])
        return carry

    lax.fori_loop(1, nc, gather_far, 0)

    offset = lax.rem(share * me, 8)
    for number, (shift_rows, shift_lanes, begin, end) in enumerate(SHIFTS):
        def turn(b, carry, number=number, shift_lanes=shift_lanes):
            at = pl.ds(pl.multiple_of(b * plan.block, plan.block), plan.block)
            rolled[number, at, :] = pltpu.roll(acc[mine, at, :], LANES - shift_lanes, 1)
            return carry

        lax.fori_loop(0, 2 * plan.blocks, turn, 0)

    def share_rows(start, length):
        lane = lax.broadcasted_iota(jnp.int32, (length, LANES), 1)
        line = lax.broadcasted_iota(jnp.int32, (length, LANES), 0)
        flat = (share * me + start + line) * LANES + lane
        out = jnp.zeros((length, LANES), jnp.float32)
        for number, (shift_rows, shift_lanes, begin, end) in enumerate(SHIFTS):
            here = rolled[number, pl.ds(offset + start + shift_rows, length), :]
            after = rolled[number, pl.ds(offset + start + shift_rows + 1, length), :]
            value = jnp.where(lane < LANES - shift_lanes, here, after)
            out = jnp.where((flat >= begin) & (flat < end), value, out)
        return out

    chunk = 32
    whole, tail = share // chunk, share % chunk

    def square(b, total):
        start = pl.multiple_of(b * chunk, chunk)
        value = share_rows(start, chunk)
        step[pl.ds(start, chunk), :] = value
        return total + jnp.sum((value * value).reshape(chunk // 8, 8, LANES), axis=0)

    total = lax.fori_loop(0, whole, square, jnp.zeros((8, LANES), jnp.float32))
    stats[me, 8:16, :] = extra[...]
    stats[me, 0:8, :] = total
    if tail:
        value = share_rows(whole * chunk, tail)
        step[whole * chunk : share, :] = value
        stats[me, 0:1, :] += jnp.sum(value * value, axis=0, keepdims=True)

    def stat_copy(target, source):
        return remote(
            stats.at[me], stats.at[me], sem_ts.at[target], sem_tr.at[me], target // nc, target % nc
        )

    def stat_wait(source):
        return remote(
            stats.at[source], stats.at[source], sem_ts.at[source], sem_tr.at[source],
            source // nc, source % nc,
        )

    def send_stat(d, carry):
        stat_copy(lax.rem(me + d, n), me).start()
        return carry

    lax.fori_loop(1, n, send_stat, 0)

    def wait_stat(d, carry):
        stat_wait(lax.rem(me + d, n)).wait_recv()
        return carry

    lax.fori_loop(1, n, wait_stat, 0)

    def add_stat(k, total):
        return total + stats[k]

    sums = lax.fori_loop(0, n, add_stat, jnp.zeros((16, LANES), jnp.float32))
    norm = jnp.sqrt(jnp.sum(sums[0:8], keepdims=True))
    totals[0:8, :] = sums[8:16]
    totals[8:16, :] = jnp.broadcast_to(norm, (8, LANES))
    clip = jnp.minimum(1.0, clip_limit / norm)

    def update(start, length):
        clipped = step[pl.ds(start, length), :] * clip
        one = decay_first * m_first[pl.ds(start, length), :] + (1.0 - decay_first) * clipped
        two = decay_second * m_second[pl.ds(start, length), :] + (1.0 - decay_second) * clipped * clipped
        first[pl.ds(start, length), :] = one
        second[pl.ds(start, length), :] = two
        step[pl.ds(start, length), :] = (
            one / (1.0 - decay_first**STEP) / (jnp.sqrt(two / (1.0 - decay_second**STEP)) + epsilon)
        )

    def update_chunk(b, carry):
        update(pl.multiple_of(b * chunk, chunk), chunk)
        return carry

    lax.fori_loop(0, whole, update_chunk, 0)
    if tail:
        update(whole * chunk, tail)
    if plan.padded > share:
        step[share : plan.padded, :] = jnp.zeros((plan.padded - share, LANES), jnp.float32)

    def narrow(b, carry):
        at = pl.ds(pl.multiple_of(b * 16, 16), 16)
        low[at, :] = step[at, :].astype(jnp.bfloat16)
        return carry

    lax.fori_loop(0, plan.padded // 16, narrow, 0)

    own = pltpu.make_async_copy(low, full.at[me], sem_own)
    own.start()
    own.wait()

    back = [list(reversed(order)) for order in plan.orders]

    def piece(mask, col, p):
        begin, length = plan.cuts[p]
        return full.at[flipped(mask) * nc + col, pl.ds(begin, length)]

    def along(direction, col, p, receive):
        step_col = 1 if direction == 0 else -1
        target = c - step_col if receive else c + step_col
        ref = piece((), col, p)
        return remote(ref, ref, sem_gs.at[direction, col, p], sem_gr.at[direction, col, p], r, target)

    def gather_masks(p, stage):
        return bit_masks(back[p][:stage])

    def gather_base(stage):
        return sum(1 << s for s in range(stage)) * nc

    def across(p, stage, number, mask, col):
        at = gather_base(stage) + number * nc + col
        ref = piece(mask, col, p)
        return remote(ref, ref, sem_hs.at[p, at], sem_hr.at[p, at], flipped((back[p][stage],)), c)

    def across_recv(p, stage, number, mask, col):
        at = gather_base(stage) + number * nc + col
        ref = piece(mask + (back[p][stage],), col, p)
        return remote(ref, ref, sem_hs.at[p, at], sem_hr.at[p, at], flipped((back[p][stage],)), c)

    def inward(p, mask, col):
        number = masks.index(tuple(sorted(mask)))
        at = number * nc + col
        ref = piece(mask, col, p)
        return remote(ref, ref, sem_cs.at[p, at], sem_cr.at[p, at], flipped((0,)), c)

    def inward_recv(p, mask, col):
        number = masks.index(tuple(sorted(mask)))
        at = number * nc + col
        ref = piece(mask + (0,), col, p)
        return remote(ref, ref, sem_cs.at[p, at], sem_cr.at[p, at], flipped((0,)), c)

    def spread(p, mask, col, stage):
        for later in range(stage, plan.stages):
            options = [sorted(o) for o in gather_masks(p, later)]
            if sorted(mask) in options:
                across(p, later, options.index(sorted(mask)), mask, col).start()
        inward(p, mask, col).start()

    def near_cols(t):
        if t == 0:
            return [(0, c)]
        return [(0, c - t), (1, c + t)]

    def inside(col):
        return (col >= 0) & (col < nc)

    for time in range(nc + plan.stages):
        for stage in range(plan.stages + 1):
            t = time - stage
            if not 0 <= t < nc:
                continue
            if stage == 0:
                if t == 0:
                    for p in range(2):
                        @pl.when(c < nc - 1)
                        def _(p=p):
                            along(0, c, p, False).start()

                        @pl.when(c > 0)
                        def _(p=p):
                            along(1, c, p, False).start()

                        spread(p, (), c, 0)
                else:
                    for direction, col in near_cols(t):
                        @pl.when(inside(col))
                        def _(direction=direction, col=col):
                            for p in range(2):
                                along(direction, col, p, True).wait_recv()
                                if direction == 0:
                                    @pl.when(c < nc - 1)
                                    def _():
                                        along(0, col, p, False).start()
                                else:
                                    @pl.when(c > 0)
                                    def _():
                                        along(1, col, p, False).start()
                                spread(p, (), col, 0)
            else:
                for direction, col in near_cols(t):
                    @pl.when(inside(col))
                    def _(col=col, stage=stage):
                        for number in range(1 << (stage - 1)):
                            for p in range(2):
                                mask = gather_masks(p, stage - 1)[number]
                                across_recv(p, stage - 1, number, mask, col).wait_recv()
                                spread(p, mask + (back[p][stage - 1],), col, stage)

    for mask in masks:
        def finish(col, carry, mask=mask):
            for p in range(2):
                inward_recv(p, mask, col).wait_recv()
                inward(p, mask, col).wait_send()
            near_copy(mask, col).wait_send()
            return carry

        lax.fori_loop(0, nc, finish, 0)
    for p in range(2):
        for stage in range(plan.stages):
            for number, mask in enumerate(gather_masks(p, stage)):
                def sent(col, carry, p=p, stage=stage, number=number, mask=mask):
                    across(p, stage, number, mask, col).wait_send()
                    return carry

                lax.fori_loop(0, nc, sent, 0)
            for number in range(1 << (plan.stages - 1 - stage)):
                def left(col, carry, p=p, stage=stage, number=number):
                    for copy in hop(p, stage, number * nc + col):
                        copy.wait_send()
                    return carry

                lax.fori_loop(0, nc, left, 0)

        def gone(col, carry, p=p):
            @pl.when((col <= c) & (c < nc - 1))
            def _():
                along(0, col, p, False).wait_send()

            @pl.when((col >= c) & (c > 0))
            def _():
                along(1, col, p, False).wait_send()

            return carry

        lax.fori_loop(0, nc, gone, 0)

        def far_gone(d, carry, p=p):
            for copy in far_copy(p, d):
                copy.wait_send()
            return carry

        lax.fori_loop(1, nc, far_gone, 0)

    def stat_gone(d, carry):
        stat_copy(lax.rem(me + d, n), me).wait_send()
        return carry

    lax.fori_loop(1, n, stat_gone, 0)


def exchange(rows, cols, grad, m_first, m_second, extra):
    plan = Plan(rows, cols, m_first.size * rows * cols)
    n, nc, share = plan.count, plan.cols, plan.share
    hops = sum(1 << s for s in range(plan.stages)) * nc
    dma = pltpu.SemaphoreType.DMA
    far = max(nc - 1, 1)
    vmem = pl.BlockSpec(memory_space=pltpu.VMEM)
    hbm = pl.BlockSpec(memory_space=pl.ANY)
    return plan, pl.pallas_call(
        functools.partial(exchange_kernel, plan),
        out_shape=(
            jax.ShapeDtypeStruct((n, plan.padded, LANES), jnp.bfloat16),
            jax.ShapeDtypeStruct((share, LANES), jnp.float32),
            jax.ShapeDtypeStruct((share, LANES), jnp.float32),
            jax.ShapeDtypeStruct((16, LANES), jnp.float32),
        ),
        in_specs=[hbm, vmem, vmem, vmem],
        out_specs=(hbm, vmem, vmem, vmem),
        scratch_shapes=[
            pltpu.VMEM((plan.local, plan.window, LANES), jnp.float32),
            pltpu.VMEM((plan.local, plan.window, LANES), jnp.float32),
            pltpu.VMEM((2, hops, plan.part, LANES), jnp.int16),
            pltpu.VMEM((2, hops, plan.part, LANES), jnp.int16),
            pltpu.VMEM((2, hops, plan.scales, LANES), jnp.float32),
            pltpu.VMEM((2, hops, plan.scales, LANES), jnp.float32),
            pltpu.VMEM((2, far, plan.part, LANES), jnp.int16),
            pltpu.VMEM((2, far, plan.part, LANES), jnp.int16),
            pltpu.VMEM((2, far, plan.scales, LANES), jnp.float32),
            pltpu.VMEM((2, far, plan.scales, LANES), jnp.float32),
            pltpu.VMEM((len(SHIFTS), plan.window, LANES), jnp.float32),
            pltpu.VMEM((plan.padded, LANES), jnp.float32),
            pltpu.VMEM((plan.padded, LANES), jnp.bfloat16),
            pltpu.VMEM((n, 16, LANES), jnp.float32),
            dma((plan.local,)), dma((plan.local,)), dma((plan.local,)),
            dma((2, hops)), dma((2, hops)), dma((2, hops)), dma((2, hops)),
            dma((2, far)), dma((2, far)), dma((2, far)), dma((2, far)),
            dma((n,)), dma((n,)), dma,
            dma((2, nc, 2)), dma((2, nc, 2)),
            dma((2, hops)), dma((2, hops)),
            dma((2, plan.local)), dma((2, plan.local)),
        ],
        compiler_params=pltpu.CompilerParams(
            collective_id=0, has_side_effects=True, vmem_limit_bytes=56 << 20
        ),
    )(grad, m_first.reshape(share, LANES), m_second.reshape(share, LANES), extra)


def padded_2(cells, sides, width):
    for axis, dim in sides:
        count = lax.axis_size(axis)
        head = lax.slice_in_dim(cells, 0, width, axis=dim)
        tail = lax.slice_in_dim(cells, cells.shape[dim] - width, cells.shape[dim], axis=dim)
        cells = jnp.concatenate(
            [
                lax.ppermute(tail, axis, [(i, (i + 1) % count) for i in range(count)]),
                cells,
                lax.ppermute(head, axis, [((i + 1) % count, i) for i in range(count)]),
            ],
            axis=dim,
        )
    return cells


def split_vector(vector):
    lengths = [C0, C1, C1, C1, C1, CH, C1, C0, CI]
    pieces = []
    start = 0
    for length in lengths:
        pieces.append(vector[start : start + length])
        start = start + length
    return pieces


def product(left, right):
    return jnp.dot(left, right, preferred_element_type=jnp.float32)


def inner_rows(left, right):
    return jnp.einsum("nk,nd->kd", left, right, preferred_element_type=jnp.float32)


def outer_cols(left, right):
    return jnp.einsum("nd,kd->nk", left, right, preferred_element_type=jnp.float32)


def column_sum(values):
    return jnp.sum(values, axis=0, dtype=jnp.float32)


def clear_edges(padded, width):
    place = lax.axis_index("rows")
    count = lax.axis_size("rows")
    line = jnp.arange(padded.shape[1])[None, :, None, None]
    top = (place == 0) & (line < width)
    bottom = (place == count - 1) & (line >= padded.shape[1] - width)
    return jnp.where(top | bottom, jnp.zeros((), padded.dtype), padded)


def to_coarse(field, height, breadth):
    chans = field.shape[-1]
    return (
        field.reshape(MB, height // 2, 2, breadth // 2, 2, chans)
        .transpose(0, 1, 3, 2, 4, 5)
        .reshape(-1, 4 * chans)
    )


def to_fine(field, height, breadth):
    chans = field.shape[-1] // 4
    return (
        field.reshape(MB, height // 2, breadth // 2, 2, 2, chans)
        .transpose(0, 1, 3, 2, 4, 5)
        .reshape(-1, chans)
    )


def layer_norm(values, gain, shift):
    mean = jnp.mean(values, -1, keepdims=True)
    centered = values - mean
    var = jnp.mean(centered * centered, -1, keepdims=True)
    return centered * lax.rsqrt(var + 1e-06) * gain + shift


def depthwise(padded, w_dw, height, breadth, back):
    total = jnp.zeros((MB, height, breadth, padded.shape[-1]), jnp.float32)
    for y in range(7):
        for x in range(7):
            at_y, at_x = (6 - y, 6 - x) if back else (y, x)
            window = padded[:, at_y : at_y + height, at_x : at_x + breadth].astype(jnp.float32)
            total = total + window * w_dw[y * 7 + x].astype(jnp.float32)
    return total


def depthwise_kernel_grad(padded, grad_map, height, breadth):
    rows_out = []
    grad_float = grad_map.astype(jnp.float32)
    for y in range(7):
        for x in range(7):
            window = padded[:, y : y + height, x : x + breadth].astype(jnp.float32)
            rows_out.append(jnp.sum(window * grad_float, axis=(0, 1, 2)))
    return jnp.stack(rows_out)


def as_rows(piece, rows):
    flat = piece.reshape(-1)
    return jnp.pad(flat, (0, rows * LANES - flat.shape[0])).reshape(rows, LANES)


def on_device(
    inputs,
    targets,
    land_mask,
    volume,
    date_index,
    perm_narrow,
    perm_wide,
    w_in,
    w_down,
    w_dw,
    w_hidden,
    w_out,
    w_up,
    w_head,
    biases_gains,
    moment_first,
    moment_second,
):
    b_in, b_down, b_dw, gain, shift, b_hidden, b_out, b_up, b_head = split_vector(biases_gains)
    weight = land_mask.astype(jnp.float32) * volume
    height, breadth = weight.shape
    half_h, half_w = (height // 2, breadth // 2)
    weight_col = jnp.tile(weight.reshape(-1, 1), (MB, 1))
    matrices = (w_in, w_down, w_dw, w_hidden, w_out, w_up, w_head)
    sides = (("rows", 1), ("cols", 2))

    def dates(field):
        return jnp.concatenate(
            [lax.dynamic_slice_in_dim(field, date_index[m], 1, 0) for m in range(MB)]
        )

    narrow_turn = (jnp.arange(C1)[:, None] == perm_narrow[None, :]).astype(jnp.bfloat16)
    wide_turn = (jnp.arange(CH)[:, None] == perm_wide[None, :]).astype(jnp.bfloat16)

    def turned(values, turn):
        return product(values, turn).astype(jnp.bfloat16)

    state, target = dates(inputs), dates(targets)
    state_pad = clear_edges(padded_2(state, sides, 1), 1)
    taps = jnp.concatenate(
        [state_pad[:, y : y + height, x : x + breadth] for y in range(3) for x in range(3)], -1
    ).reshape(-1, 9 * CI)
    a_zero = product(taps, w_in) + b_in
    h_zero, gelu_zero = jax.vjp(jax.nn.gelu, a_zero)
    h_low = h_zero.astype(jnp.bfloat16)
    patches = to_coarse(h_low.reshape(MB, height, breadth, C0), height, breadth)
    coarse = product(patches, w_down) + b_down
    coarse_low = coarse.astype(jnp.bfloat16).reshape(MB, half_h, half_w, C1)
    coarse_pad = clear_edges(padded_2(coarse_low, sides, 3), 3)
    conv_out = depthwise(coarse_pad, w_dw, half_h, half_w, False).reshape(-1, C1) + b_dw
    normed, norm_pull = jax.vjp(layer_norm, conv_out, gain, shift)
    normed_low = normed.astype(jnp.bfloat16)
    pre = product(normed_low, w_hidden) + b_hidden
    act, act_pull = jax.vjp(jax.nn.gelu, pre)
    act_low = act.astype(jnp.bfloat16)
    branch = product(act_low, w_out) + b_out
    mixed_low = (coarse + branch).astype(jnp.bfloat16)
    upper = product(mixed_low, w_up) + jnp.tile(b_up, 4)
    summed_low = (to_fine(upper, height, breadth) + h_zero).astype(jnp.bfloat16)
    output = product(summed_low, w_head) + b_head
    error = output - target.reshape(-1, CI).astype(jnp.float32)
    loss_local = jnp.sum(weight_col * error * error)
    grad_out = (2.0 * weight_col * error).astype(jnp.bfloat16)
    d_head = inner_rows(summed_low, grad_out)
    grad_summed = outer_cols(grad_out, w_head)
    grad_upper = to_coarse(
        grad_summed.astype(jnp.bfloat16).reshape(MB, height, breadth, C0), height, breadth
    )
    d_up = inner_rows(mixed_low, grad_upper)
    grad_mixed = outer_cols(grad_upper, w_up)
    grad_branch = grad_mixed.astype(jnp.bfloat16)
    d_out = inner_rows(turned(act_low, wide_turn), turned(grad_branch, narrow_turn))
    grad_act = outer_cols(grad_branch, w_out)
    grad_pre = act_pull(grad_act)[0].astype(jnp.bfloat16)
    d_hidden = inner_rows(turned(normed_low, narrow_turn), turned(grad_pre, wide_turn))
    grad_normed = outer_cols(grad_pre, w_hidden)
    grad_conv, d_gain, d_shift = norm_pull(grad_normed)
    grad_conv = grad_conv.astype(jnp.bfloat16)
    grad_map = grad_conv.reshape(MB, half_h, half_w, C1)
    d_dw = depthwise_kernel_grad(coarse_pad, grad_map, half_h, half_w)
    grad_pad = clear_edges(padded_2(grad_map, sides, 3), 3)
    grad_coarse_low = depthwise(grad_pad, w_dw, half_h, half_w, True).reshape(-1, C1)
    grad_coarse = (grad_coarse_low + grad_mixed).astype(jnp.bfloat16)
    d_down = inner_rows(patches, grad_coarse)
    grad_h = to_fine(outer_cols(grad_coarse, w_down), height, breadth) + grad_summed
    grad_a = gelu_zero(grad_h)[0].astype(jnp.bfloat16)
    d_in = inner_rows(taps, grad_a)
    d_vector = jnp.concatenate(
        [
            column_sum(grad_a),
            column_sum(grad_coarse),
            column_sum(grad_conv),
            d_gain,
            d_shift,
            column_sum(grad_pre),
            column_sum(grad_branch),
            jnp.sum(column_sum(grad_upper).reshape(4, C0), 0),
            column_sum(grad_out),
        ]
    )
    terms = (d_in, d_down, d_dw, d_hidden, d_out, d_up, d_head, d_vector)
    rows, cols = lax.axis_size("rows"), lax.axis_size("cols")
    space = Plan(rows, cols, PADDED).space
    ends = ROW_AT[1:] + [space]
    blocks = [jnp.zeros((ROW_AT[0], LANES), jnp.float32)]
    for term, begin, end in zip(terms, ROW_AT, ends):
        blocks.append(as_rows(term, end - begin))
    grad = jnp.concatenate(blocks)
    line = jnp.arange(8)[:, None]
    extra = jnp.where(line == 0, loss_local, jnp.where(line == 1, jnp.sum(weight), 0.0))
    extra = jnp.where(jnp.arange(LANES)[None, :] == 0, extra, 0.0)
    plan, (gathered, first, second, totals) = exchange(
        rows, cols, grad, moment_first, moment_second, extra
    )
    full = gathered[:, : plan.share, :].astype(jnp.float32).reshape(-1)
    back_narrow = jnp.zeros((C1,), jnp.int32).at[perm_narrow].set(jnp.arange(C1, dtype=jnp.int32))
    back_wide = jnp.zeros((CH,), jnp.int32).at[perm_wide].set(jnp.arange(CH, dtype=jnp.int32))
    olds = matrices + (biases_gains,)
    news = []
    for index, old in enumerate(olds):
        start = FLAT_AT[index]
        piece = full[start : start + old.size].reshape(old.shape)
        if index == 3:
            piece = piece[back_narrow][:, back_wide]
        if index == 4:
            piece = piece[back_wide][:, back_narrow]
        if index < 7:
            news.append(
                old.astype(jnp.float32) * (1.0 - learn_rate * weight_decay) - learn_rate * piece
            )
        else:
            news.append(old - learn_rate * piece)
    return tuple(news) + (
        first.reshape(-1),
        second.reshape(-1),
        totals[0, 0],
        MB * CI * totals[1, 0],
        totals[8, 0],
    )


def solution(mesh):
    return jax.shard_map(
        on_device,
        mesh=mesh,
        in_specs=(
            P(None, "rows", "cols", None),
            P(None, "rows", "cols", None),
            P("rows", "cols"),
            P("rows", "cols"),
            P(),
            P(),
            P(),
            P(),
            P(),
            P(),
            P(),
            P(),
            P(),
            P(),
            P(),
            P(("rows", "cols")),
            P(("rows", "cols")),
        ),
        out_specs=(
            P(),
            P(),
            P(),
            P(),
            P(),
            P(),
            P(),
            P(),
            P(("rows", "cols")),
            P(("rows", "cols")),
            P(),
            P(),
            P(),
        ),
        check_vma=False,
    )
```

time: 1690 us -> 830 us (0.49); the launches traced: 1660 us -> 822 us
  waiting for transfers between devices: 545 us -> 10.7 us
  local copies, waits for them, and re-layouts: 729 us -> 364 us
  Pallas kernels: 0 us -> 175 us
  blocking collectives: 41.2 us -> 0 us
  other arithmetic: 163 us -> 131 us
  starting transfers between devices: 32.4 us -> 14.3 us
  loops' own time: 17.6 us -> 0 us
    psum x1 -> x0, waiting for transfers between devices: 405 us -> none  [on_device(): lax.psum((flat, loss_local, weight_local), ('rows', 'cols'))]
    concatenate x5, local copies, waits for them, and re-layouts: 221 us -> 16.1 us  [the longest x2 15.4 us: on_device(): jnp.concatenate([state_pad[:, y:y + height, x:x + breadth] for y in range...]
    pallas_call x0 -> x1, Pallas kernels: none -> 175 us  [exchange(): pl.pallas_call(functools.partial(exchange_kernel, plan), out_shape=(jax.S...]
    gather x8 -> x0, local copies, waits for them, and re-layouts: 116 us -> none  [the longest x4 58.2 us: on_device(): rotated[4] = sums[4][perm_wide][:, perm_narrow]]
    all_gather x1 -> x0, waiting for transfers between devices: 88.7 us -> none  [on_device(): lax.all_gather(direction.astype(jnp.bfloat16), ('rows', 'cols'), axis=0,...]
    another operation x100 -> x50, local copies, waits for them, and re-layouts: 62 us -> 1.23 us  [depthwise_kernel_grad(): return jnp.stack(rows_out)]
    convert_element_type x10 -> x4, other arithmetic: 47.7 us -> 4.23 us  [the longest x1 2.55 us: on_device(): summed_low = (to_fine(upper, height, breadth) + h_zero).astype(jnp.bfloat16)]
    psum x1 -> x0, blocking collectives: 41.2 us -> none  [on_device(): lax.psum((flat, loss_local, weight_local), ('rows', 'cols'))]
  transfers between devices with their start and end apart: 26 -> 12, of which waited for: 15 -> 3; matrix products, arithmetic and copies ran while one was open for 6% -> 12% of each run, Pallas kernels for 0% -> 0%
where the time goes in v1:
time: 830 us; the launch traced here: 822 us
  local copies, waits for them, and re-layouts  364 us (44%)
  Pallas kernels  175 us (21%)
  other arithmetic  131 us (16%)
  matrix products  117 us (14%)
  starting transfers between devices  14.3 us (2%)
  waiting for transfers between devices  10.7 us (1%)
  between operations  9.94 us (1%)
    pallas_call x1, Pallas kernels, exchange(): pl.pallas_call(functools.partial(exchange_kernel, plan), out_shape=(jax.S...  175 us
    dot_general x8, matrix products, product(): return jnp.dot(left, right, preferred_element_type=jnp.float32)  64.6 us
    unnamed x407, local copies, waits for them, and re-layouts  56.1 us
    gather x3, local copies, waits for them, and re-layouts, on_device(): piece = piece[back_narrow][:, back_wide]  46.1 us
    gather x3, local copies, waits for them, and re-layouts, on_device(): piece = piece[back_wide][:, back_narrow]  45.8 us
    reshape x4, local copies, waits for them, and re-layouts, as_rows(): return jnp.pad(flat, (0, rows * LANES - flat.shape[0])).reshape(rows, LANES)  33.9 us
    sub x7, other arithmetic, on_device(): old.astype(jnp.float32) * (1.0 - learn_rate * weight_decay)  30.1 us
    dot_general x6, matrix products, inner_rows(): jnp.einsum('nk,nd->kd', left, right, preferred_element_type=jnp.float32)  28.4 us
  transfers between devices with their start and end apart: 12, of which 3 were waited for; matrix products, arithmetic and copies ran while one was open for 12% of the time, Pallas kernels for 0%

profile of v1, /device:TPU:0, one launch (start us, length us, event | category | flops | bytes accessed | tf_op | source)
XLA Modules:
  0.0 822.2 jit_solution(1710324116977291608)
XLA Ops:
  7.2 3.4 collective-permute-start.1
  13.2 5.3 scatter_custom_fusion
  18.5 15.8 %scatter_custom_fusion.1 = s32[3200]{0:T(1024)S(1)} fusion(s32[3200]{0:T(1024)S(1)} %compare_select_fusion.1, s32[3200]{0:T(1024)S(1)} %iota.48, s32[]{:T(128)} %constant.29.clone.1), kind=kCustom, calls=%fused_computation.311 | custom fusion | bytes 12804 | tf_op jit(solution)/shard_map/scatter | solution.py:789
  37.0 3.6 collective-permute-start.3
  42.3 4.3 collective-permute-done.2
  49.6 15.0 %concatenate.36 = bf16[2,8,128,693]{2,3,1,0:T(8,128)(2,1)S(1)} concatenate(bf16[2,8,128,77]{2,3,1,0:T(8,128)(2,1)} %get-tuple-element.211, bf16[2,8,128,77]{2,3,1,0:T(8,128)(2,1)} %get-tuple-element.210, bf16[2,8,128,77]{2,3,1,0:T(8,128)(2,1)} %get-tuple-element.209, bf16[2,8,128,77]{2,3,1,0:T(8,128)(2,1)} %get-tuple-element.208, bf16[2,8,128,77]{2,3,1,0:T(8,128)(2,1)} %get-tuple-element.207, ...), dimensions={3} | concatenate | bytes 5677056 | tf_op jit(solution)/shard_map/concatenate | solution.py:712
  71.4 3.9 add_convert_fusion.5
  84.6 8.7 %copy.120 = bf16[800,3200]{0,1:T(8,128)(2,1)} copy(bf16[800,3200]{1,0:T(8,128)(2,1)} %param.27) | data formatting | bytes 10240000 | tf_op args[10]
  99.4 5.6 collective-permute-done.7
  105.0 2.9 maximum_select_fusion
  108.3 15.6 %add_reduce_fusion = (f32[2,4,64]{2,1,0:T(4,128)S(1)}, f32[2,4,64,800]{3,2,1,0:T(8,128)}) fusion(f32[800]{0:T(1024)S(1)} %get-tuple-element.222, f32[800]{0:T(1024)} %get-tuple-element.173, bf16[2,10,70,800]{3,2,1,0:T(8,128)(2,1)S(1)} %maximum_select_fusion, f32[800]{0:T(1024)S(1)} %get-tuple-element.126, f32[800]{0:T(1024)S(1)} %get-tuple-element.127, ...), kind=kLoop, calls=%fused_computation.242 | loop fusion | flops 60620288 | bytes 41941248 | tf_op jit(solution)/shard_map/jvp()/reduce_sum | solution.py:641
  125.9 2.7 copy.105
  128.8 7.1 convolution_add_fusion
  136.0 7.9 add_convert_fusion.3
  147.0 2.7 copy.106
  149.7 6.0 reshape.627
  155.8 3.8 copy.107
  159.6 3.6 reshape.628
  163.2 2.8 copy.108
  175.6 2.9 copy.111
  178.5 3.9 reshape.629
  182.5 2.8 fusion.155
  185.3 13.0 %convert_reduce_fusion = (f32[3200]{0:T(1024)}, bf16[512,3200]{1,0:T(8,128)(2,1)S(1)}) fusion(f32[512,3200]{1,0:T(8,128)} %copy-done.6, bf16[3200,800]{0,1:T(8,128)(2,1)} %param.28, f32[512,800]{0,1:T(8,128)S(1)} %fusion.155), kind=kOutput, calls=%fused_computation.72 | convolution fusion | flops 2657891328 | bytes 16601600 | tf_op jit(solution)/shard_map/nd,kd->nk/dot_general | solution.py:606
  198.4 3.9 multiply_reduce_fusion.1
  205.4 4.0 fusion.76
  209.4 5.5 fusion.94
  214.9 5.5 fusion.112
  220.4 18.9 %fusion.11 = bf16[512,3200]{1,0:T(8,128)(2,1)} fusion(bf16[512,3200]{1,0:T(8,128)(2,1)} %copy-done.185, s32[3200]{0:T(1024)S(1)} %copy-done.127), kind=kOutput, calls=%fused_computation.75 | convolution fusion | flops 10497638400 | bytes 6566400 | tf_op jit(solution)/shard_map/dot_general | solution.py:598
  239.3 21.2 %fusion.12 = bf16[512,3200]{1,0:T(8,128)(2,1)} fusion(s32[3200]{0:T(1024)S(1)} %copy-done.128, f32[512,3200]{1,0:T(8,128)} %copy-done.6), kind=kOutput, calls=%fused_computation.76 | convolution fusion | flops 10512384000 | bytes 9843200 | tf_op jit(solution)/shard_map/dot_general | solution.py:598
  269.0 10.4 %fusion.125 = f32[800,3200]{1,0:T(8,128)} fusion(bf16[512,3200]{1,0:T(8,128)(2,1)} %fusion.11, s32[800]{0:T(1024)S(1)} %copy-done.176, f32[512,800]{0,1:T(8,128)S(1)} %copy-done.1, f32[800]{0:T(1024)S(1)} %copy-done.38, f32[800]{0:T(1024)S(1)} %get-tuple-element.221, f32[512]{0:T(512)S(1)} %copy-done.118, f32[512]{0:T(512)S(1)} %div.21, ...), kind=kOutput, calls=%fused_computation.272 | convolution fusion | flops 3280307200 | bytes 15172096 | tf_op jit(solution)/shard_map/nk,nd->kd/dot_general | solution.py:602
  280.8 11.4 %fusion.126 = f32[3200,800]{1,0:T(8,128)} fusion(bf16[512,3200]{1,0:T(8,128)(2,1)} %fusion.12, s32[800]{0:T(1024)S(1)} %copy-done.176, f32[512,800]{0,1:T(8,128)} %copy-done.17), kind=kOutput, calls=%fused_computation.273 | convolution fusion | flops 3278259200 | bytes 15158400 | tf_op jit(solution)/shard_map/nk,nd->kd/dot_general | solution.py:602
  299.8 11.6 %reshape.639 = f32[20000,128]{1,0:T(8,128)} reshape(f32[800,3200]{1,0:T(8,128)} %fusion.125) | data formatting | bytes 20480000 | tf_op jit(solution)/shard_map/reshape | solution.py:669
  311.4 14.1 %reshape.640 = f32[20000,128]{1,0:T(8,128)} reshape(f32[3200,800]{1,0:T(8,128)} %fusion.126) | data formatting | bytes 20480000 | tf_op jit(solution)/shard_map/reshape | solution.py:669
  325.5 4.8 reshape.641
  334.3 14.6 %multiply_add_fusion = f32[2,4,64,800]{3,2,1,0:T(8,128)S(1)} fusion(bf16[2,10,70,800]{3,2,1,0:T(8,128)(2,1)S(1)} %maximum_select_fusion.1, f32[800]{0:T(1024)} %get-tuple-element.173, f32[800]{0:T(1024)S(1)} %copy-done.83, f32[800]{0:T(1024)S(1)} %copy-done.85, f32[800]{0:T(1024)S(1)} %copy-done.87, f32[800]{0:T(1024)S(1)} %copy-done.89, ...), kind=kLoop, calls=%fused_computation.240 | loop fusion | flops 59801600 | bytes 41936000 | tf_op jit(solution)/shard_map/add | solution.py:653
  355.8 5.9 reshape.632
  361.7 3.8 copy.115
  365.5 3.8 reshape.633
  369.3 2.8 copy.116
  372.1 3.9 convert_reduce_fusion.5
  379.8 3.4 reshape.636
  384.0 3.5 constant_dynamic-update-slice_fusion.3
  388.2 9.1 %constant_dynamic-update-slice_fusion.2 = f32[51632,128]{1,0:T(8,128)} fusion(f32[51632,128]{1,0:T(8,128)} %bitcast_dynamic-update-slice_fusion.1, f32[20000,128]{1,0:T(8,128)} %reshape.639), kind=kLoop, calls=%fused_computation.304 | loop fusion | bytes 20480000
  397.4 4.2 constant_dynamic-update-slice_fusion.1
  404.7 174.9 %shard_map.264 = (bf16[32,1616,128]{2,1,0:T(8,128)(2,1)}, f32[1612,128]{1,0:T(8,128)}, f32[1612,128]{1,0:T(8,128)}, f32[16,128]{1,0:T(8,128)}) custom-call(f32[51632,128]{1,0:T(8,128)} %bitcast_dynamic-update-slice_fusion.3.grad, f32[1612,128]{1,0:T(8,128)} %bitcast.156, f32[1612,128]{1,0:T(8,128)} %bitcast.157, f32[8,128]{1,0:T(8,128)} %broadcast_select_fusion.extra), custom_call_target="tpu_custom_call" | custom-call | tf_op jit(solution)/shard_map/pallas_call | solution.py:532
  579.6 14.7 %slice_convert_fusion = f32[32,1612,128]{2,1,0:T(8,128)} fusion(bf16[32,1616,128]{2,1,0:T(8,128)(2,1)} %get-tuple-element.17), kind=kLoop, calls=%fused_computation.60 | loop fusion | flops 6602752 | bytes 39616512 | tf_op jit(solution)/shard_map/reshape | solution.py:787
  594.4 22.9 %reshape.704 = f32[6602752]{0:T(1024)} reshape(f32[32,1612,128]{2,1,0:T(8,128)} %slice_convert_fusion) | data formatting | bytes 52822016 | tf_op jit(solution)/shard_map/reshape | solution.py:787
  618.6 6.2 slice_multiply_fusion
  625.8 17.2 %fusion.144 = (f32[2560000]{0:T(1024)}, f32[2560000]{0:T(1024)}) fusion(f32[6602752]{0:T(1024)} %reshape.704), kind=kLoop, calls=%fused_computation.388 | loop fusion | bytes 40960000 | tf_op jit(solution)/shard_map/slice | solution.py:794
  648.3 3.4 mul.1358
  651.7 3.3 multiply_subtract_fusion.1
  655.9 11.7 %reshape.649 = f32[800,3200]{1,0:T(8,128)} reshape(f32[2560000]{0:T(1024)} %get-tuple-element.189) | data formatting | bytes 20480000 | tf_op jit(solution)/shard_map/reshape | solution.py:794
  667.6 15.7 %gather_fusion = f32[800,3200]{1,0:T(8,128)} fusion(f32[800,3200]{1,0:T(8,128)} %reshape.649, s32[1024]{0:T(1024)S(1)} %copy-done.116), kind=kCustom, calls=%fused_computation | custom fusion | bytes 20483200 | tf_op jit(solution)/shard_map/gather | solution.py:796
  683.3 12.3 %copy.121 = f32[800,3200]{0,1:T(8,128)} copy(f32[800,3200]{1,0:T(8,128)} %gather_fusion) | data formatting | bytes 20480000 | tf_op jit(solution)/shard_map/gather | solution.py:796
  695.6 18.1 %gather_fusion.1 = f32[3200,800]{1,0:T(8,128)} fusion(f32[800,3200]{0,1:T(8,128)} %copy.121, s32[4096]{0:T(1024)S(1)} %copy-done.37), kind=kCustom, calls=%fused_computation.1 | custom fusion | bytes 20492800 | tf_op jit(solution)/shard_map/gather | solution.py:796
  713.7 11.8 %bitcast_subtract_fusion = f32[800,3200]{0,1:T(8,128)} fusion(f32[3200,800]{1,0:T(8,128)} %gather_fusion.1, bf16[800,3200]{0,1:T(8,128)(2,1)} %copy.120), kind=kLoop, calls=%fused_computation.61 | loop fusion | flops 10240000 | bytes 25600000 | tf_op jit(solution)/shard_map/sub | solution.py:801
  725.5 12.2 %copy.125 = f32[800,3200]{1,0:T(8,128)} copy(f32[800,3200]{0,1:T(8,128)} %bitcast_subtract_fusion) | data formatting | bytes 20480000
  737.7 13.5 %reshape.650 = f32[3200,800]{1,0:T(8,128)} reshape(f32[2560000]{0:T(1024)} %get-tuple-element.188) | data formatting | bytes 20480000 | tf_op jit(solution)/shard_map/reshape | solution.py:794
  751.2 17.9 %gather_fusion.2 = f32[3200,800]{1,0:T(8,128)} fusion(f32[3200,800]{1,0:T(8,128)} %reshape.650, s32[4096]{0:T(1024)S(1)} %copy-done.37), kind=kCustom, calls=%fused_computation.2 | custom fusion | bytes 20492800 | tf_op jit(solution)/shard_map/gather | solution.py:798
  769.1 12.2 %copy.122 = f32[3200,800]{0,1:T(8,128)} copy(f32[3200,800]{1,0:T(8,128)} %gather_fusion.2) | data formatting | bytes 20480000 | tf_op jit(solution)/shard_map/gather | solution.py:798
  781.3 15.7 %gather_fusion.3 = f32[800,3200]{1,0:T(8,128)} fusion(f32[3200,800]{0,1:T(8,128)} %copy.122, s32[1024]{0:T(1024)S(1)} %copy-done.116), kind=kCustom, calls=%fused_computation.3 | custom fusion | bytes 20483200 | tf_op jit(solution)/shard_map/gather | solution.py:798
  797.0 10.9 %bitcast_subtract_fusion.1 = f32[3200,800]{0,1:T(8,128)} fusion(f32[800,3200]{1,0:T(8,128)} %gather_fusion.3, bf16[3200,800]{0,1:T(8,128)(2,1)} %param.28), kind=kLoop, calls=%fused_computation.62 | loop fusion | flops 10240000 | bytes 25600000 | tf_op jit(solution)/shard_map/sub | solution.py:801
  807.9 3.4 mul.1374
  811.4 3.3 multiply_subtract_fusion
  (562 shorter events, 101.0 us)
Async XLA Ops:
  0.7 12.4 %copy-start.175 = (s32[800]{0:T(1024)S(1)}, s32[800]{0:T(1024)}, u32[]{:S(2)}) copy-start(s32[800]{0:T(1024)} %param.22) | copy-start | bytes 9604
  0.7 17.8 %copy-start.126 = (s32[3200]{0:T(1024)S(1)}, s32[3200]{0:T(1024)}, u32[]{:S(2)}) copy-start(s32[3200]{0:T(1024)} %param.23) | copy-start | bytes 38404
  7.2 29.2 %collective-permute-start.1 = (bf16[2,1,128,77]{2,3,1,0:T(8,128)(2,1)S(1)}, bf16[2,1,128,77]{2,3,1,0:T(8,128)(2,1)S(1)}, u32[]{:S(2)}, u32[]{:S(2)}) collective-permute-start(bf16[2,1,128,77]{2,3,1,0:T(8,128)(2,1)S(1)} %get-tuple-element.216), channel_id=1, source_target_pairs={{4,0},{8,4},{12,8},{16,12},{20,16},{24,20},{28,24},{0,28},{5,1},{9... | collective-permute-start | bytes 118280 | tf_op jit(solution)/shard_map/ppermute | solution.py:580
  10.6 25.8 %collective-permute-start = (bf16[2,1,128,77]{2,3,1,0:T(8,128)(2,1)S(1)}, bf16[2,1,128,77]{2,3,1,0:T(8,128)(2,1)S(1)}, u32[]{:S(2)}, u32[]{:S(2)}) collective-permute-start(bf16[2,1,128,77]{2,3,1,0:T(8,128)(2,1)S(1)} %get-tuple-element.215), channel_id=1, source_target_pairs={{0,4},{4,8},{8,12},{12,16},{16,20},{20,24},{24,28},{28,0},{1,5},{5... | collective-permute-start | bytes 118280 | tf_op jit(solution)/shard_map/ppermute | solution.py:578
  13.1 68.0 %copy-start.39 = (f32[1,8,2,128]{3,2,1,0:T(2,128)}, f32[1,8,2,128]{3,2,1,0:T(2,128)S(1)}, u32[]{:S(2)}) copy-start(f32[1,8,2,128]{3,2,1,0:T(2,128)S(1)} %broadcast_bitcast_fusion) | copy-start | bytes 24580
  37.0 5.0 collective-permute-start.3
  41.0 5.7 collective-permute-start.2
  77.2 19.4 %collective-permute-start.5 = (bf16[2,3,64,800]{3,2,1,0:T(8,128)(2,1)}, bf16[2,3,64,800]{3,2,1,0:T(8,128)(2,1)S(1)}, u32[]{:S(2)}, u32[]{:S(2)}) collective-permute-start(bf16[2,3,64,800]{3,2,1,0:T(8,128)(2,1)} %get-tuple-element.202), channel_id=1, source_target_pairs={{4,0},{8,4},{12,8},{16,12},{20,16},{24,20},{28,24},{0,28},{5,1},{9... | collective-permute-start | bytes 1843208 | tf_op jit(solution)/shard_map/ppermute | solution.py:580
  78.4 18.2 %collective-permute-start.4 = (bf16[2,3,64,800]{3,2,1,0:T(8,128)(2,1)}, bf16[2,3,64,800]{3,2,1,0:T(8,128)(2,1)S(1)}, u32[]{:S(2)}, u32[]{:S(2)}) collective-permute-start(bf16[2,3,64,800]{3,2,1,0:T(8,128)(2,1)} %get-tuple-element.201), channel_id=1, source_target_pairs={{0,4},{4,8},{8,12},{12,16},{16,20},{20,24},{24,28},{28,0},{1,5},{5... | collective-permute-start | bytes 1843208 | tf_op jit(solution)/shard_map/ppermute | solution.py:578
  94.9 13.1 %copy-start.42 = (f32[800]{0:T(1024)}, f32[800]{0:T(1024)S(1)}, u32[]{:S(2)}) copy-start(f32[800]{0:T(1024)S(1)} %get-tuple-element.144) | copy-start | bytes 9604
  94.9 13.1 %copy-start.44 = (f32[800]{0:T(1024)}, f32[800]{0:T(1024)S(1)}, u32[]{:S(2)}) copy-start(f32[800]{0:T(1024)S(1)} %get-tuple-element.145) | copy-start | bytes 9604
  94.9 13.1 %copy-start.46 = (f32[800]{0:T(1024)}, f32[800]{0:T(1024)S(1)}, u32[]{:S(2)}) copy-start(f32[800]{0:T(1024)S(1)} %get-tuple-element.146) | copy-start | bytes 9604
  94.9 13.1 %copy-start.48 = (f32[800]{0:T(1024)}, f32[800]{0:T(1024)S(1)}, u32[]{:S(2)}) copy-start(f32[800]{0:T(1024)S(1)} %get-tuple-element.147) | copy-start | bytes 9604
  94.9 13.1 %copy-start.50 = (f32[800]{0:T(1024)}, f32[800]{0:T(1024)S(1)}, u32[]{:S(2)}) copy-start(f32[800]{0:T(1024)S(1)} %get-tuple-element.148) | copy-start | bytes 9604
  94.9 13.1 %copy-start.52 = (f32[800]{0:T(1024)}, f32[800]{0:T(1024)S(1)}, u32[]{:S(2)}) copy-start(f32[800]{0:T(1024)S(1)} %get-tuple-element.149) | copy-start | bytes 9604
  94.9 13.1 %copy-start.54 = (f32[800]{0:T(1024)}, f32[800]{0:T(1024)S(1)}, u32[]{:S(2)}) copy-start(f32[800]{0:T(1024)S(1)} %get-tuple-element.150) | copy-start | bytes 9604
  95.0 13.1 %copy-start.56 = (f32[800]{0:T(1024)}, f32[800]{0:T(1024)S(1)}, u32[]{:S(2)}) copy-start(f32[800]{0:T(1024)S(1)} %get-tuple-element.151) | copy-start | bytes 9604
  95.0 13.1 %copy-start.58 = (f32[800]{0:T(1024)}, f32[800]{0:T(1024)S(1)}, u32[]{:S(2)}) copy-start(f32[800]{0:T(1024)S(1)} %get-tuple-element.152) | copy-start | bytes 9604
  95.0 13.1 %copy-start.60 = (f32[800]{0:T(1024)}, f32[800]{0:T(1024)S(1)}, u32[]{:S(2)}) copy-start(f32[800]{0:T(1024)S(1)} %get-tuple-element.153) | copy-start | bytes 9604
  95.0 13.1 %copy-start.62 = (f32[800]{0:T(1024)}, f32[800]{0:T(1024)S(1)}, u32[]{:S(2)}) copy-start(f32[800]{0:T(1024)S(1)} %get-tuple-element.154) | copy-start | bytes 9604
  95.0 13.1 %copy-start.64 = (f32[800]{0:T(1024)}, f32[800]{0:T(1024)S(1)}, u32[]{:S(2)}) copy-start(f32[800]{0:T(1024)S(1)} %get-tuple-element.155) | copy-start | bytes 9604
  95.0 13.1 %copy-start.66 = (f32[800]{0:T(1024)}, f32[800]{0:T(1024)S(1)}, u32[]{:S(2)}) copy-start(f32[800]{0:T(1024)S(1)} %get-tuple-element.156) | copy-start | bytes 9604
  95.0 13.1 %copy-start.68 = (f32[800]{0:T(1024)}, f32[800]{0:T(1024)S(1)}, u32[]{:S(2)}) copy-start(f32[800]{0:T(1024)S(1)} %get-tuple-element.157) | copy-start | bytes 9604
  95.0 13.1 %copy-start.70 = (f32[800]{0:T(1024)}, f32[800]{0:T(1024)S(1)}, u32[]{:S(2)}) copy-start(f32[800]{0:T(1024)S(1)} %get-tuple-element.158) | copy-start | bytes 9604
  95.0 13.1 %copy-start.72 = (f32[800]{0:T(1024)}, f32[800]{0:T(1024)S(1)}, u32[]{:S(2)}) copy-start(f32[800]{0:T(1024)S(1)} %get-tuple-element.159) | copy-start | bytes 9604
  95.0 13.1 %copy-start.74 = (f32[800]{0:T(1024)}, f32[800]{0:T(1024)S(1)}, u32[]{:S(2)}) copy-start(f32[800]{0:T(1024)S(1)} %get-tuple-element.160) | copy-start | bytes 9604
  95.1 13.1 %copy-start.76 = (f32[800]{0:T(1024)}, f32[800]{0:T(1024)S(1)}, u32[]{:S(2)}) copy-start(f32[800]{0:T(1024)S(1)} %get-tuple-element.161) | copy-start | bytes 9604
  95.1 13.1 %copy-start.78 = (f32[800]{0:T(1024)}, f32[800]{0:T(1024)S(1)}, u32[]{:S(2)}) copy-start(f32[800]{0:T(1024)S(1)} %get-tuple-element.162) | copy-start | bytes 9604
  95.9 12.3 %copy-start.80 = (f32[800]{0:T(1024)}, f32[800]{0:T(1024)S(1)}, u32[]{:S(2)}) copy-start(f32[800]{0:T(1024)S(1)} %get-tuple-element.125) | copy-start | bytes 9604
  95.9 12.3 %copy-start.82 = (f32[800]{0:T(1024)}, f32[800]{0:T(1024)S(1)}, u32[]{:S(2)}) copy-start(f32[800]{0:T(1024)S(1)} %get-tuple-element.126) | copy-start | bytes 9604
  95.9 12.3 %copy-start.84 = (f32[800]{0:T(1024)}, f32[800]{0:T(1024)S(1)}, u32[]{:S(2)}) copy-start(f32[800]{0:T(1024)S(1)} %get-tuple-element.127) | copy-start | bytes 9604
  95.9 12.3 %copy-start.86 = (f32[800]{0:T(1024)}, f32[800]{0:T(1024)S(1)}, u32[]{:S(2)}) copy-start(f32[800]{0:T(1024)S(1)} %get-tuple-element.128) | copy-start | bytes 9604
  95.9 12.3 %copy-start.88 = (f32[800]{0:T(1024)}, f32[800]{0:T(1024)S(1)}, u32[]{:S(2)}) copy-start(f32[800]{0:T(1024)S(1)} %get-tuple-element.129) | copy-start | bytes 9604
  95.9 12.3 %copy-start.90 = (f32[800]{0:T(1024)}, f32[800]{0:T(1024)S(1)}, u32[]{:S(2)}) copy-start(f32[800]{0:T(1024)S(1)} %get-tuple-element.130) | copy-start | bytes 9604
  95.9 12.3 %copy-start.92 = (f32[800]{0:T(1024)}, f32[800]{0:T(1024)S(1)}, u32[]{:S(2)}) copy-start(f32[800]{0:T(1024)S(1)} %get-tuple-element.131) | copy-start | bytes 9604
  95.9 12.3 %copy-start.94 = (f32[800]{0:T(1024)}, f32[800]{0:T(1024)S(1)}, u32[]{:S(2)}) copy-start(f32[800]{0:T(1024)S(1)} %get-tuple-element.132) | copy-start | bytes 9604
  95.9 12.3 %copy-start.96 = (f32[800]{0:T(1024)}, f32[800]{0:T(1024)S(1)}, u32[]{:S(2)}) copy-start(f32[800]{0:T(1024)S(1)} %get-tuple-element.133) | copy-start | bytes 9604
  95.9 12.3 %copy-start.98 = (f32[800]{0:T(1024)}, f32[800]{0:T(1024)S(1)}, u32[]{:S(2)}) copy-start(f32[800]{0:T(1024)S(1)} %get-tuple-element.134) | copy-start | bytes 9604
  95.9 12.3 %copy-start.100 = (f32[800]{0:T(1024)}, f32[800]{0:T(1024)S(1)}, u32[]{:S(2)}) copy-start(f32[800]{0:T(1024)S(1)} %get-tuple-element.135) | copy-start | bytes 9604
  96.0 12.3 %copy-start.102 = (f32[800]{0:T(1024)}, f32[800]{0:T(1024)S(1)}, u32[]{:S(2)}) copy-start(f32[800]{0:T(1024)S(1)} %get-tuple-element.136) | copy-start | bytes 9604
  96.0 12.3 %copy-start.104 = (f32[800]{0:T(1024)}, f32[800]{0:T(1024)S(1)}, u32[]{:S(2)}) copy-start(f32[800]{0:T(1024)S(1)} %get-tuple-element.137) | copy-start | bytes 9604
  96.0 12.3 %copy-start.106 = (f32[800]{0:T(1024)}, f32[800]{0:T(1024)S(1)}, u32[]{:S(2)}) copy-start(f32[800]{0:T(1024)S(1)} %get-tuple-element.138) | copy-start | bytes 9604
  96.0 12.3 %copy-start.108 = (f32[800]{0:T(1024)}, f32[800]{0:T(1024)S(1)}, u32[]{:S(2)}) copy-start(f32[800]{0:T(1024)S(1)} %get-tuple-element.139) | copy-start | bytes 9604
  96.0 12.3 %copy-start.110 = (f32[800]{0:T(1024)}, f32[800]{0:T(1024)S(1)}, u32[]{:S(2)}) copy-start(f32[800]{0:T(1024)S(1)} %get-tuple-element.140) | copy-start | bytes 9604
  96.0 12.3 %copy-start.112 = (f32[800]{0:T(1024)}, f32[800]{0:T(1024)S(1)}, u32[]{:S(2)}) copy-start(f32[800]{0:T(1024)S(1)} %get-tuple-element.141) | copy-start | bytes 9604
  96.0 12.3 %copy-start.114 = (f32[800]{0:T(1024)}, f32[800]{0:T(1024)S(1)}, u32[]{:S(2)}) copy-start(f32[800]{0:T(1024)S(1)} %get-tuple-element.142) | copy-start | bytes 9604
  96.8 8.2 %collective-permute-start.7 = (bf16[2,10,3,800]{3,2,1,0:T(4,128)(2,1)S(1)}, bf16[2,10,3,800]{3,2,1,0:T(4,128)(2,1)S(1)}, u32[]{:S(2)}, u32[]{:S(2)}) collective-permute-start(bf16[2,10,3,800]{3,2,1,0:T(4,128)(2,1)S(1)} %get-tuple-element.193), channel_id=1, source_target_pairs={{1,0},{2,1},{3,2},{0,3},{5,4},{6,5},{7,6},{4,7},{9,8},{10,9},{11,1... | collective-permute-start | bytes 288008 | tf_op jit(solution)/shard_map/ppermute | solution.py:580
  96.9 8.1 collective-permute-start.6
  182.5 15.8 %slice-start.3 = ((s8[5120000]{0:T(1024)(128)(4,1)}), s8[4194304]{0:T(1024)(128)(4,1)S(1)}, s32[]{:S(2)}) async-start(s8[5120000]{0:T(1024)(128)(4,1)} %bitcast.138), calls=%async_computation.3 | async-start | bytes 8388608
  185.3 13.0 %copy-start.17 = (f32[512,800]{0,1:T(8,128)}, f32[512,800]{0,1:T(8,128)S(1)}, u32[]{:S(2)}) copy-start(f32[512,800]{0,1:T(8,128)S(1)} %fusion.155) | copy-start | bytes 4915204
  185.3 13.0 %slice-start.4 = ((s8[5120000]{0:T(1024)(128)(4,1)}), s8[925696]{0:T(1024)(128)(4,1)S(1)}, s32[]{:S(2)}) async-start(s8[5120000]{0:T(1024)(128)(4,1)} %bitcast.138), calls=%async_computation.4 | async-start | bytes 1851392
  185.3 13.0 %copy-start = (f32[512,800]{0,1:T(8,128)S(1)}, f32[512,800]{0,1:T(8,128)}, u32[]{:S(2)}) copy-start(f32[512,800]{0,1:T(8,128)} %copy.105) | copy-start | bytes 4915204
  185.3 13.0 %copy-start.118 = (f32[512]{0:T(512)S(1)}, f32[512]{0:T(512)}, u32[]{:S(2)}) copy-start(f32[512]{0:T(512)} %copy-done.117) | copy-start | bytes 6148
  220.4 18.9 %copy-start.128 = (s32[3200]{0:T(1024)S(1)}, s32[3200]{0:T(1024)}, u32[]{:S(2)}) copy-start(s32[3200]{0:T(1024)} %param.23) | copy-start | bytes 38404
  239.3 21.2 %copy-start.8 = (bf16[512,800]{1,0:T(8,128)(2,1)S(1)}, bf16[512,800]{1,0:T(8,128)(2,1)}, u32[]{:S(2)}) copy-start(bf16[512,800]{1,0:T(8,128)(2,1)} %copy-done.7) | copy-start | bytes 2457604
  239.3 21.2 %copy-start.12 = (bf16[512,800]{0,1:T(8,128)(2,1)S(1)}, bf16[512,800]{0,1:T(8,128)(2,1)}, u32[]{:S(2)}) copy-start(bf16[512,800]{0,1:T(8,128)(2,1)} %copy-done.11) | copy-start | bytes 2457604
  267.3 25.2 %collective-permute-start.9 = (bf16[2,3,64,800]{3,2,1,0:T(8,128)(2,1)}, bf16[2,3,64,800]{3,2,1,0:T(8,128)(2,1)S(1)}, u32[]{:S(2)}, u32[]{:S(2)}) collective-permute-start(bf16[2,3,64,800]{3,2,1,0:T(8,128)(2,1)} %get-tuple-element.200), channel_id=1, source_target_pairs={{4,0},{8,4},{12,8},{16,12},{20,16},{24,20},{28,24},{0,28},{5,1},{9... | collective-permute-start | bytes 1843208 | tf_op jit(solution)/shard_map/ppermute | solution.py:580
  268.8 23.8 %collective-permute-start.8 = (bf16[2,3,64,800]{3,2,1,0:T(8,128)(2,1)}, bf16[2,3,64,800]{3,2,1,0:T(8,128)(2,1)}, u32[]{:S(2)}, u32[]{:S(2)}) collective-permute-start(bf16[2,3,64,800]{3,2,1,0:T(8,128)(2,1)} %get-tuple-element.199), channel_id=1, source_target_pairs={{0,4},{4,8},{8,12},{12,16},{16,20},{20,24},{24,28},{28,0},{1,5},{5... | collective-permute-start | bytes 1843208 | tf_op jit(solution)/shard_map/ppermute | solution.py:578
  293.6 37.9 %collective-permute-start.11 = (bf16[2,10,3,800]{3,2,1,0:T(4,128)(2,1)S(1)}, bf16[2,10,3,800]{3,2,1,0:T(4,128)(2,1)S(1)}, u32[]{:S(2)}, u32[]{:S(2)}) collective-permute-start(bf16[2,10,3,800]{3,2,1,0:T(4,128)(2,1)S(1)} %get-tuple-element.191), channel_id=1, source_target_pairs={{1,0},{2,1},{3,2},{0,3},{5,4},{6,5},{7,6},{4,7},{9,8},{10,9},{11,1... | collective-permute-start | bytes 288008 | tf_op jit(solution)/shard_map/ppermute | solution.py:580
  294.2 37.3 %collective-permute-start.10 = (bf16[2,10,3,800]{3,2,1,0:T(4,128)(2,1)S(1)}, bf16[2,10,3,800]{3,2,1,0:T(4,128)(2,1)S(1)}, u32[]{:S(2)}, u32[]{:S(2)}) collective-permute-start(bf16[2,10,3,800]{3,2,1,0:T(4,128)(2,1)S(1)} %get-tuple-element.190), channel_id=1, source_target_pairs={{0,1},{1,2},{2,3},{3,0},{4,5},{5,6},{6,7},{7,4},{8,9},{9,10},{10,1... | collective-permute-start | bytes 288008 | tf_op jit(solution)/shard_map/ppermute | solution.py:578
  384.0 13.3 %slice-start = ((s8[10240000]{0:T(1024)(128)(4,1)}), s8[4194304]{0:T(1024)(128)(4,1)S(1)}, s32[]{:S(2)}) async-start(s8[10240000]{0:T(1024)(128)(4,1)} %bitcast.136), calls=%async_computation | async-start | bytes 8388608
  625.8 18.9 %copy-start.36 = (f32[7677]{0:T(1024)S(1)}, f32[7677]{0:T(1024)}, u32[]{:S(2)}) copy-start(f32[7677]{0:T(1024)} %param.31) | copy-start | bytes 92128
  625.8 21.3 %copy-start.20 = (bf16[693,200]{1,0:T(8,128)(2,1)S(1)}, bf16[693,200]{1,0:T(8,128)(2,1)}, u32[]{:S(2)}) copy-start(bf16[693,200]{1,0:T(8,128)(2,1)} %copy.94) | copy-start | bytes 831604
  683.3 12.3 %copy-start.37 = (s32[4096]{0:T(1024)S(1)}, s32[4096]{0:T(1024)}, u32[]{:S(2)}) copy-start(s32[4096]{0:T(1024)} %pad_clamp_fusion) | copy-start | bytes 49156
  (139 other events, 649.7 us)

commit v2 on v1

--- a/solution.py
+++ b/solution.py
@@ -568,20 +568,721 @@
     )(grad, m_first.reshape(share, LANES), m_second.reshape(share, LANES), extra)
 
 
-def padded_2(cells, sides, width):
-    for axis, dim in sides:
-        count = lax.axis_size(axis)
-        head = lax.slice_in_dim(cells, 0, width, axis=dim)
-        tail = lax.slice_in_dim(cells, cells.shape[dim] - width, cells.shape[dim], axis=dim)
-        cells = jnp.concatenate(
-            [
-                lax.ppermute(tail, axis, [(i, (i + 1) % count) for i in range(count)]),
-                cells,
-                lax.ppermute(head, axis, [((i + 1) % count, i) for i in range(count)]),
-            ],
-            axis=dim,
+WIDE = CH + LANES
+KEPT = ((8, 1104), (6096, 6408), (51400, 51584))
+PLACES = tuple(divmod(FLAT_AT[i], LANES) for i in (3, 4, 5, 1))
+
+def unpack_kernel(plan, gathered, old_up, old_down, hidden, out, up, down, small_a, small_b, small_c, held, flat, woven, sems):
+    n, share = plan.count, plan.share
+    step = CH // LANES
+
+    def fetch(k, slot):
+        return pltpu.make_async_copy(gathered.at[k], held.at[slot], sems.at[slot])
+
+    fetch(0, 0).start()
+
+    def widen(k, carry):
+        slot = lax.rem(k, 2)
+
+        @pl.when(k + 1 < n)
+        def _():
+            fetch(k + 1, 1 - slot).start()
+
+        fetch(k, slot).wait()
+
+        def body(b, inner):
+            at = pl.ds(pl.multiple_of(b * 16, 16), 16)
+            flat[pl.ds(share * k + b * 16, 16), :] = held[slot, at, :].astype(jnp.float32)
+            return inner
+
+        lax.fori_loop(0, plan.padded // 16, body, 0, unroll=4)
+        return carry
+
+    lax.fori_loop(0, n, widen, 0)
+
+    for ref, (row, lane) in zip((hidden, out), PLACES):
+        def column(t, carry, ref=ref, row=row):
+            for begin in range(0, C1, 160):
+                values = flat[pl.ds(row + begin * step + t, 160, stride=step), :]
+                ref[begin : begin + 160, pl.ds(pl.multiple_of(t * LANES, LANES), LANES)] = values.astype(
+                    jnp.bfloat16
+                )
+            return carry
+
+        lax.fori_loop(0, WIDE // LANES, column, 0)
+
+    quarter = C1 // 4
+    for ref, old, (row, lane) in zip((up, down), (old_up, old_down), PLACES[2:]):
+        for u in range(-(-C1 // LANES)):
+            width = min(LANES, C1 - u * LANES)
+            place = lax.broadcasted_iota(jnp.int32, (quarter, LANES), 1)
+            for b in range(4):
+                first, rest = divmod(C1 * b + lane, LANES)
+                here = flat[pl.ds(row + first + u, quarter, stride=step), :]
+                after = flat[pl.ds(row + first + u + 1, quarter, stride=step), :]
+                value = pltpu.roll(jnp.where(place >= rest, here, after), LANES - rest, 1)
+                woven[pl.ds(b, quarter, stride=4), :] = value
+            at = slice(u * LANES, u * LANES + width)
+            ref[:, at] = moved(old[:, at], woven[:, :width])
+    for ref, (begin, end) in zip((small_a, small_b, small_c), KEPT):
+        ref[...] = flat[begin:end, :]
+
+
+def unpack(plan, gathered, old_up, old_down):
+    lines = PADDED // LANES
+    vmem = pl.BlockSpec(memory_space=pltpu.VMEM)
+    return pl.pallas_call(
+        functools.partial(unpack_kernel, plan),
+        out_shape=tuple(jax.ShapeDtypeStruct((C1, WIDE), jnp.bfloat16) for _ in range(2))
+        + tuple(jax.ShapeDtypeStruct((C1, C1), jnp.float32) for _ in range(2))
+        + tuple(jax.ShapeDtypeStruct((end - begin, LANES), jnp.float32) for begin, end in KEPT),
+        in_specs=[pl.BlockSpec(memory_space=pl.ANY), vmem, vmem],
+        out_specs=tuple([vmem] * 7),
+        scratch_shapes=[
+            pltpu.VMEM((2, plan.padded, LANES), jnp.bfloat16),
+            pltpu.VMEM((-(-lines // 8) * 8 + 16, LANES), jnp.float32),
+            pltpu.VMEM((C1, LANES), jnp.float32),
+            pltpu.SemaphoreType.DMA((2,)),
+        ],
+        compiler_params=pltpu.CompilerParams(vmem_limit_bytes=54 << 20),
+    )(gathered, old_up, old_down)
+
+
+def moved(old, direction):
+    return old.astype(jnp.float32) * (1.0 - learn_rate * weight_decay) - learn_rate * direction
+
+
+def one_hot(condition):
+    return jnp.where(condition, 1.0, 0.0).astype(jnp.bfloat16)
+
+
+def product(left, right):
+    return jnp.dot(left, right, preferred_element_type=jnp.float32)
+
+
+def product_t(left, right):
+    return lax.dot_general(left, right, (((1,), (1,)), ((), ())), preferred_element_type=jnp.float32)
+
+
+TILE = 640
+
+
+def turn_kernel(prepare, packed, narrow, wide, old, new, lines, hot):
+    depth = lines.shape[1]
+
+    @pl.when(pl.program_id(0) == 0)
+    def _():
+        prepare(packed, narrow, lines)
+
+    base = pl.program_id(0) * TILE
+
+    def build(b, carry):
+        at = pl.ds(pl.multiple_of(b * LANES, LANES), LANES)
+        column = lax.broadcasted_iota(jnp.int32, (LANES, TILE), 1) + base
+        hot[at, :] = one_hot(column == wide[at, 0:1])
+        return carry
+
+    lax.fori_loop(0, depth // LANES, build, 0)
+    new[...] = moved(old[...], product(lines[...], hot[...]))
+
+
+def prepare_hidden(packed, narrow, lines):
+    turn = one_hot(lax.broadcasted_iota(jnp.int32, (C1, C1), 0) == narrow[...])
+    for begin in range(0, WIDE, 832):
+        lines[:, begin : begin + 832] = product(turn, packed[:, begin : begin + 832]).astype(jnp.bfloat16)
+
+
+def quarter_spans(lane):
+    spans = []
+    for b in range(4):
+        begin = (C1 * b + lane) // LANES * LANES
+        end = -(-(C1 * b + lane + C1) // LANES) * LANES
+        spans.append((begin, end))
+    return spans
+
+
+def prepare_out(packed, narrow, lines):
+    for b, (begin, end) in enumerate(quarter_spans(PLACES[1][1])):
+        turn = one_hot(
+            lax.broadcasted_iota(jnp.int32, (C1, end - begin), 0) == narrow[b : b + 1, begin:end]
         )
-    return cells
+        lines[:, b * C1 : (b + 1) * C1] = product_t(turn, packed[:, begin:end]).astype(jnp.bfloat16)
+
+
+def turn_back(prepare, packed, narrow, wide, old):
+    depth = wide.shape[0]
+    return pl.pallas_call(
+        functools.partial(turn_kernel, prepare),
+        out_shape=jax.ShapeDtypeStruct((C1, CH), jnp.float32),
+        grid=(CH // TILE,),
+        in_specs=[
+            pl.BlockSpec((C1, WIDE), lambda i: (0, 0)),
+            pl.BlockSpec(narrow.shape, lambda i: (0, 0)),
+            pl.BlockSpec((depth, LANES), lambda i: (0, 0)),
+            pl.BlockSpec((C1, TILE), lambda i: (0, i)),
+        ],
+        out_specs=pl.BlockSpec((C1, TILE), lambda i: (0, i)),
+        scratch_shapes=[pltpu.VMEM((C1, depth), jnp.bfloat16), pltpu.VMEM((depth, TILE), jnp.bfloat16)],
+        compiler_params=pltpu.CompilerParams(vmem_limit_bytes=48 << 20),
+    )(packed, narrow, jnp.broadcast_to(wide[:, None], (depth, LANES)), old)
+
+
+def rebuild_hidden(packed, narrow, wide, old):
+    lane = PLACES[0][1]
+    shifted = jnp.full((WIDE,), -1, jnp.int32).at[lane : lane + CH].set(wide)
+    return turn_back(prepare_hidden, packed, narrow[None, :], shifted, old)
+
+
+def rebuild_out(packed, narrow, wide, old):
+    lane = PLACES[1][1]
+    place = jnp.arange(WIDE)
+    lanes = jnp.full((WIDE,), -1, jnp.int32).at[lane : lane + CH].set(jnp.tile(narrow, 4))
+    table = jnp.stack(
+        [
+            jnp.where((place >= C1 * b + lane) & (place < C1 * (b + 1) + lane), lanes, -1)
+            for b in range(4)
+        ]
+    )
+    order = wide.reshape(C1, 4).T.reshape(-1)
+    return turn_back(prepare_out, packed, table, order, old.T).T
+
+
+def weave(source, rows, put):
+    for t in range(CH // LANES):
+        b, begin = divmod(t * LANES, C1)
+        u, rest = divmod(begin, LANES)
+        place = lax.broadcasted_iota(jnp.int32, (rows, LANES), 1)
+        value = source[u, pl.ds(b, rows, stride=4), :]
+        if rest:
+            if begin + LANES - rest < C1:
+                after = source[u + 1, pl.ds(b, rows, stride=4), :]
+                value = jnp.where(place >= rest, value, after)
+            value = pltpu.roll(value, LANES - rest, 1)
+        left = C1 - begin
+        if left < LANES:
+            following = source[0, pl.ds(b + 1, rows, stride=4), :]
+            value = jnp.where(place < left, value, pltpu.roll(following, left, 1))
+        put(t, value)
+
+
+def place_kernel(
+    norm_t, branch, pre, act, wide, up, down, piece_in, piece_dw, piece_head, piece_vec,
+    grad, hot, hidden, out, loose, up_rows, down_rows, sem_out, sems,
+):
+    step = pl.program_id(0)
+    steps = pl.num_programs(0)
+    ratio = CH // LANES
+    lines = TILE // 4
+    tiles = TILE // LANES
+
+    def out_copy(n):
+        rows = lines * ratio
+        return pltpu.make_async_copy(
+            out.at[pl.ds(pl.multiple_of(n * rows, 8), rows)],
+            grad.at[pl.ds(pl.multiple_of(ROW_AT[4] + n * rows, 8), rows)],
+            sem_out.at[n],
+        )
+
+    copies = [
+        pltpu.make_async_copy(ref, grad.at[pl.ds(row, ref.shape[0])], sems.at[i])
+        for i, (ref, row) in enumerate(
+            (
+                (piece_in, 0), (piece_dw, ROW_AT[2]), (piece_head, ROW_AT[6]), (piece_vec, ROW_AT[7]),
+                (up_rows, ROW_AT[5]), (down_rows, ROW_AT[1]), (hidden, ROW_AT[3]),
+            )
+        )
+    ]
+
+    @pl.when(step == 0)
+    def _():
+        for copy in copies[:4]:
+            copy.start()
+
+    for number, (source, target) in enumerate(((up, up_rows), (down, down_rows))):
+        @pl.when(step == number)
+        def _(number=number, source=source, target=target):
+            for u in range(-(-C1 // LANES)):
+                width = min(LANES, C1 - u * LANES)
+                loose[u, :, 0:width] = source[:, u * LANES : u * LANES + width]
+
+            def put(t, value):
+                target[pl.ds(t, C1 // 4, stride=ratio), :] = value
+
+            weave(loose, C1 // 4, put)
+            copies[4 + number].start()
+
+    def build(b, carry):
+        at = pl.ds(pl.multiple_of(b * LANES, LANES), LANES)
+        line = lax.broadcasted_iota(jnp.int32, (LANES, TILE), 0) + b * LANES
+        hot[at, :] = one_hot(line == wide[...])
+        return carry
+
+    lax.fori_loop(0, CH // LANES, build, 0)
+    turned_pre = product(pre[...], hot[...]).astype(jnp.bfloat16)
+    part = product(norm_t[...], turned_pre)
+    for t in range(tiles):
+        hidden[pl.ds(step * tiles + t, C1, stride=ratio), :] = part[:, t * LANES : (t + 1) * LANES]
+    turned_act = product(act[...], hot[...]).astype(jnp.bfloat16)
+    part = lax.dot_general(
+        turned_act, branch[...], (((0,), (0,)), ((), ())), preferred_element_type=jnp.float32
+    )
+    for u in range(-(-C1 // LANES)):
+        loose[u, 0:TILE, :] = part[:, u * LANES : (u + 1) * LANES]
+
+    def put_out(t, value):
+        out[pl.ds(step * (lines * ratio) + t, lines, stride=ratio), :] = value
+
+    weave(loose, lines, put_out)
+    out_copy(step).start()
+
+    @pl.when(step == steps - 1)
+    def _():
+        copies[6].start()
+
+        def finish(n, carry):
+            out_copy(n).wait()
+            return carry
+
+        lax.fori_loop(0, steps, finish, 0)
+        for copy in copies:
+            copy.wait()
+
+
+def place_gradients(space, norm_t, branch, pre, act, wide, up, down, pieces):
+    whole = lambda *shape: pl.BlockSpec(shape, lambda i: (0,) * len(shape))
+    hbm = pl.BlockSpec(memory_space=pl.ANY)
+    rows = pre.shape[0]
+    padded = -(-C1 // LANES) * LANES
+    return pl.pallas_call(
+        place_kernel,
+        out_shape=jax.ShapeDtypeStruct((space, LANES), jnp.float32),
+        grid=(CH // TILE,),
+        in_specs=[
+            whole(C1, rows), whole(rows, padded), whole(rows, CH), whole(rows, CH),
+            pl.BlockSpec((1, TILE), lambda i: (0, i)),
+            whole(C1, C1), whole(C1, C1), hbm, hbm, hbm, hbm,
+        ],
+        out_specs=hbm,
+        scratch_shapes=[
+            pltpu.VMEM((CH, TILE), jnp.bfloat16),
+            pltpu.VMEM((C1 * CH // LANES, LANES), jnp.float32),
+            pltpu.VMEM((C1 * CH // LANES, LANES), jnp.float32),
+            pltpu.VMEM((padded // LANES, C1, LANES), jnp.float32),
+            pltpu.VMEM((C1 * C1 // LANES, LANES), jnp.float32),
+            pltpu.VMEM((C1 * C1 // LANES, LANES), jnp.float32),
+            pltpu.SemaphoreType.DMA((CH // TILE,)),
+            pltpu.SemaphoreType.DMA((7,)),
+        ],
+        compiler_params=pltpu.CompilerParams(vmem_limit_bytes=58 << 20),
+    )(norm_t, branch, pre, act, wide[None, :], up, down, *pieces)
+
+
+C0P = 256
+C1P = 896
+CIP = 128
+EDGE = 16
+CURVE = 0.7978845608028654
+CUBE = 0.044715
+
+
+def inner_rows(left, right):
+    return lax.dot_general(left, right, (((0,), (0,)), ((), ())), preferred_element_type=jnp.float32)
+
+
+def column_sum(values):
+    return jnp.sum(values.astype(jnp.float32), axis=0, keepdims=True)
+
+
+def gelu(t):
+    return 0.5 * t * (1.0 + jnp.tanh(CURVE * (t + CUBE * (t * t * t))))
+
+
+def gelu_slope(t):
+    bend = jnp.tanh(CURVE * (t + CUBE * (t * t * t)))
+    return 0.5 * (1.0 + bend) + 0.5 * t * (1.0 - bend * bend) * (CURVE * (1.0 + 3.0 * CUBE * (t * t)))
+
+
+def halo_kernel(nr, nc, width, cells, out, sem_s, sem_r):
+    r = lax.axis_index("rows")
+    c = lax.axis_index("cols")
+    height, breadth = cells.shape[1], cells.shape[2]
+    ways = [(dr, dc) for dr in (-1, 0, 1) for dc in (-1, 0, 1) if (dr, dc) != (0, 0)]
+
+    def there(dr):
+        return (r + dr >= 0) & (r + dr < nr)
+
+    barrier = pltpu.get_barrier_semaphore()
+    for dr, dc in ways:
+        @pl.when(there(dr))
+        def _(dr=dr, dc=dc):
+            pl.semaphore_signal(
+                barrier, inc=1, device_id=(r + dr, lax.rem(c + dc + nc, nc)), device_id_type=MESH
+            )
+
+    edge = (r == 0) | (r == nr - 1)
+
+    @pl.when(edge)
+    def _():
+        pl.semaphore_wait(barrier, 5)
+
+    @pl.when(jnp.logical_not(edge))
+    def _():
+        pl.semaphore_wait(barrier, 8)
+
+    def copy(i, receive):
+        dr, dc = ways[i]
+        rows_from = {-1: (0, width), 0: (0, height), 1: (height - width, width)}[dr]
+        rows_to = {-1: height + width, 0: width, 1: 0}[dr]
+        cols_from = {-1: (0, EDGE), 0: (0, breadth), 1: (breadth - EDGE, EDGE)}[dc]
+        cols_to = {-1: EDGE + breadth, 0: EDGE, 1: 0}[dc]
+        sign = -1 if receive else 1
+        return pltpu.make_async_remote_copy(
+            src_ref=cells.at[:, pl.ds(*rows_from), pl.ds(*cols_from)],
+            dst_ref=out.at[:, pl.ds(rows_to, rows_from[1]), pl.ds(cols_to, cols_from[1])],
+            send_sem=sem_s.at[i],
+            recv_sem=sem_r.at[i],
+            device_id=(r + sign * dr, lax.rem(c + sign * dc + nc, nc)),
+            device_id_type=MESH,
+        )
+
+    order = sorted(range(8), key=lambda i: (ways[i][1] != 0, ways[i][0] == 0))
+    for i in order:
+        @pl.when(there(ways[i][0]))
+        def _(i=i):
+            copy(i, False).start()
+
+    for m in range(cells.shape[0]):
+        for row in range(height):
+            out[m, width + row, EDGE : EDGE + breadth, :] = cells[m, row]
+
+    @pl.when(r == 0)
+    def _():
+        out[:, 0:width] = jnp.zeros((out.shape[0], width) + out.shape[2:], out.dtype)
+
+    @pl.when(r == nr - 1)
+    def _():
+        out[:, height + width :] = jnp.zeros((out.shape[0], width) + out.shape[2:], out.dtype)
+
+    for i in order:
+        @pl.when(there(-ways[i][0]))
+        def _(i=i):
+            copy(i, True).wait_recv()
+
+        @pl.when(there(ways[i][0]))
+        def _(i=i):
+            copy(i, False).wait_send()
+
+
+def halo(nr, nc, width, cells, identity):
+    batch, height, breadth, chans = cells.shape
+    vmem = pl.BlockSpec(memory_space=pltpu.VMEM)
+    return pl.pallas_call(
+        functools.partial(halo_kernel, nr, nc, width),
+        out_shape=jax.ShapeDtypeStruct(
+            (batch, height + 2 * width, breadth + 2 * EDGE, chans), cells.dtype
+        ),
+        in_specs=[vmem],
+        out_specs=vmem,
+        scratch_shapes=[pltpu.SemaphoreType.DMA((8,)), pltpu.SemaphoreType.DMA((8,))],
+        compiler_params=pltpu.CompilerParams(
+            collective_id=identity, has_side_effects=True, vmem_limit_bytes=24 << 20
+        ),
+    )(cells)
+
+
+def input_kernel(state, w_in, b_in, w_down, b_down, taps, a_zero, h_zero, coarse, coarse_low, wide):
+    batch, rows, breadth, _ = state.shape
+    half_h, half_w = (rows - 2) // 2, (breadth - 2 * EDGE) // 2
+    for m in range(batch):
+        for y in range(rows):
+            wide[m, y] = state[m, y].astype(jnp.float32)
+    for m in range(batch):
+        for y in range(rows):
+            for f in range(4):
+                line = wide[m, y, pl.ds(EDGE - 1 + f, half_w, stride=2), :].astype(jnp.bfloat16)
+                for dy in range(3):
+                    i, sy = divmod(y - dy, 2)
+                    if not 0 <= i < half_h:
+                        continue
+                    for dx in range(3):
+                        if 0 <= f - dx < 2:
+                            begin = (m * half_h + i) * half_w
+                            tap = (dy * 3 + dx) * CIP
+                            taps[sy * 2 + f - dx, begin : begin + half_w, tap : tap + CIP] = line
+    coarse[...] = jnp.broadcast_to(b_down[...], coarse.shape)
+    for s in range(4):
+        value = product(taps[s], w_in[...]) + b_in[...]
+        a_zero[s] = value
+        value = gelu(value)
+        h_zero[s] = value
+        coarse[...] += product(value.astype(jnp.bfloat16), w_down[s])
+    coarse_low[...] = coarse[...].astype(jnp.bfloat16).reshape(coarse_low.shape)
+
+
+def input_part(state, w_in, b_in, w_down, b_down):
+    batch, rows, breadth, _ = state.shape
+    half_h, half_w = (rows - 2) // 2, (breadth - 2 * EDGE) // 2
+    cells = batch * half_h * half_w
+    vmem = pl.BlockSpec(memory_space=pltpu.VMEM)
+    return pl.pallas_call(
+        input_kernel,
+        out_shape=(
+            jax.ShapeDtypeStruct((4, cells, 9 * CIP), jnp.bfloat16),
+            jax.ShapeDtypeStruct((4, cells, C0P), jnp.float32),
+            jax.ShapeDtypeStruct((4, cells, C0P), jnp.float32),
+            jax.ShapeDtypeStruct((cells, C1P), jnp.float32),
+            jax.ShapeDtypeStruct((batch, half_h, half_w, C1P), jnp.bfloat16),
+        ),
+        in_specs=[vmem] * 5,
+        out_specs=tuple([vmem] * 5),
+        scratch_shapes=[pltpu.VMEM(state.shape, jnp.float32)],
+        compiler_params=pltpu.CompilerParams(vmem_limit_bytes=40 << 20),
+    )(state, w_in, b_in, w_down, b_down)
+
+
+def spread_lanes(padded, held):
+    for m in range(padded.shape[0]):
+        def body(y, carry, m=m):
+            for u in range(C1P // LANES):
+                held[u, m, y] = padded[m, y, :, u * LANES : (u + 1) * LANES].astype(jnp.float32)
+            return carry
+
+        lax.fori_loop(0, padded.shape[1], body, 0)
+
+
+def convolve(held, w_dw, put, back):
+    tiles, batch, rows, breadth = held.shape[:4]
+    height, half_w = rows - 6, breadth - 2 * EDGE
+
+    def body(number, carry):
+        u, m = number // batch, number % batch
+        sums = [jnp.zeros((half_w, LANES), jnp.float32) for _ in range(height)]
+        for x in range(7):
+            for y in range(rows):
+                window = held[u, m, y, pl.ds(EDGE - 3 + x, half_w), :]
+                for i in range(height):
+                    if 0 <= y - i < 7:
+                        tap = (6 - (y - i)) * 7 + 6 - x if back else (y - i) * 7 + x
+                        sums[i] = sums[i] + window * w_dw[u, pl.ds(tap, 1), :]
+        for i in range(height):
+            put(u, m, i, sums[i])
+        return carry
+
+    lax.fori_loop(0, tiles * batch, body, 0)
+
+
+def rows_at(m, i, height, half_w):
+    return pl.ds(pl.multiple_of((m * height + i) * half_w, half_w), half_w)
+
+
+def lanes_at(u):
+    return pl.ds(pl.multiple_of(u * LANES, LANES), LANES)
+
+
+PART = 640
+
+
+def middle_kernel(
+    padded, coarse, h_zero, target, weight, w_dw, w_hidden, w_out_t, w_up, w_head,
+    b_dw, gain, shift, b_hidden, b_out, b_up, b_head,
+    normed, act, grad_pre, grad_mixed, grad_branch, grad_summed, grad_conv, d_up, d_head, sums,
+    conv, total,
+):
+    cells = coarse.shape[0]
+    batch, rows, breadth, _ = padded.shape
+    height, half_w = rows - 6, breadth - 2 * EDGE
+
+    def depthwise(held):
+        spread_lanes(padded, held)
+
+        def put(u, m, i, value):
+            conv[rows_at(m, i, height, half_w), lanes_at(u)] = value
+
+        convolve(held, w_dw, put, False)
+
+    pl.run_scoped(depthwise, pltpu.VMEM((C1P // LANES, batch, rows, breadth, LANES), jnp.float32))
+    pl.run_scoped(
+        functools.partial(
+            pointwise_kernel, coarse, h_zero, target, weight, w_hidden, w_out_t, w_up, w_head,
+            b_dw, gain, shift, b_hidden, b_out, b_up, b_head,
+            normed, act, grad_pre, grad_mixed, grad_branch, grad_summed, grad_conv, d_up, d_head, sums,
+            conv, total,
+        ),
+        pltpu.VMEM((cells, CH), jnp.float32),
+    )
+
+
+def pointwise_kernel(
+    coarse, h_zero, target, weight, w_hidden, w_out_t, w_up, w_head,
+    b_dw, gain, shift, b_hidden, b_out, b_up, b_head,
+    normed, act, grad_pre, grad_mixed, grad_branch, grad_summed, grad_conv, d_up, d_head, sums,
+    conv, total, pre,
+):
+    inside = lax.broadcasted_iota(jnp.int32, (1, C1P), 1) < C1
+    values = conv[...] + b_dw[...]
+    mean = jnp.sum(values, axis=1, keepdims=True) * (1.0 / C1)
+    centered = jnp.where(inside, values - mean, 0.0)
+    scale = lax.rsqrt(jnp.sum(centered * centered, axis=1, keepdims=True) * (1.0 / C1) + 1e-06)
+    conv[...] = centered * scale
+    normed[...] = (conv[...] * gain[...] + shift[...]).astype(jnp.bfloat16)
+
+    total[...] = coarse[...]
+    for begin in range(0, CH, PART):
+        span = slice(begin, begin + PART)
+        value = product(normed[:, :C1], w_hidden[:, span]) + b_hidden[:, span]
+        pre[:, span] = value
+        act[:, span] = gelu(value).astype(jnp.bfloat16)
+        total[:, :C1] += product_t(act[:, span], w_out_t[:, span])
+    mixed = (total[...] + b_out[...]).astype(jnp.bfloat16)
+
+    grad_mixed[...] = jnp.zeros_like(grad_mixed)
+    loss = jnp.zeros((1, CIP), jnp.float32)
+    head_sum = jnp.zeros((1, CIP), jnp.float32)
+    up_sum = jnp.zeros((1, C0P), jnp.float32)
+    for s in range(4):
+        upper = product(mixed[:, :C1], w_up[s]) + b_up[...]
+        summed = (upper + h_zero[s]).astype(jnp.bfloat16)
+        error = product(summed, w_head[...]) + b_head[...] - target[s].astype(jnp.float32)
+        weighted = weight[s] * error
+        loss = loss + column_sum(weighted * error)
+        grad_out = (2.0 * weighted).astype(jnp.bfloat16)
+        head_sum = head_sum + column_sum(grad_out)
+        if s == 0:
+            d_head[...] = inner_rows(summed, grad_out)
+        else:
+            d_head[...] += inner_rows(summed, grad_out)
+        spread = product_t(grad_out, w_head[...])
+        grad_summed[s] = spread
+        grad_upper = spread.astype(jnp.bfloat16)
+        up_sum = up_sum + column_sum(grad_upper)
+        d_up[s] = inner_rows(mixed, grad_upper)
+        grad_mixed[:, :C1] += product_t(grad_upper, w_up[s])
+    grad_branch[...] = grad_mixed[...].astype(jnp.bfloat16)
+    sums[...] = jnp.zeros_like(sums)
+    sums[0:1, 0:CIP] = loss
+    sums[1:2, 0:CIP] = head_sum
+    sums[2:3, 0:C0P] = up_sum
+    sums[3:4, 0:C1P] = column_sum(grad_branch[...])
+
+    total[...] = jnp.zeros_like(total)
+    for begin in range(0, CH, PART):
+        span = slice(begin, begin + PART)
+        value = product(grad_branch[:, :C1], w_out_t[:, span]) * gelu_slope(pre[:, span])
+        low = value.astype(jnp.bfloat16)
+        grad_pre[:, span] = low
+        sums[4:5, span] = column_sum(low)
+        total[:, :C1] += product_t(low, w_hidden[:, span])
+
+    grad_normed = total[...]
+    sums[5:6, 0:C1P] = column_sum(grad_normed * conv[...])
+    sums[6:7, 0:C1P] = column_sum(grad_normed)
+    inward = grad_normed * gain[...]
+    first = jnp.sum(inward, axis=1, keepdims=True) * (1.0 / C1)
+    second = jnp.sum(inward * conv[...], axis=1, keepdims=True) * (1.0 / C1)
+    value = scale * jnp.where(inside, inward - first - conv[...] * second, 0.0)
+    low = value.astype(jnp.bfloat16)
+    sums[7:8, 0:C1P] = column_sum(low)
+    grad_conv[...] = low.reshape(grad_conv.shape)
+
+
+def middle_part(padded, coarse, h_zero, target, weight, *rest):
+    cells = coarse.shape[0]
+    batch, rows, breadth, _ = padded.shape
+    half_h, half_w = rows - 6, breadth - 2 * EDGE
+    vmem = pl.BlockSpec(memory_space=pltpu.VMEM)
+    f32, low = jnp.float32, jnp.bfloat16
+    return pl.pallas_call(
+        middle_kernel,
+        out_shape=(
+            jax.ShapeDtypeStruct((cells, C1P), low),
+            jax.ShapeDtypeStruct((cells, CH), low),
+            jax.ShapeDtypeStruct((cells, CH), low),
+            jax.ShapeDtypeStruct((cells, C1P), f32),
+            jax.ShapeDtypeStruct((cells, C1P), low),
+            jax.ShapeDtypeStruct((4, cells, C0P), f32),
+            jax.ShapeDtypeStruct((batch, half_h, half_w, C1P), low),
+            jax.ShapeDtypeStruct((4, C1P, C0P), f32),
+            jax.ShapeDtypeStruct((C0P, CIP), f32),
+            jax.ShapeDtypeStruct((8, CH), f32),
+        ),
+        in_specs=[vmem] * 17,
+        out_specs=tuple([vmem] * 10),
+        scratch_shapes=[
+            pltpu.VMEM((cells, C1P), f32),
+            pltpu.VMEM((cells, C1P), f32),
+        ],
+        compiler_params=pltpu.CompilerParams(vmem_limit_bytes=62 << 20),
+    )(padded, coarse, h_zero, target, weight, *rest)
+
+
+def outer_kernel(
+    padded, grad_padded, grad_conv, grad_mixed, grad_summed, a_zero, h_zero, taps, w_dw, w_down,
+    d_dw, d_down, d_in, sums, held, conv,
+):
+    batch, height, half_w, _ = grad_conv.shape
+    spread_lanes(padded, held)
+    tiles = C1P // LANES
+    d_dw[...] = jnp.zeros_like(d_dw)
+
+    def taps_of(number, carry):
+        u, m = number // batch, number % batch
+        grads = [grad_conv[m, i, :, lanes_at(u)].astype(jnp.float32) for i in range(height)]
+        for x in range(7):
+            found = [jnp.zeros((8, LANES), jnp.float32) for _ in range(7)]
+            for y in range(height + 6):
+                window = held[u, m, y, pl.ds(EDGE - 3 + x, half_w), :]
+                for i in range(height):
+                    if 0 <= y - i < 7:
+                        term = (window * grads[i]).reshape(half_w // 8, 8, LANES)
+                        found[y - i] = found[y - i] + jnp.sum(term, axis=0)
+            for dy in range(7):
+                d_dw[u, pl.ds(dy * 7 + x, 1), :] += jnp.sum(found[dy], axis=0, keepdims=True)
+        return carry
+
+    lax.fori_loop(0, tiles * batch, taps_of, 0)
+    spread_lanes(grad_padded, held)
+
+    def put(u, m, i, value):
+        conv[rows_at(m, i, height, half_w), lanes_at(u)] = value
+
+    convolve(held, w_dw, put, True)
+    grad_coarse = (conv[...] + grad_mixed[...]).astype(jnp.bfloat16)
+    sums[...] = jnp.zeros_like(sums)
+    sums[0:1, 0:C1P] = column_sum(grad_coarse)
+    in_sum = jnp.zeros((1, C0P), jnp.float32)
+    for s in range(4):
+        d_down[s] = inner_rows(h_zero[s].astype(jnp.bfloat16), grad_coarse)
+        grad_h = product_t(grad_coarse, w_down[s]) + grad_summed[s]
+        grad_a = (gelu_slope(a_zero[s]) * grad_h).astype(jnp.bfloat16)
+        in_sum = in_sum + column_sum(grad_a)
+        if s == 0:
+            d_in[...] = inner_rows(taps[s], grad_a)
+        else:
+            d_in[...] += inner_rows(taps[s], grad_a)
+    sums[1:2, 0:C0P] = in_sum
+
+
+def outer_part(padded, grad_padded, grad_conv, grad_mixed, grad_summed, a_zero, h_zero, taps, w_dw, w_down):
+    cells = grad_mixed.shape[0]
+    batch, rows, breadth, _ = padded.shape
+    vmem = pl.BlockSpec(memory_space=pltpu.VMEM)
+    f32 = jnp.float32
+    return pl.pallas_call(
+        outer_kernel,
+        out_shape=(
+            jax.ShapeDtypeStruct((C1P // LANES, 56, LANES), f32),
+            jax.ShapeDtypeStruct((4, C0P, C1P), f32),
+            jax.ShapeDtypeStruct((9 * CIP, C0P), f32),
+            jax.ShapeDtypeStruct((8, C1P), f32),
+        ),
+        in_specs=[vmem] * 10,
+        out_specs=tuple([vmem] * 4),
+        scratch_shapes=[
+            pltpu.VMEM((C1P // LANES, batch, rows, breadth, LANES), f32),
+            pltpu.VMEM((cells, C1P), f32),
+        ],
+        compiler_params=pltpu.CompilerParams(vmem_limit_bytes=62 << 20),
+    )(padded, grad_padded, grad_conv, grad_mixed, grad_summed, a_zero, h_zero, taps, w_dw, w_down)
 
 
 def split_vector(vector):
@@ -594,79 +1295,13 @@
     return pieces
 
 
-def product(left, right):
-    return jnp.dot(left, right, preferred_element_type=jnp.float32)
-
-
-def inner_rows(left, right):
-    return jnp.einsum("nk,nd->kd", left, right, preferred_element_type=jnp.float32)
-
-
-def outer_cols(left, right):
-    return jnp.einsum("nd,kd->nk", left, right, preferred_element_type=jnp.float32)
-
-
-def column_sum(values):
-    return jnp.sum(values, axis=0, dtype=jnp.float32)
-
-
-def clear_edges(padded, width):
-    place = lax.axis_index("rows")
-    count = lax.axis_size("rows")
-    line = jnp.arange(padded.shape[1])[None, :, None, None]
-    top = (place == 0) & (line < width)
-    bottom = (place == count - 1) & (line >= padded.shape[1] - width)
-    return jnp.where(top | bottom, jnp.zeros((), padded.dtype), padded)
-
-
-def to_coarse(field, height, breadth):
-    chans = field.shape[-1]
-    return (
-        field.reshape(MB, height // 2, 2, breadth // 2, 2, chans)
-        .transpose(0, 1, 3, 2, 4, 5)
-        .reshape(-1, 4 * chans)
-    )
-
-
-def to_fine(field, height, breadth):
-    chans = field.shape[-1] // 4
-    return (
-        field.reshape(MB, height // 2, breadth // 2, 2, 2, chans)
-        .transpose(0, 1, 3, 2, 4, 5)
-        .reshape(-1, chans)
-    )
-
-
-def layer_norm(values, gain, shift):
-    mean = jnp.mean(values, -1, keepdims=True)
-    centered = values - mean
-    var = jnp.mean(centered * centered, -1, keepdims=True)
-    return centered * lax.rsqrt(var + 1e-06) * gain + shift
-
-
-def depthwise(padded, w_dw, height, breadth, back):
-    total = jnp.zeros((MB, height, breadth, padded.shape[-1]), jnp.float32)
-    for y in range(7):
-        for x in range(7):
-            at_y, at_x = (6 - y, 6 - x) if back else (y, x)
-            window = padded[:, at_y : at_y + height, at_x : at_x + breadth].astype(jnp.float32)
-            total = total + window * w_dw[y * 7 + x].astype(jnp.float32)
-    return total
-
-
-def depthwise_kernel_grad(padded, grad_map, height, breadth):
-    rows_out = []
-    grad_float = grad_map.astype(jnp.float32)
-    for y in range(7):
-        for x in range(7):
-            window = padded[:, y : y + height, x : x + breadth].astype(jnp.float32)
-            rows_out.append(jnp.sum(window * grad_float, axis=(0, 1, 2)))
-    return jnp.stack(rows_out)
-
-
 def as_rows(piece, rows):
     flat = piece.reshape(-1)
     return jnp.pad(flat, (0, rows * LANES - flat.shape[0])).reshape(rows, LANES)
+
+
+def widened(array, *shape):
+    return jnp.pad(array, [(0, full - now) for full, now in zip(shape, array.shape)])
 
 
 def on_device(
@@ -688,120 +1323,103 @@
     moment_first,
     moment_second,
 ):
+    rows, cols = lax.axis_size("rows"), lax.axis_size("cols")
     b_in, b_down, b_dw, gain, shift, b_hidden, b_out, b_up, b_head = split_vector(biases_gains)
     weight = land_mask.astype(jnp.float32) * volume
     height, breadth = weight.shape
     half_h, half_w = (height // 2, breadth // 2)
-    weight_col = jnp.tile(weight.reshape(-1, 1), (MB, 1))
+    cells = MB * half_h * half_w
     matrices = (w_in, w_down, w_dw, w_hidden, w_out, w_up, w_head)
-    sides = (("rows", 1), ("cols", 2))
 
     def dates(field):
-        return jnp.concatenate(
+        picked = jnp.concatenate(
             [lax.dynamic_slice_in_dim(field, date_index[m], 1, 0) for m in range(MB)]
         )
+        return widened(picked, MB, height, breadth, CIP)
+
+    def by_subcell(field):
+        chans = field.shape[-1]
+        return (
+            field.reshape(MB, half_h, 2, half_w, 2, chans)
+            .transpose(2, 4, 0, 1, 3, 5)
+            .reshape(4, cells, chans)
+        )
+
+    def line(vector, size):
+        return widened(vector[None, :], 1, size)
 
     narrow_turn = (jnp.arange(C1)[:, None] == perm_narrow[None, :]).astype(jnp.bfloat16)
-    wide_turn = (jnp.arange(CH)[:, None] == perm_wide[None, :]).astype(jnp.bfloat16)
-
-    def turned(values, turn):
-        return product(values, turn).astype(jnp.bfloat16)
-
-    state, target = dates(inputs), dates(targets)
-    state_pad = clear_edges(padded_2(state, sides, 1), 1)
-    taps = jnp.concatenate(
-        [state_pad[:, y : y + height, x : x + breadth] for y in range(3) for x in range(3)], -1
-    ).reshape(-1, 9 * CI)
-    a_zero = product(taps, w_in) + b_in
-    h_zero, gelu_zero = jax.vjp(jax.nn.gelu, a_zero)
-    h_low = h_zero.astype(jnp.bfloat16)
-    patches = to_coarse(h_low.reshape(MB, height, breadth, C0), height, breadth)
-    coarse = product(patches, w_down) + b_down
-    coarse_low = coarse.astype(jnp.bfloat16).reshape(MB, half_h, half_w, C1)
-    coarse_pad = clear_edges(padded_2(coarse_low, sides, 3), 3)
-    conv_out = depthwise(coarse_pad, w_dw, half_h, half_w, False).reshape(-1, C1) + b_dw
-    normed, norm_pull = jax.vjp(layer_norm, conv_out, gain, shift)
-    normed_low = normed.astype(jnp.bfloat16)
-    pre = product(normed_low, w_hidden) + b_hidden
-    act, act_pull = jax.vjp(jax.nn.gelu, pre)
-    act_low = act.astype(jnp.bfloat16)
-    branch = product(act_low, w_out) + b_out
-    mixed_low = (coarse + branch).astype(jnp.bfloat16)
-    upper = product(mixed_low, w_up) + jnp.tile(b_up, 4)
-    summed_low = (to_fine(upper, height, breadth) + h_zero).astype(jnp.bfloat16)
-    output = product(summed_low, w_head) + b_head
-    error = output - target.reshape(-1, CI).astype(jnp.float32)
-    loss_local = jnp.sum(weight_col * error * error)
-    grad_out = (2.0 * weight_col * error).astype(jnp.bfloat16)
-    d_head = inner_rows(summed_low, grad_out)
-    grad_summed = outer_cols(grad_out, w_head)
-    grad_upper = to_coarse(
-        grad_summed.astype(jnp.bfloat16).reshape(MB, height, breadth, C0), height, breadth
+    w_in_p = widened(w_in.reshape(9, CI, C0), 9, CIP, C0P).reshape(9 * CIP, C0P)
+    w_down_p = widened(w_down.reshape(4, C0, C1), 4, C0P, C1P)
+    w_up_p = widened(w_up.reshape(C1, 4, C0).transpose(1, 0, 2), 4, C1, C0P)
+    w_dw_p = widened(w_dw.astype(jnp.float32), 56, C1P).reshape(56, C1P // LANES, LANES).transpose(1, 0, 2)
+    target = by_subcell(dates(targets))
+    weight_col = jnp.broadcast_to(weight[None, :, :, None], (MB, height, breadth, 1))
+    weight_col = jnp.broadcast_to(by_subcell(weight_col), (4, cells, CIP))
+
+    state = halo(rows, cols, 1, dates(inputs), 1)
+    taps, a_zero, h_zero, coarse, coarse_low = input_part(
+        state, w_in_p, line(b_in, C0P), w_down_p, line(b_down, C1P)
     )
-    d_up = inner_rows(mixed_low, grad_upper)
-    grad_mixed = outer_cols(grad_upper, w_up)
-    grad_branch = grad_mixed.astype(jnp.bfloat16)
-    d_out = inner_rows(turned(act_low, wide_turn), turned(grad_branch, narrow_turn))
-    grad_act = outer_cols(grad_branch, w_out)
-    grad_pre = act_pull(grad_act)[0].astype(jnp.bfloat16)
-    d_hidden = inner_rows(turned(normed_low, narrow_turn), turned(grad_pre, wide_turn))
-    grad_normed = outer_cols(grad_pre, w_hidden)
-    grad_conv, d_gain, d_shift = norm_pull(grad_normed)
-    grad_conv = grad_conv.astype(jnp.bfloat16)
-    grad_map = grad_conv.reshape(MB, half_h, half_w, C1)
-    d_dw = depthwise_kernel_grad(coarse_pad, grad_map, half_h, half_w)
-    grad_pad = clear_edges(padded_2(grad_map, sides, 3), 3)
-    grad_coarse_low = depthwise(grad_pad, w_dw, half_h, half_w, True).reshape(-1, C1)
-    grad_coarse = (grad_coarse_low + grad_mixed).astype(jnp.bfloat16)
-    d_down = inner_rows(patches, grad_coarse)
-    grad_h = to_fine(outer_cols(grad_coarse, w_down), height, breadth) + grad_summed
-    grad_a = gelu_zero(grad_h)[0].astype(jnp.bfloat16)
-    d_in = inner_rows(taps, grad_a)
+    padded = halo(rows, cols, 3, coarse_low, 2)
+    (
+        normed, act, grad_pre, grad_mixed, grad_branch, grad_summed, grad_conv, d_up, d_head, sums
+    ) = middle_part(
+        padded, coarse, h_zero, target, weight_col, w_dw_p, w_hidden, w_out.T, w_up_p,
+        widened(w_head, C0P, CIP), line(b_dw, C1P), line(gain, C1P), line(shift, C1P),
+        line(b_hidden, CH), line(b_out, C1P), line(b_up, C0P), line(b_head, CIP),
+    )
+    grad_padded = halo(rows, cols, 3, grad_conv, 3)
+    d_dw, d_down, d_in, sums_out = outer_part(
+        padded, grad_padded, grad_conv, grad_mixed, grad_summed, a_zero, h_zero, taps, w_dw_p, w_down_p
+    )
+    d_up = d_up[:, :C1, :C0].transpose(1, 0, 2).reshape(C1, 4 * C0)
+    d_down = d_down[:, :C0, :C1].reshape(4 * C0, C1)
+    d_in = d_in.reshape(9, CIP, C0P)[:, :CI, :C0].reshape(9 * CI, C0)
+    d_dw = d_dw[:, :49].transpose(1, 0, 2).reshape(49, C1P)[:, :C1]
     d_vector = jnp.concatenate(
         [
-            column_sum(grad_a),
-            column_sum(grad_coarse),
-            column_sum(grad_conv),
-            d_gain,
-            d_shift,
-            column_sum(grad_pre),
-            column_sum(grad_branch),
-            jnp.sum(column_sum(grad_upper).reshape(4, C0), 0),
-            column_sum(grad_out),
+            sums_out[1, :C0], sums_out[0, :C1], sums[7, :C1], sums[5, :C1], sums[6, :C1],
+            sums[4], sums[3, :C1], sums[2, :C0], sums[1, :CI],
         ]
     )
-    terms = (d_in, d_down, d_dw, d_hidden, d_out, d_up, d_head, d_vector)
-    rows, cols = lax.axis_size("rows"), lax.axis_size("cols")
+    loss_local = jnp.sum(sums[0, :CIP])
     space = Plan(rows, cols, PADDED).space
-    ends = ROW_AT[1:] + [space]
-    blocks = [jnp.zeros((ROW_AT[0], LANES), jnp.float32)]
-    for term, begin, end in zip(terms, ROW_AT, ends):
-        blocks.append(as_rows(term, end - begin))
-    grad = jnp.concatenate(blocks)
-    line = jnp.arange(8)[:, None]
-    extra = jnp.where(line == 0, loss_local, jnp.where(line == 1, jnp.sum(weight), 0.0))
+    norm_t = jnp.einsum(
+        "nk,kj->jn", normed[:, :C1], narrow_turn, preferred_element_type=jnp.float32
+    ).astype(jnp.bfloat16)
+    branch_r = product(grad_branch[:, :C1], widened(narrow_turn, C1, C1P)).astype(jnp.bfloat16)
+    pieces = (
+        jnp.pad(as_rows(d_in, ROW_AT[1] - ROW_AT[0]), ((ROW_AT[0], 0), (0, 0))),
+        as_rows(d_dw, ROW_AT[3] - ROW_AT[2]),
+        as_rows(d_head[:C0, :CI], ROW_AT[7] - ROW_AT[6]),
+        as_rows(d_vector, space - ROW_AT[7]),
+    )
+    grad = place_gradients(space, norm_t, branch_r, grad_pre, act, perm_wide, d_up, d_down, pieces)
+    lead = jnp.arange(8)[:, None]
+    extra = jnp.where(lead == 0, loss_local, jnp.where(lead == 1, jnp.sum(weight), 0.0))
     extra = jnp.where(jnp.arange(LANES)[None, :] == 0, extra, 0.0)
     plan, (gathered, first, second, totals) = exchange(
         rows, cols, grad, moment_first, moment_second, extra
     )
-    full = gathered[:, : plan.share, :].astype(jnp.float32).reshape(-1)
-    back_narrow = jnp.zeros((C1,), jnp.int32).at[perm_narrow].set(jnp.arange(C1, dtype=jnp.int32))
-    back_wide = jnp.zeros((CH,), jnp.int32).at[perm_wide].set(jnp.arange(CH, dtype=jnp.int32))
+    hidden_p, out_p, new_up, new_down, small_a, small_b, small_c = unpack(plan, gathered, w_up, w_down)
+    small = {0: (small_a, 0), 2: (small_b, 1), 6: (small_c, 2), 7: (small_c, 2)}
+    whole = {
+        1: new_down,
+        3: rebuild_hidden(hidden_p, perm_narrow, perm_wide, w_hidden),
+        4: rebuild_out(out_p, perm_narrow, perm_wide, w_out),
+        5: new_up,
+    }
     olds = matrices + (biases_gains,)
     news = []
     for index, old in enumerate(olds):
-        start = FLAT_AT[index]
-        piece = full[start : start + old.size].reshape(old.shape)
-        if index == 3:
-            piece = piece[back_narrow][:, back_wide]
-        if index == 4:
-            piece = piece[back_wide][:, back_narrow]
-        if index < 7:
-            news.append(
-                old.astype(jnp.float32) * (1.0 - learn_rate * weight_decay) - learn_rate * piece
-            )
+        if index in whole:
+            news.append(whole[index])
         else:
-            news.append(old - learn_rate * piece)
+            source, which = small[index]
+            start = FLAT_AT[index] - KEPT[which][0] * LANES
+            piece = source.reshape(-1)[start : start + old.size].reshape(old.shape)
+            news.append(moved(old, piece) if index < 7 else old - learn_rate * piece)
     return tuple(news) + (
         first.reshape(-1),
         second.reshape(-1),

time: 830 us -> 579 us (0.70)
  Pallas kernels: 175 us -> 498 us
  local copies, waits for them, and re-layouts: 364 us -> 54.8 us
  other arithmetic: 131 us -> 6.78 us
  matrix products: 117 us -> 4.25 us
  starting transfers between devices: 14.3 us -> 0 us
  waiting for transfers between devices: 10.7 us -> 0 us
    pallas_call x0 -> x10, Pallas kernels: none -> 310 us  [the longest x2 90.2 us: turn_back(): pl.pallas_call(functools.partial(turn_kernel, prepare), out_shape=jax.Sha...]
    gather x6 -> x0, local copies, waits for them, and re-layouts: 92 us -> none  [the longest x3 46.1 us: on_device(): piece = piece[back_narrow][:, back_wide]]
    reshape x13 -> x4, local copies, waits for them, and re-layouts: 81.3 us -> 5.53 us  [the longest x1 4.2 us: on_device(): d_up = d_up[:, :C1, :C0].transpose(1, 0, 2).reshape(C1, 4 * C0)]
    dot_general x8 -> x1, matrix products: 64.6 us -> 2.14 us  [product(): return jnp.dot(left, right, preferred_element_type=jnp.float32)]
    dot_general x11 -> x1, matrix products: 52.3 us -> 2.11 us  [on_device(): jnp.einsum('nk,kj->jn', normed[:, :C1], narrow_turn, preferred_element_ty...]
    unnamed x407 -> x81, local copies, waits for them, and re-layouts: 56.1 us -> 12.6 us
    reduce_sum x10 -> x1, other arithmetic: 42 us -> 1.28 us  [on_device(): loss_local = jnp.sum(sums[0, :CIP])]
    reshape x4, local copies, waits for them, and re-layouts: 33.9 us -> 1.98 us  [as_rows(): return jnp.pad(flat, (0, rows * LANES - flat.shape[0])).reshape(rows, LANES)]
  transfers between devices with their start and end apart: 12 -> 0, of which waited for: 3 -> 0; matrix products, arithmetic and copies ran while one was open for 12% -> 0% of each run, Pallas kernels for 0% -> 0%
where the time goes in v2:
time: 579 us; the launch traced here: 572 us
  Pallas kernels  498 us (86%)
  local copies, waits for them, and re-layouts  54.8 us (9%)
  between operations  7.38 us (1%)
  other arithmetic  6.78 us (1%)
    pallas_call x1, Pallas kernels, exchange(): pl.pallas_call(functools.partial(exchange_kernel, plan), out_shape=(jax.S...  188 us
    pallas_call x2, Pallas kernels, turn_back(): pl.pallas_call(functools.partial(turn_kernel, prepare), out_shape=jax.Sha...  90.2 us
    pallas_call x1, Pallas kernels, place_gradients(): pl.pallas_call(place_kernel, out_shape=jax.ShapeDtypeStruct((space, LANES...  60.3 us
    pallas_call x3, Pallas kernels, halo(): pl.pallas_call(functools.partial(halo_kernel, nr, nc, width), out_shape=j...  55.7 us
    pallas_call x1, Pallas kernels, middle_part(): pl.pallas_call(middle_kernel, out_shape=(jax.ShapeDtypeStruct((cells, C1P...  39.9 us
    pallas_call x1, Pallas kernels, unpack(): pl.pallas_call(functools.partial(unpack_kernel, plan), out_shape=tuple((j...  30.9 us
    pallas_call x1, Pallas kernels, outer_part(): pl.pallas_call(outer_kernel, out_shape=(jax.ShapeDtypeStruct((C1P // LANE...  27.7 us
    unnamed x81, local copies, waits for them, and re-layouts  12.6 us

profile of v2, /device:TPU:0, one launch (start us, length us, event | category | flops | bytes accessed | tf_op | source)
XLA Modules:
  0.0 571.6 jit_solution(10111500057498058032)
XLA Ops:
  0.7 1.3 fusion.32
  5.9 1.9 constant_dynamic-slice_fusion.1
  8.4 10.0 %shard_map.264.state = bf16[2,10,160,128]{3,2,1,0:T(8,128)(2,1)S(1)} custom-call(bf16[2,8,128,128]{3,2,1,0:T(8,128)(2,1)S(1)} %fusion.16.cells), custom_call_target="tpu_custom_call" | custom-call | tf_op jit(solution)/shard_map/pallas_call | solution.py:979
  18.4 0.7 fusion.30
  19.7 1.4 fusion.29
  21.2 5.1 shard_map.265
  26.2 1.3 copy-done.6
  27.5 22.2 %shard_map.266.padded = bf16[2,10,96,896]{3,2,1,0:T(8,128)(2,1)S(1)} custom-call(bf16[2,4,64,896]{3,2,1,0:T(8,128)(2,1)S(1)} %get-tuple-element.67.cells), custom_call_target="tpu_custom_call" | custom-call | tf_op jit(solution)/shard_map/pallas_call | solution.py:979
  49.8 1.7 copy-done
  52.2 0.9 copy.43
  53.1 0.6 pad.96.b_dw
  53.7 0.6 pad.97.gain
  54.3 0.6 pad.98.shift
  54.9 0.6 pad.99.b_out
  55.5 0.6 fusion.28
  56.5 1.3 broadcast_in_dim.109.weight
  57.9 0.7 bitcast_bitcast_fusion.w_dw
  58.7 0.7 pad.95.w_head
  59.3 0.5 pad.100.b_up
  59.9 1.4 copy.46
  61.3 0.8 copy.47
  62.1 1.5 pad.94.w_up
  63.6 0.6 broadcast_in_dim.113.b_hidden
  64.3 0.5 pad.101.b_head
  64.8 39.9 %shard_map.267 = (bf16[512,896]{1,0:T(8,128)(2,1)}, bf16[512,3200]{1,0:T(8,128)(2,1)}, bf16[512,3200]{1,0:T(8,128)(2,1)}, f32[512,896]{1,0:T(8,128)}, bf16[512,8...) custom-call(bf16[2,10,96,896]{3,2,1,0:T(8,128)(2,1)} %copy-done, ...), custom_call_target="tpu_custom_call" | custom-call | tf_op jit(solution)/shard_map/pallas_call | solution.py:1194
  104.7 1.2 copy-done.4
  105.8 23.5 %shard_map.268.grad_padded = bf16[2,10,96,896]{3,2,1,0:T(8,128)(2,1)S(1)} custom-call(bf16[2,4,64,896]{3,2,1,0:T(8,128)(2,1)S(1)} %copy-done.4), custom_call_target="tpu_custom_call" | custom-call | tf_op jit(solution)/shard_map/pallas_call | solution.py:979
  129.4 1.8 copy-done.2
  131.2 27.7 %shard_map.269 = (f32[7,56,128]{2,1,0:T(8,128)}, f32[4,256,896]{2,1,0:T(8,128)}, f32[1152,256]{1,0:T(8,128)}, f32[8,896]{1,0:T(8,128)}) custom-call(bf16[2,10,96,896]{3,2,1,0:T(8,128)(2,1)} %copy-done, bf16[2,10,96,896]{3,2,1,0:T(8,128)(2,1)} %copy-done.2, bf16[2,4,64,896]{3,2,1,0:T(8,128)(2,1)} %get-tuple-element.75.cells.grad_conv, ...), custom_call_target="tpu_custom_call" | custom-call | tf_op jit(solution)/shard_map/pallas_call | solution.py:1270
  159.0 0.8 slice_reduce_fusion.5
  159.7 0.7 slice.151
  160.4 0.9 slice_reduce_fusion.1
  161.4 0.9 slice_reduce_fusion
  162.3 0.7 slice.158
  163.0 0.7 slice_bitcast_fusion.2
  163.8 0.6 pad_bitcast_fusion.4.piece_vec
  164.4 3.7 slice.146
  168.1 0.6 reshape_reshape.3
  168.8 0.8 pad.105.piece_in
  169.9 0.7 pad_bitcast_fusion.2.piece_dw
  170.6 2.1 slice_bitcast_fusion
  172.7 2.4 copy.49
  175.1 4.2 copy.51.up
  179.4 0.5 iota_compare_fusion
  179.9 2.1 fusion.2.branch
  182.0 2.1 fusion.7.norm_t
  184.4 0.6 pad_bitcast_fusion.3.piece_head
  185.0 0.6 broadcast_in_dim.117.wide
  185.6 60.3 %shard_map.270.grad = f32[51632,128]{1,0:T(8,128)} custom-call(bf16[800,512]{1,0:T(8,128)(2,1)} %fusion.7.norm_t, bf16[512,896]{1,0:T(8,128)(2,1)} %fusion.2.branch, bf16[512,3200]{1,0:T(8,128)(2,1)} %get-tuple-element.72.pre, bf16[512,3200]{1,0:T(8,128)(2,1)} %get-tuple-element.73.act, s32[1,3200]{1,0:T(1,128)} %broadcast_in_dim.117.wide, ...), custom_call_target="tpu_custom_call" | custom-call | tf_op jit(solution)/shard_map/pallas_call | solution.py:856
  246.0 1.3 slice_reduce_fusion.6
  247.2 1.3 compare_select_fusion.1
  248.5 0.7 broadcast_select_fusion.extra
  249.2 188.4 %shard_map.271 = (bf16[32,1616,128]{2,1,0:T(8,128)(2,1)}, f32[1612,128]{1,0:T(8,128)}, f32[1612,128]{1,0:T(8,128)}, f32[16,128]{1,0:T(8,128)}) custom-call(f32[51632,128]{1,0:T(8,128)} %shard_map.270.grad, f32[1612,128]{1,0:T(8,128)} %bitcast.76, f32[1612,128]{1,0:T(8,128)} %bitcast.77, f32[8,128]{1,0:T(8,128)} %broadcast_select_fusion.extra), custom_call_target="tpu_custom_call" | custom-call | tf_op jit(solution)/shard_map/pallas_call | solution.py:532
  437.6 30.9 %shard_map.272 = (bf16[800,3328]{1,0:T(8,128)(2,1)}, bf16[800,3328]{1,0:T(8,128)(2,1)}, f32[800,800]{1,0:T(8,128)}, f32[800,800]{1,0:T(8,128)}, f32[1096,128]{1,...) custom-call(bf16[32,1616,128]{2,1,0:T(8,128)(2,1)} %get-tuple-element.86.gathered, bf16[800,800]{1,0:T(8,128)(2,1)} %old_up.1, ...), custom_call_target="tpu_custom_call" | custom-call | tf_op jit(solution)/shard_map/pallas_call | solution.py:634
  470.1 44.7 %shard_map.274 = f32[800,3200]{1,0:T(8,128)} custom-call(bf16[800,3328]{1,0:T(8,128)(2,1)} %get-tuple-element.91.packed, s32[4,3328]{1,0:T(4,128)S(1)} %pad_add_fusion.narrow, s32[3200,128]{1,0:T(8,128)S(1)} %broadcast_in_dim.128.wide, bf16[800,3200]{1,0:T(8,128)(2,1)} %bitcast.63), custom_call_target="tpu_custom_call" | custom-call | tf_op jit(solution)/shard_map/pallas_call | solution.py:714
  515.4 45.6 %shard_map.273 = f32[800,3200]{1,0:T(8,128)} custom-call(bf16[800,3328]{1,0:T(8,128)(2,1)} %get-tuple-element.90.packed, s32[1,800]{1,0:T(1,128)S(1)} %broadcast_in_dim.124.narrow, s32[3328,128]{1,0:T(8,128)S(1)} %broadcast_in_dim.125.wide, bf16[800,3200]{1,0:T(8,128)(2,1)} %old.1), custom_call_target="tpu_custom_call" | custom-call | tf_op jit(solution)/shard_map/pallas_call | solution.py:714
  561.2 1.0 mul.59
  562.4 1.1 copy.54
  563.7 0.7 multiply_subtract_fusion.1
  564.7 0.7 copy.55
  565.5 0.7 fusion.18
  566.2 1.3 fusion.31
  568.1 0.9 copy.67
  569.1 0.9 copy.68
  (122 shorter events, 6.2 us)
Async XLA Ops:
  0.6 17.8 %copy-start.21 = (f32[7677]{0:T(1024)S(1)}, f32[7677]{0:T(1024)}, u32[]{:S(2)}) copy-start(f32[7677]{0:T(1024)} %param.35) | copy-start | bytes 92128
  8.2 10.9 %copy-start.7 = (bf16[800,800]{1,0:T(8,128)(2,1)S(1)}, bf16[800,800]{1,0:T(8,128)(2,1)}, u32[]{:S(2)}) copy-start(bf16[800,800]{1,0:T(8,128)(2,1)} %old_down.1) | copy-start | bytes 3840004
  8.2 11.1 %copy-start.18 = (bf16[693,200]{0,1:T(8,128)(2,1)S(1)}, bf16[693,200]{0,1:T(8,128)(2,1)}, u32[]{:S(2)}) copy-start(bf16[693,200]{0,1:T(8,128)(2,1)} %param.28) | copy-start | bytes 831604
  19.3 30.4 %copy-start.1 = (bf16[4,256,896]{2,1,0:T(8,128)(2,1)}, bf16[4,256,896]{2,1,0:T(8,128)(2,1)S(1)}, u32[]{:S(2)}) copy-start(bf16[4,256,896]{2,1,0:T(8,128)(2,1)S(1)} %pad.90.w_down) | copy-start | bytes 5505028
  19.5 30.3 %copy-start.9 = (bf16[693,200]{1,0:T(8,128)(2,1)}, bf16[693,200]{1,0:T(8,128)(2,1)S(1)}, u32[]{:S(2)}) copy-start(bf16[693,200]{1,0:T(8,128)(2,1)S(1)} %copy.37) | copy-start | bytes 831604
  26.2 1.3 copy-start.6
  27.5 24.0 %copy-start.3 = (f32[4,512,256]{2,1,0:T(8,128)}, f32[4,512,256]{2,1,0:T(8,128)S(1)}, u32[]{:S(2)}) copy-start(f32[4,512,256]{2,1,0:T(8,128)S(1)} %get-tuple-element.69.h_zero) | copy-start | bytes 6291460
  27.5 24.0 %copy-start.5 = (f32[4,512,256]{2,1,0:T(8,128)}, f32[4,512,256]{2,1,0:T(8,128)S(1)}, u32[]{:S(2)}) copy-start(f32[4,512,256]{2,1,0:T(8,128)S(1)} %get-tuple-element.78.a_zero) | copy-start | bytes 6291460
  27.5 24.0 %copy-start.13 = (bf16[1,8,128,77]{2,1,3,0:T(8,128)(2,1)S(1)}, bf16[1,8,128,77]{2,1,3,0:T(8,128)(2,1)}, u32[]{:S(2)}) copy-start(bf16[1,8,128,77]{2,1,3,0:T(8,128)(2,1)} %get-tuple-element.116) | copy-start | bytes 473092
  27.5 25.6 %copy-start.28 = (f32[800]{0:T(1024)S(1)}, f32[800]{0:T(1024)}, u32[]{:S(2)}) copy-start(f32[800]{0:T(1024)} %get-tuple-element.125) | copy-start | bytes 9604
  27.5 28.0 %copy-start.29 = (f32[8,128]{1,0:T(8,128)S(1)}, f32[8,128]{1,0:T(8,128)}, u32[]{:S(2)}) copy-start(f32[8,128]{1,0:T(8,128)} %param.24) | copy-start | bytes 12292
  27.5 28.0 %copy-start.30 = (s32[8,128]{1,0:T(8,128)S(1)}, s32[8,128]{1,0:T(8,128)}, u32[]{:S(2)}) copy-start(s32[8,128]{1,0:T(8,128)} %param.23) | copy-start | bytes 12292
  49.8 1.8 copy-start
  51.5 6.3 %copy-start.16 = (bf16[49,800]{1,0:T(8,128)(2,1)S(1)}, bf16[49,800]{1,0:T(8,128)(2,1)}, u32[]{:S(2)}) copy-start(bf16[49,800]{1,0:T(8,128)(2,1)} %param.30) | copy-start | bytes 235204
  51.5 7.0 %copy-start.26 = (bf16[200,77]{0,1:T(8,128)(2,1)S(1)}, bf16[200,77]{0,1:T(8,128)(2,1)}, u32[]{:S(2)}) copy-start(bf16[200,77]{0,1:T(8,128)(2,1)} %param.34) | copy-start | bytes 92404
  51.5 7.8 %copy-start.31 = (f32[200]{0:T(256)S(1)}, f32[200]{0:T(256)}, u32[]{:S(2)}) copy-start(f32[200]{0:T(256)} %get-tuple-element.120) | copy-start | bytes 2404
  51.5 8.3 %copy-start.8 = (bf16[800,800]{1,0:T(8,128)(2,1)S(1)}, bf16[800,800]{1,0:T(8,128)(2,1)}, u32[]{:S(2)}) copy-start(bf16[800,800]{1,0:T(8,128)(2,1)} %old_up.1) | copy-start | bytes 3840004
  61.3 2.3 copy-start.22
  104.7 1.2 copy-start.4
  129.4 1.8 copy-start.2
  164.4 3.7 copy-start.15
  168.1 1.6 copy-start.19
  175.1 4.2 copy-start.27
  175.1 4.7 copy-start.33
  179.3 2.7 copy-start.32
  182.0 2.1 copy-start.25
  182.0 3.0 copy-start.23
  515.3 45.6 %copy-start.14 = (f32[1096,128]{1,0:T(8,128)S(1)}, f32[1096,128]{1,0:T(8,128)}, u32[]{:S(2)}) copy-start(f32[1096,128]{1,0:T(8,128)} %get-tuple-element.87) | copy-start | bytes 1683460
  515.4 46.9 %copy-start.10 = (bf16[693,200]{1,0:T(8,128)(2,1)S(1)}, bf16[693,200]{1,0:T(8,128)(2,1)}, u32[]{:S(2)}) copy-start(bf16[693,200]{1,0:T(8,128)(2,1)} %copy-done.9) | copy-start | bytes 831604
  560.9 2.5 copy-start.20
  561.0 2.8 copy-start.17
  561.2 3.2 copy-start.24
  562.2 5.9 %copy-start.12 = (f32[1612,128]{1,0:T(8,128)S(1)}, f32[1612,128]{1,0:T(8,128)}, u32[]{:S(2)}) copy-start(f32[1612,128]{1,0:T(8,128)} %get-tuple-element.94) | copy-start | bytes 2476036
  562.4 6.7 %copy-start.11 = (f32[1612,128]{1,0:T(8,128)S(1)}, f32[1612,128]{1,0:T(8,128)}, u32[]{:S(2)}) copy-start(f32[1612,128]{1,0:T(8,128)} %get-tuple-element.95) | copy-start | bytes 2476036

commit v3 on v2

--- a/solution.py
+++ b/solution.py
@@ -134,13 +134,13 @@
             grad.at[pl.ds(window_start(flipped(mask), col), window)], acc.at[index], sem_load.at[index]
         )
 
-    for mask in masks:
-        def begin(col, carry, mask=mask):
-            near_copy(mask, col).start()
-            load_copy(mask, col).start()
-            return carry
-
-        lax.fori_loop(0, nc, begin, 0)
+    def begin(d, carry):
+        for mask in masks:
+            near_copy(mask, lax.rem(c + d, nc)).start()
+            load_copy(mask, lax.rem(c + d, nc)).start()
+        return carry
+
+    lax.fori_loop(1, nc + 1, begin, 0)
 
     def encode(index, p, q_ref, s_ref):
         def body(b, carry):
@@ -199,13 +199,21 @@
             found = [m for m in found if rest[0] in m] + [m for m in found if rest[0] not in m]
         return found
 
-    for mask in masks:
-        def join(col, carry, mask=mask):
+    def far_copy(p, d):
+        col = lax.rem(c + d, nc)
+        return (
+            remote(z_send.at[p, d - 1], z_recv.at[p, d - 1], sem_zs.at[p, d - 1], sem_zr.at[p, d - 1], r, col),
+            remote(zs_send.at[p, d - 1], zs_recv.at[p, d - 1], sem_zss.at[p, d - 1], sem_zsr.at[p, d - 1], r, col),
+        )
+
+    def join(d):
+        col = lax.rem(c + d, nc)
+        for mask in masks:
             index = local_index(mask, col)
             near_copy(mask, col).wait_recv()
             load_copy(mask, col).wait()
 
-            def body(b, inner):
+            def body(b, inner, index=index):
                 at = pl.ds(pl.multiple_of(b * plan.block, plan.block), plan.block)
                 acc[index, at, :] += near[index, at, :]
                 return inner
@@ -218,47 +226,42 @@
                     options = free_masks(p, 0)
                     number = [sorted(o) for o in options].index(sorted(rest))
                     send_stage(p, 0, number, rest, col)
-            return carry
-
-        lax.fori_loop(0, nc, join, 0)
-
-    def far_copy(p, d):
+
+    def take(stage, d):
         col = lax.rem(c + d, nc)
-        return (
-            remote(z_send.at[p, d - 1], z_recv.at[p, d - 1], sem_zs.at[p, d - 1], sem_zr.at[p, d - 1], r, col),
-            remote(zs_send.at[p, d - 1], zs_recv.at[p, d - 1], sem_zss.at[p, d - 1], sem_zsr.at[p, d - 1], r, col),
-        )
-
-    for stage in range(plan.stages):
         for number in range(1 << (plan.stages - 1 - stage)):
-            def take(d, carry, stage=stage, number=number):
-                col = lax.rem(c + d, nc)
-                for p in range(2):
-                    mask = free_masks(p, stage)[number]
-                    take_stage(p, stage, number, mask, col)
-                    if stage + 1 < plan.stages:
-                        bit = plan.orders[p][stage + 1]
-                        if bit in mask:
-                            rest = tuple(b for b in mask if b != bit)
-                            options = free_masks(p, stage + 1)
-                            following = [sorted(o) for o in options].index(sorted(rest))
-                            send_stage(p, stage + 1, following, rest, col)
-                return carry
-
-            if stage + 1 < plan.stages:
-                lax.fori_loop(1, nc + 1, take, 0)
-            else:
-                def take_last(d, carry, take=take):
-                    take(d, 0)
-                    col = lax.rem(c + d, nc)
-                    for p in range(2):
+            for p in range(2):
+                mask = free_masks(p, stage)[number]
+                take_stage(p, stage, number, mask, col)
+                if stage + 1 < plan.stages:
+                    bit = plan.orders[p][stage + 1]
+                    if bit in mask:
+                        rest = tuple(b for b in mask if b != bit)
+                        options = free_masks(p, stage + 1)
+                        following = [sorted(o) for o in options].index(sorted(rest))
+                        send_stage(p, stage + 1, following, rest, col)
+                else:
+                    @pl.when(d < nc)
+                    def _(p=p):
                         encode(local_index((), col), p, z_send.at[p, d - 1], zs_send.at[p, d - 1])
                         for copy in far_copy(p, d):
                             copy.start()
-                    return carry
-
-                lax.fori_loop(1, nc, take_last, 0)
-                take(nc, 0)
+
+    def turn_of(t, carry):
+        @pl.when(t <= nc)
+        def _():
+            join(t)
+
+        for stage in range(plan.stages):
+            d = t - 1 - stage
+
+            @pl.when((d >= 1) & (d <= nc))
+            def _(stage=stage, d=d):
+                take(stage, d)
+
+        return carry
+
+    lax.fori_loop(1, nc + plan.stages + 1, turn_of, 0)
 
     mine = local_index((), c)
 
@@ -667,7 +670,10 @@
 TILE = 640
 
 
-def turn_kernel(prepare, packed, narrow, wide, old, new, lines, hot):
+DEEP = 256
+
+
+def turn_kernel(prepare, packed, narrow, wide, old, new, lines):
     depth = lines.shape[1]
 
     @pl.when(pl.program_id(0) == 0)
@@ -675,15 +681,15 @@
         prepare(packed, narrow, lines)
 
     base = pl.program_id(0) * TILE
-
-    def build(b, carry):
-        at = pl.ds(pl.multiple_of(b * LANES, LANES), LANES)
-        column = lax.broadcasted_iota(jnp.int32, (LANES, TILE), 1) + base
-        hot[at, :] = one_hot(column == wide[at, 0:1])
-        return carry
-
-    lax.fori_loop(0, depth // LANES, build, 0)
-    new[...] = moved(old[...], product(lines[...], hot[...]))
+    direction = None
+    for begin in range(0, depth, DEEP):
+        end = min(begin + DEEP, depth)
+        place = wide[begin:end, :] - base
+        lane = lax.broadcasted_iota(jnp.int32, (end - begin, LANES), 1)
+        hot = jnp.concatenate([one_hot(lane + u == place) for u in range(0, TILE, LANES)], axis=1)
+        term = product(lines[:, begin:end], hot)
+        direction = term if direction is None else direction + term
+    new[...] = moved(old[...], direction)
 
 
 def prepare_hidden(packed, narrow, lines):
@@ -722,7 +728,7 @@
             pl.BlockSpec((C1, TILE), lambda i: (0, i)),
         ],
         out_specs=pl.BlockSpec((C1, TILE), lambda i: (0, i)),
-        scratch_shapes=[pltpu.VMEM((C1, depth), jnp.bfloat16), pltpu.VMEM((depth, TILE), jnp.bfloat16)],
+        scratch_shapes=[pltpu.VMEM((C1, depth), jnp.bfloat16)],
         compiler_params=pltpu.CompilerParams(vmem_limit_bytes=48 << 20),
     )(packed, narrow, jnp.broadcast_to(wide[:, None], (depth, LANES)), old)
 
@@ -766,8 +772,9 @@
 
 
 def place_kernel(
-    norm_t, branch, pre, act, wide, up, down, piece_in, piece_dw, piece_head, piece_vec,
-    grad, hot, hidden, out, loose, up_rows, down_rows, sem_out, sems,
+    nr, nc, normed, branch, pre, act, narrow_row, narrow_col, wide, up, cells,
+    grad, padded, hidden, out, loose, up_rows, norm_t, branch_r, halo_cells,
+    sem_out, sems, sem_halo_s, sem_halo_r,
 ):
     step = pl.program_id(0)
     steps = pl.num_programs(0)
@@ -785,96 +792,142 @@
 
     copies = [
         pltpu.make_async_copy(ref, grad.at[pl.ds(row, ref.shape[0])], sems.at[i])
+        for i, (ref, row) in enumerate(((up_rows, ROW_AT[5]), (hidden, ROW_AT[3])))
+    ] + [pltpu.make_async_copy(halo_cells, padded, sems.at[2])]
+
+    @pl.when(step == 0)
+    def _():
+        halo_start(nr, nc, 3, cells, halo_cells, sem_halo_s, sem_halo_r)
+        line = lax.broadcasted_iota(jnp.int32, (C1, C1), 1)
+        norm_t[...] = product_t(one_hot(line == narrow_col[:, 0:1]), normed[:, :C1]).astype(jnp.bfloat16)
+        line = lax.broadcasted_iota(jnp.int32, (C1, C1P), 0)
+        branch_r[...] = product(branch[:, :C1], one_hot(line == narrow_row[...])).astype(jnp.bfloat16)
+        for u in range(-(-C1 // LANES)):
+            width = min(LANES, C1 - u * LANES)
+            loose[u, :, 0:width] = up[0:C1, u * LANES : u * LANES + width]
+
+        def put(t, value):
+            up_rows[pl.ds(t, C1 // 4, stride=ratio), :] = value
+
+        weave(loose, C1 // 4, put)
+        copies[0].start()
+
+    turned_pre = turned_act = None
+    for begin in range(0, CH, DEEP):
+        end = min(begin + DEEP, CH)
+        line = lax.broadcasted_iota(jnp.int32, (end - begin, TILE), 0) + begin
+        hot = one_hot(line == wide[...])
+        one = product(pre[:, begin:end], hot)
+        two = product(act[:, begin:end], hot)
+        turned_pre = one if turned_pre is None else turned_pre + one
+        turned_act = two if turned_act is None else turned_act + two
+    part = product(norm_t[...], turned_pre.astype(jnp.bfloat16))
+    for t in range(tiles):
+        hidden[pl.ds(step * tiles + t, C1, stride=ratio), :] = part[:, t * LANES : (t + 1) * LANES]
+    part = inner_rows(turned_act.astype(jnp.bfloat16), branch_r[...])
+    for u in range(-(-C1 // LANES)):
+        loose[u, 0:TILE, :] = part[:, u * LANES : (u + 1) * LANES]
+
+    def put_out(t, value):
+        out[pl.ds(step * (lines * ratio) + t, lines, stride=ratio), :] = value
+
+    weave(loose, lines, put_out)
+    out_copy(step).start()
+
+    @pl.when(step == steps - 1)
+    def _():
+        copies[1].start()
+        halo_finish(nr, nc, 3, cells, halo_cells, sem_halo_s, sem_halo_r)
+        copies[2].start()
+
+        def finish(n, carry):
+            out_copy(n).wait()
+            return carry
+
+        lax.fori_loop(0, steps, finish, 0)
+        for copy in copies:
+            copy.wait()
+
+
+def place_gradients(nr, nc, space, normed, branch, pre, act, narrow, wide, up, cells):
+    def whole(array):
+        return pl.BlockSpec(
+            array.shape, lambda i: (0,) * len(array.shape), pipeline_mode=pl.Buffered(1)
+        )
+
+    hbm = pl.BlockSpec(memory_space=pl.ANY)
+    rows = pre.shape[0]
+    batch, height, breadth, chans = cells.shape
+    narrow_row = jnp.pad(narrow, (0, C1P - C1), constant_values=-1)[None, :]
+    narrow_col = jnp.broadcast_to(narrow[:, None], (C1, LANES))
+    framed = jax.ShapeDtypeStruct((batch, height + 6, breadth + 2 * EDGE, chans), cells.dtype)
+    dma = pltpu.SemaphoreType.DMA
+    return pl.pallas_call(
+        functools.partial(place_kernel, nr, nc),
+        out_shape=(jax.ShapeDtypeStruct((space, LANES), jnp.float32), framed),
+        grid=(CH // TILE,),
+        in_specs=[
+            whole(normed), whole(branch), whole(pre), whole(act), whole(narrow_row), whole(narrow_col),
+            pl.BlockSpec((1, TILE), lambda i: (0, i)),
+            whole(up), whole(cells),
+        ],
+        out_specs=(hbm, hbm),
+        scratch_shapes=[
+            pltpu.VMEM((C1 * CH // LANES, LANES), jnp.float32),
+            pltpu.VMEM((C1 * CH // LANES, LANES), jnp.float32),
+            pltpu.VMEM((C1P // LANES, C1, LANES), jnp.float32),
+            pltpu.VMEM((C1 * C1 // LANES, LANES), jnp.float32),
+            pltpu.VMEM((C1, rows), jnp.bfloat16),
+            pltpu.VMEM((rows, C1P), jnp.bfloat16),
+            pltpu.VMEM(framed.shape, framed.dtype),
+            dma((CH // TILE,)), dma((3,)), dma((8,)), dma((8,)),
+        ],
+        compiler_params=pltpu.CompilerParams(
+            collective_id=3, has_side_effects=True, vmem_limit_bytes=60 << 20
+        ),
+    )(normed, branch, pre, act, narrow_row, narrow_col, wide[None, :], up, cells)
+
+
+def complete_kernel(before, down, piece_in, piece_dw, piece_head, piece_vec, grad, loose, down_rows, sems):
+    copies = [
+        pltpu.make_async_copy(ref, grad.at[pl.ds(row, ref.shape[0])], sems.at[i])
         for i, (ref, row) in enumerate(
             (
                 (piece_in, 0), (piece_dw, ROW_AT[2]), (piece_head, ROW_AT[6]), (piece_vec, ROW_AT[7]),
-                (up_rows, ROW_AT[5]), (down_rows, ROW_AT[1]), (hidden, ROW_AT[3]),
+                (down_rows, ROW_AT[1]),
             )
         )
     ]
-
-    @pl.when(step == 0)
-    def _():
-        for copy in copies[:4]:
-            copy.start()
-
-    for number, (source, target) in enumerate(((up, up_rows), (down, down_rows))):
-        @pl.when(step == number)
-        def _(number=number, source=source, target=target):
-            for u in range(-(-C1 // LANES)):
-                width = min(LANES, C1 - u * LANES)
-                loose[u, :, 0:width] = source[:, u * LANES : u * LANES + width]
-
-            def put(t, value):
-                target[pl.ds(t, C1 // 4, stride=ratio), :] = value
-
-            weave(loose, C1 // 4, put)
-            copies[4 + number].start()
-
-    def build(b, carry):
-        at = pl.ds(pl.multiple_of(b * LANES, LANES), LANES)
-        line = lax.broadcasted_iota(jnp.int32, (LANES, TILE), 0) + b * LANES
-        hot[at, :] = one_hot(line == wide[...])
-        return carry
-
-    lax.fori_loop(0, CH // LANES, build, 0)
-    turned_pre = product(pre[...], hot[...]).astype(jnp.bfloat16)
-    part = product(norm_t[...], turned_pre)
-    for t in range(tiles):
-        hidden[pl.ds(step * tiles + t, C1, stride=ratio), :] = part[:, t * LANES : (t + 1) * LANES]
-    turned_act = product(act[...], hot[...]).astype(jnp.bfloat16)
-    part = lax.dot_general(
-        turned_act, branch[...], (((0,), (0,)), ((), ())), preferred_element_type=jnp.float32
-    )
-    for u in range(-(-C1 // LANES)):
-        loose[u, 0:TILE, :] = part[:, u * LANES : (u + 1) * LANES]
-
-    def put_out(t, value):
-        out[pl.ds(step * (lines * ratio) + t, lines, stride=ratio), :] = value
-
-    weave(loose, lines, put_out)
-    out_copy(step).start()
-
-    @pl.when(step == steps - 1)
-    def _():
-        copies[6].start()
-
-        def finish(n, carry):
-            out_copy(n).wait()
-            return carry
-
-        lax.fori_loop(0, steps, finish, 0)
-        for copy in copies:
-            copy.wait()
-
-
-def place_gradients(space, norm_t, branch, pre, act, wide, up, down, pieces):
-    whole = lambda *shape: pl.BlockSpec(shape, lambda i: (0,) * len(shape))
+    for copy in copies[:4]:
+        copy.start()
+    for u in range(C1P // LANES):
+        loose[u] = down[:, u * LANES : (u + 1) * LANES]
+
+    def put(t, value):
+        down_rows[pl.ds(t, C1 // 4, stride=CH // LANES), :] = value
+
+    weave(loose, C1 // 4, put)
+    copies[4].start()
+    for copy in copies:
+        copy.wait()
+
+
+def complete_gradients(grad, down, pieces):
+    vmem = pl.BlockSpec(memory_space=pltpu.VMEM)
     hbm = pl.BlockSpec(memory_space=pl.ANY)
-    rows = pre.shape[0]
-    padded = -(-C1 // LANES) * LANES
     return pl.pallas_call(
-        place_kernel,
-        out_shape=jax.ShapeDtypeStruct((space, LANES), jnp.float32),
-        grid=(CH // TILE,),
-        in_specs=[
-            whole(C1, rows), whole(rows, padded), whole(rows, CH), whole(rows, CH),
-            pl.BlockSpec((1, TILE), lambda i: (0, i)),
-            whole(C1, C1), whole(C1, C1), hbm, hbm, hbm, hbm,
+        complete_kernel,
+        out_shape=jax.ShapeDtypeStruct(grad.shape, grad.dtype),
+        in_specs=[hbm, vmem, vmem, vmem, vmem, vmem],
+        out_specs=hbm,
+        input_output_aliases={0: 0},
+        scratch_shapes=[
+            pltpu.VMEM((C1P // LANES, C1, LANES), jnp.float32),
+            pltpu.VMEM((C1 * C1 // LANES, LANES), jnp.float32),
+            pltpu.SemaphoreType.DMA((5,)),
         ],
-        out_specs=hbm,
-        scratch_shapes=[
-            pltpu.VMEM((CH, TILE), jnp.bfloat16),
-            pltpu.VMEM((C1 * CH // LANES, LANES), jnp.float32),
-            pltpu.VMEM((C1 * CH // LANES, LANES), jnp.float32),
-            pltpu.VMEM((padded // LANES, C1, LANES), jnp.float32),
-            pltpu.VMEM((C1 * C1 // LANES, LANES), jnp.float32),
-            pltpu.VMEM((C1 * C1 // LANES, LANES), jnp.float32),
-            pltpu.SemaphoreType.DMA((CH // TILE,)),
-            pltpu.SemaphoreType.DMA((7,)),
-        ],
-        compiler_params=pltpu.CompilerParams(vmem_limit_bytes=58 << 20),
-    )(norm_t, branch, pre, act, wide[None, :], up, down, *pieces)
+        compiler_params=pltpu.CompilerParams(vmem_limit_bytes=60 << 20),
+    )(grad, down, *pieces)
 
 
 C0P = 256
@@ -902,17 +955,39 @@
     return 0.5 * (1.0 + bend) + 0.5 * t * (1.0 - bend * bend) * (CURVE * (1.0 + 3.0 * CUBE * (t * t)))
 
 
-def halo_kernel(nr, nc, width, cells, out, sem_s, sem_r):
+WAYS = [(dr, dc) for dr in (-1, 0, 1) for dc in (-1, 0, 1) if (dr, dc) != (0, 0)]
+ORDER = sorted(range(8), key=lambda i: (WAYS[i][1] != 0, WAYS[i][0] == 0))
+
+
+def halo_place(nr, nc):
     r = lax.axis_index("rows")
-    c = lax.axis_index("cols")
+    return r, lax.axis_index("cols"), lambda dr: (r + dr >= 0) & (r + dr < nr)
+
+
+def halo_copy(nr, nc, width, cells, out, sem_s, sem_r, i, receive):
+    r, c, there = halo_place(nr, nc)
     height, breadth = cells.shape[1], cells.shape[2]
-    ways = [(dr, dc) for dr in (-1, 0, 1) for dc in (-1, 0, 1) if (dr, dc) != (0, 0)]
-
-    def there(dr):
-        return (r + dr >= 0) & (r + dr < nr)
-
+    dr, dc = WAYS[i]
+    rows_from = {-1: (0, width), 0: (0, height), 1: (height - width, width)}[dr]
+    rows_to = {-1: height + width, 0: width, 1: 0}[dr]
+    cols_from = {-1: (0, EDGE), 0: (0, breadth), 1: (breadth - EDGE, EDGE)}[dc]
+    cols_to = {-1: EDGE + breadth, 0: EDGE, 1: 0}[dc]
+    sign = -1 if receive else 1
+    return pltpu.make_async_remote_copy(
+        src_ref=cells.at[:, pl.ds(*rows_from), pl.ds(*cols_from)],
+        dst_ref=out.at[:, pl.ds(rows_to, rows_from[1]), pl.ds(cols_to, cols_from[1])],
+        send_sem=sem_s.at[i],
+        recv_sem=sem_r.at[i],
+        device_id=(r + sign * dr, lax.rem(c + sign * dc + nc, nc)),
+        device_id_type=MESH,
+    )
+
+
+def halo_start(nr, nc, width, cells, out, sem_s, sem_r):
+    r, c, there = halo_place(nr, nc)
+    height, breadth = cells.shape[1], cells.shape[2]
     barrier = pltpu.get_barrier_semaphore()
-    for dr, dc in ways:
+    for dr, dc in WAYS:
         @pl.when(there(dr))
         def _(dr=dr, dc=dc):
             pl.semaphore_signal(
@@ -929,27 +1004,10 @@
     def _():
         pl.semaphore_wait(barrier, 8)
 
-    def copy(i, receive):
-        dr, dc = ways[i]
-        rows_from = {-1: (0, width), 0: (0, height), 1: (height - width, width)}[dr]
-        rows_to = {-1: height + width, 0: width, 1: 0}[dr]
-        cols_from = {-1: (0, EDGE), 0: (0, breadth), 1: (breadth - EDGE, EDGE)}[dc]
-        cols_to = {-1: EDGE + breadth, 0: EDGE, 1: 0}[dc]
-        sign = -1 if receive else 1
-        return pltpu.make_async_remote_copy(
-            src_ref=cells.at[:, pl.ds(*rows_from), pl.ds(*cols_from)],
-            dst_ref=out.at[:, pl.ds(rows_to, rows_from[1]), pl.ds(cols_to, cols_from[1])],
-            send_sem=sem_s.at[i],
-            recv_sem=sem_r.at[i],
-            device_id=(r + sign * dr, lax.rem(c + sign * dc + nc, nc)),
-            device_id_type=MESH,
-        )
-
-    order = sorted(range(8), key=lambda i: (ways[i][1] != 0, ways[i][0] == 0))
-    for i in order:
-        @pl.when(there(ways[i][0]))
+    for i in ORDER:
+        @pl.when(there(WAYS[i][0]))
         def _(i=i):
-            copy(i, False).start()
+            halo_copy(nr, nc, width, cells, out, sem_s, sem_r, i, False).start()
 
     for m in range(cells.shape[0]):
         for row in range(height):
@@ -963,14 +1021,22 @@
     def _():
         out[:, height + width :] = jnp.zeros((out.shape[0], width) + out.shape[2:], out.dtype)
 
-    for i in order:
-        @pl.when(there(-ways[i][0]))
+
+def halo_finish(nr, nc, width, cells, out, sem_s, sem_r):
+    r, c, there = halo_place(nr, nc)
+    for i in ORDER:
+        @pl.when(there(-WAYS[i][0]))
         def _(i=i):
-            copy(i, True).wait_recv()
-
-        @pl.when(there(ways[i][0]))
+            halo_copy(nr, nc, width, cells, out, sem_s, sem_r, i, True).wait_recv()
+
+        @pl.when(there(WAYS[i][0]))
         def _(i=i):
-            copy(i, False).wait_send()
+            halo_copy(nr, nc, width, cells, out, sem_s, sem_r, i, False).wait_send()
+
+
+def halo_kernel(nr, nc, width, cells, out, sem_s, sem_r):
+    halo_start(nr, nc, width, cells, out, sem_s, sem_r)
+    halo_finish(nr, nc, width, cells, out, sem_s, sem_r)
 
 
 def halo(nr, nc, width, cells, identity):
@@ -1109,6 +1175,7 @@
             conv, total,
         ),
         pltpu.VMEM((cells, CH), jnp.float32),
+        pltpu.VMEM((cells, C1), jnp.bfloat16),
     )
 
 
@@ -1116,7 +1183,7 @@
     coarse, h_zero, target, weight, w_hidden, w_out_t, w_up, w_head,
     b_dw, gain, shift, b_hidden, b_out, b_up, b_head,
     normed, act, grad_pre, grad_mixed, grad_branch, grad_summed, grad_conv, d_up, d_head, sums,
-    conv, total, pre,
+    conv, total, pre, spread_all,
 ):
     inside = lax.broadcasted_iota(jnp.int32, (1, C1P), 1) < C1
     values = conv[...] + b_dw[...]
@@ -1155,8 +1222,9 @@
         grad_summed[s] = spread
         grad_upper = spread.astype(jnp.bfloat16)
         up_sum = up_sum + column_sum(grad_upper)
-        d_up[s] = inner_rows(mixed, grad_upper)
+        spread_all[:, s * C0 : (s + 1) * C0] = grad_upper[:, :C0]
         grad_mixed[:, :C1] += product_t(grad_upper, w_up[s])
+    d_up[...] = inner_rows(mixed, spread_all[...])
     grad_branch[...] = grad_mixed[...].astype(jnp.bfloat16)
     sums[...] = jnp.zeros_like(sums)
     sums[0:1, 0:CIP] = loss
@@ -1201,7 +1269,7 @@
             jax.ShapeDtypeStruct((cells, C1P), low),
             jax.ShapeDtypeStruct((4, cells, C0P), f32),
             jax.ShapeDtypeStruct((batch, half_h, half_w, C1P), low),
-            jax.ShapeDtypeStruct((4, C1P, C0P), f32),
+            jax.ShapeDtypeStruct((C1P, C1), f32),
             jax.ShapeDtypeStruct((C0P, CIP), f32),
             jax.ShapeDtypeStruct((8, CH), f32),
         ),
@@ -1251,7 +1319,7 @@
     sums[0:1, 0:C1P] = column_sum(grad_coarse)
     in_sum = jnp.zeros((1, C0P), jnp.float32)
     for s in range(4):
-        d_down[s] = inner_rows(h_zero[s].astype(jnp.bfloat16), grad_coarse)
+        d_down[s * C0 : (s + 1) * C0, :] = inner_rows(h_zero[s].astype(jnp.bfloat16), grad_coarse)[:C0]
         grad_h = product_t(grad_coarse, w_down[s]) + grad_summed[s]
         grad_a = (gelu_slope(a_zero[s]) * grad_h).astype(jnp.bfloat16)
         in_sum = in_sum + column_sum(grad_a)
@@ -1271,7 +1339,7 @@
         outer_kernel,
         out_shape=(
             jax.ShapeDtypeStruct((C1P // LANES, 56, LANES), f32),
-            jax.ShapeDtypeStruct((4, C0P, C1P), f32),
+            jax.ShapeDtypeStruct((C1, C1P), f32),
             jax.ShapeDtypeStruct((9 * CIP, C0P), f32),
             jax.ShapeDtypeStruct((8, C1P), f32),
         ),
@@ -1348,7 +1416,6 @@
     def line(vector, size):
         return widened(vector[None, :], 1, size)
 
-    narrow_turn = (jnp.arange(C1)[:, None] == perm_narrow[None, :]).astype(jnp.bfloat16)
     w_in_p = widened(w_in.reshape(9, CI, C0), 9, CIP, C0P).reshape(9 * CIP, C0P)
     w_down_p = widened(w_down.reshape(4, C0, C1), 4, C0P, C1P)
     w_up_p = widened(w_up.reshape(C1, 4, C0).transpose(1, 0, 2), 4, C1, C0P)
@@ -1369,12 +1436,13 @@
         widened(w_head, C0P, CIP), line(b_dw, C1P), line(gain, C1P), line(shift, C1P),
         line(b_hidden, CH), line(b_out, C1P), line(b_up, C0P), line(b_head, CIP),
     )
-    grad_padded = halo(rows, cols, 3, grad_conv, 3)
+    space = Plan(rows, cols, PADDED).space
+    grad, grad_padded = place_gradients(
+        rows, cols, space, normed, grad_branch, grad_pre, act, perm_narrow, perm_wide, d_up, grad_conv
+    )
     d_dw, d_down, d_in, sums_out = outer_part(
         padded, grad_padded, grad_conv, grad_mixed, grad_summed, a_zero, h_zero, taps, w_dw_p, w_down_p
     )
-    d_up = d_up[:, :C1, :C0].transpose(1, 0, 2).reshape(C1, 4 * C0)
-    d_down = d_down[:, :C0, :C1].reshape(4 * C0, C1)
     d_in = d_in.reshape(9, CIP, C0P)[:, :CI, :C0].reshape(9 * CI, C0)
     d_dw = d_dw[:, :49].transpose(1, 0, 2).reshape(49, C1P)[:, :C1]
     d_vector = jnp.concatenate(
@@ -1384,18 +1452,13 @@
         ]
     )
     loss_local = jnp.sum(sums[0, :CIP])
-    space = Plan(rows, cols, PADDED).space
-    norm_t = jnp.einsum(
-        "nk,kj->jn", normed[:, :C1], narrow_turn, preferred_element_type=jnp.float32
-    ).astype(jnp.bfloat16)
-    branch_r = product(grad_branch[:, :C1], widened(narrow_turn, C1, C1P)).astype(jnp.bfloat16)
     pieces = (
         jnp.pad(as_rows(d_in, ROW_AT[1] - ROW_AT[0]), ((ROW_AT[0], 0), (0, 0))),
         as_rows(d_dw, ROW_AT[3] - ROW_AT[2]),
         as_rows(d_head[:C0, :CI], ROW_AT[7] - ROW_AT[6]),
         as_rows(d_vector, space - ROW_AT[7]),
     )
-    grad = place_gradients(space, norm_t, branch_r, grad_pre, act, perm_wide, d_up, d_down, pieces)
+    grad = complete_gradients(grad, d_down, pieces)
     lead = jnp.arange(8)[:, None]
     extra = jnp.where(lead == 0, loss_local, jnp.where(lead == 1, jnp.sum(weight), 0.0))
     extra = jnp.where(jnp.arange(LANES)[None, :] == 0, extra, 0.0)

time: 579 us -> 494 us (0.85)
  Pallas kernels: 498 us -> 426 us
  local copies, waits for them, and re-layouts: 54.8 us -> 45.2 us
    pallas_call x1, Pallas kernels: 188 us -> 164 us  [exchange(): pl.pallas_call(functools.partial(exchange_kernel, plan), out_shape=(jax.S...]
    pallas_call x2, Pallas kernels: 90.2 us -> 66.4 us  [turn_back(): pl.pallas_call(functools.partial(turn_kernel, prepare), out_shape=jax.Sha...]
    pallas_call x3 -> x2, Pallas kernels: 55.7 us -> 32.2 us  [halo(): pl.pallas_call(functools.partial(halo_kernel, nr, nc, width), out_shape=j...]
    pallas_call x1 -> x2, Pallas kernels: 60.3 us -> 59.8 us  [the longest x1 55.5 us: place_gradients(): pl.pallas_call(functools.partial(place_kernel, nr, nc), out_shape=(jax.Sh...]
    unnamed x81 -> x61, local copies, waits for them, and re-layouts: 12.6 us -> 12.4 us
where the time goes in v3:
time: 494 us; the launch traced here: 487 us
  Pallas kernels  426 us (86%)
  local copies, waits for them, and re-layouts  45.2 us (9%)
  other arithmetic  7.88 us (2%)
  between operations  7.29 us (1%)
    pallas_call x1, Pallas kernels, exchange(): pl.pallas_call(functools.partial(exchange_kernel, plan), out_shape=(jax.S...  164 us
    pallas_call x2, Pallas kernels, turn_back(): pl.pallas_call(functools.partial(turn_kernel, prepare), out_shape=jax.Sha...  66.4 us
    pallas_call x1, Pallas kernels, place_gradients(): pl.pallas_call(functools.partial(place_kernel, nr, nc), out_shape=(jax.Sh...  55.5 us
    pallas_call x1, Pallas kernels, middle_part(): pl.pallas_call(middle_kernel, out_shape=(jax.ShapeDtypeStruct((cells, C1P...  39.7 us
    pallas_call x2, Pallas kernels, halo(): pl.pallas_call(functools.partial(halo_kernel, nr, nc, width), out_shape=j...  32.2 us
    pallas_call x1, Pallas kernels, unpack(): pl.pallas_call(functools.partial(unpack_kernel, plan), out_shape=tuple((j...  30.9 us
    pallas_call x1, Pallas kernels, outer_part(): pl.pallas_call(outer_kernel, out_shape=(jax.ShapeDtypeStruct((C1P // LANE...  27.6 us
    unnamed x61, local copies, waits for them, and re-layouts  12.4 us

profile of v3, /device:TPU:0, one launch (start us, length us, event | category | flops | bytes accessed | tf_op | source)
XLA Modules:
  0.0 486.5 jit_solution(14012586694818117596)
XLA Ops:
  0.7 1.3 fusion.19
  5.9 1.9 constant_dynamic-slice_fusion.1
  8.4 10.0 %shard_map.264.state = bf16[2,10,160,128]{3,2,1,0:T(8,128)(2,1)S(1)} custom-call(bf16[2,8,128,128]{3,2,1,0:T(8,128)(2,1)S(1)} %fusion.4.cells), custom_call_target="tpu_custom_call" | custom-call | tf_op jit(solution)/shard_map/pallas_call | solution.py:1045
  18.7 1.3 copy.37
  20.1 0.7 copy-done.7
  20.8 0.9 reshape.184
  21.7 1.1 pad.85
  22.7 0.6 fusion.16
  23.4 5.1 %shard_map.265 = (bf16[4,512,1152]{2,1,0:T(8,128)(2,1)}, f32[4,512,256]{2,1,0:T(8,128)S(1)}, f32[4,512,256]{2,1,0:T(8,128)S(1)}, f32[512,896]{1,0:T(8,128)S(1)}, bf16[2,4,64,896]{3,2,1,0:T(8,128)(2,1)S(1)}) custom-call(bf16[2,10,160,128]{3,2,1,0:T(8,128)(2,1)S(1)} %shard_map.264.state, bf16[1152,256]{1,0:T(8,128)(2,1)S(1)} %bitcast.57, ...), custom_call_target="tpu_custom_call" | custom-call | tf_op jit(solution)/shard_map/pallas_call | solution.py:1093
  28.4 1.2 copy-done.4
  29.7 22.1 %shard_map.266.padded = bf16[2,10,96,896]{3,2,1,0:T(8,128)(2,1)S(1)} custom-call(bf16[2,4,64,896]{3,2,1,0:T(8,128)(2,1)S(1)} %get-tuple-element.69.cells), custom_call_target="tpu_custom_call" | custom-call | tf_op jit(solution)/shard_map/pallas_call | solution.py:1045
  51.8 1.8 copy-done
  53.6 1.2 copy.56
  55.3 0.9 copy.43
  56.2 0.6 pad.93.b_dw
  56.8 0.6 pad.94.gain
  57.4 0.6 pad.95.shift
  58.0 0.6 pad.96.b_out
  58.6 0.6 fusion.15
  59.6 1.3 broadcast_in_dim.116.weight
  61.0 0.7 bitcast_bitcast_fusion.w_dw
  61.8 0.7 pad.92.w_head
  62.4 0.5 pad.97.b_up
  63.0 1.4 copy.46
  64.4 0.8 copy.47
  65.2 1.5 pad.91.w_up
  66.7 0.6 broadcast_in_dim.120.b_hidden
  67.4 0.5 pad.98.b_head
  67.9 39.7 %shard_map.267 = (bf16[512,896]{1,0:T(8,128)(2,1)}, bf16[512,3200]{1,0:T(8,128)(2,1)}, bf16[512,3200]{1,0:T(8,128)(2,1)}, f32[512,896]{1,0:T(8,128)}, bf16[512,8...) custom-call(bf16[2,10,96,896]{3,2,1,0:T(8,128)(2,1)} %copy-done, ...), custom_call_target="tpu_custom_call" | custom-call | tf_op jit(solution)/shard_map/pallas_call | solution.py:1262
  107.6 0.9 broadcast_in_dim.125.narrow_col
  108.6 0.6 broadcast_in_dim.126.wide
  109.2 0.6 broadcast_in_dim.124.narrow_row
  109.8 55.5 %shard_map.268 = (f32[51632,128]{1,0:T(8,128)}, bf16[2,10,96,896]{3,2,1,0:T(8,128)(2,1)}) custom-call(bf16[512,896]{1,0:T(8,128)(2,1)} %get-tuple-element.72.normed, bf16[512,896]{1,0:T(8,128)(2,1)} %get-tuple-element.73.branch, bf16[512,3200]{1,0:T(8,128)(2,1)} %get-tuple-element.74.pre, bf16[512,3200]{1,0:T(8,128)(2,1)} %get-tuple-element.75.act, ...), custom_call_target="tpu_custom_call" | custom-call | tf_op jit(solution)/shard_map/pallas_call | solution.py:865
  165.3 27.6 %shard_map.269 = (f32[7,56,128]{2,1,0:T(8,128)}, f32[800,896]{1,0:T(8,128)}, f32[1152,256]{1,0:T(8,128)}, f32[8,896]{1,0:T(8,128)}) custom-call(bf16[2,10,96,896]{3,2,1,0:T(8,128)(2,1)} %copy-done, bf16[2,10,96,896]{3,2,1,0:T(8,128)(2,1)} %get-tuple-element.79.grad_padded, bf16[2,4,64,896]{3,2,1,0:T(8,128)(2,1)} %get-tuple-element.77.cells.grad_conv, ...), custom_call_target="tpu_custom_call" | custom-call | tf_op jit(solution)/shard_map/pallas_call | solution.py:1338
  192.9 0.8 slice_reduce_fusion.5
  193.7 0.7 slice.135
  194.4 0.9 slice_reduce_fusion.1
  195.3 0.9 slice_reduce_fusion
  196.3 0.7 slice.142
  197.0 0.7 slice_bitcast_fusion.1
  197.7 0.6 pad_bitcast_fusion.4.piece_vec
  198.4 1.2 slice.152
  199.6 0.6 reshape_reshape.3
  200.2 0.8 pad.101.piece_in
  201.3 0.7 pad_bitcast_fusion.2.piece_dw
  202.2 0.6 pad_bitcast_fusion.3.piece_head
  202.9 4.3 shard_map.270.grad
  207.2 1.3 slice_reduce_fusion.6
  208.4 1.3 compare_select_fusion.1
  209.8 0.7 broadcast_select_fusion.extra
  210.4 164.4 %shard_map.271 = (bf16[32,1616,128]{2,1,0:T(8,128)(2,1)}, f32[1612,128]{1,0:T(8,128)}, f32[1612,128]{1,0:T(8,128)}, f32[16,128]{1,0:T(8,128)}) custom-call(f32[51632,128]{1,0:T(8,128)} %shard_map.270.grad, f32[1612,128]{1,0:T(8,128)} %bitcast.70, f32[1612,128]{1,0:T(8,128)} %bitcast.71, f32[8,128]{1,0:T(8,128)} %broadcast_select_fusion.extra), custom_call_target="tpu_custom_call" | custom-call | tf_op jit(solution)/shard_map/pallas_call | solution.py:535
  374.9 30.9 %shard_map.272 = (bf16[800,3328]{1,0:T(8,128)(2,1)}, bf16[800,3328]{1,0:T(8,128)(2,1)}, f32[800,800]{1,0:T(8,128)}, f32[800,800]{1,0:T(8,128)}, f32[1096,128]{1,...) custom-call(bf16[32,1616,128]{2,1,0:T(8,128)(2,1)} %get-tuple-element.90.gathered, bf16[800,800]{1,0:T(8,128)(2,1)} %old_up.1, ...), custom_call_target="tpu_custom_call" | custom-call | tf_op jit(solution)/shard_map/pallas_call | solution.py:637
  407.3 33.2 %shard_map.274 = f32[800,3200]{1,0:T(8,128)} custom-call(bf16[800,3328]{1,0:T(8,128)(2,1)} %get-tuple-element.95.packed, s32[4,3328]{1,0:T(4,128)S(1)} %pad_add_fusion.narrow, s32[3200,128]{1,0:T(8,128)S(1)} %broadcast_in_dim.137.wide, bf16[800,3200]{1,0:T(8,128)(2,1)} %bitcast.59), custom_call_target="tpu_custom_call" | custom-call | tf_op jit(solution)/shard_map/pallas_call | solution.py:720
  440.6 0.5 broadcast_in_dim.134.wide
  441.1 33.2 %shard_map.273 = f32[800,3200]{1,0:T(8,128)} custom-call(bf16[800,3328]{1,0:T(8,128)(2,1)} %get-tuple-element.94.packed, s32[1,800]{1,0:T(1,128)S(1)} %broadcast_in_dim.133.narrow, s32[3328,128]{1,0:T(8,128)S(1)} %broadcast_in_dim.134.wide, bf16[800,3200]{1,0:T(8,128)(2,1)} %old.1), custom_call_target="tpu_custom_call" | custom-call | tf_op jit(solution)/shard_map/pallas_call | solution.py:720
  474.5 1.0 mul.59
  475.7 1.1 copy.52
  477.0 0.7 multiply_subtract_fusion.1
  477.7 1.0 slice_multiply_fusion.2
  478.9 0.7 copy.53
  479.7 1.5 fusion.6
  481.1 1.3 fusion.18
  483.1 0.9 copy.64
  484.0 0.9 copy.65
  (98 shorter events, 5.0 us)
Async XLA Ops:
  0.6 17.8 %copy-start.15 = (f32[7677]{0:T(1024)S(1)}, f32[7677]{0:T(1024)}, u32[]{:S(2)}) copy-start(f32[7677]{0:T(1024)} %param.35) | copy-start | bytes 92128
  8.2 10.3 %copy-start.5 = (bf16[800,800]{1,0:T(8,128)(2,1)S(1)}, bf16[800,800]{1,0:T(8,128)(2,1)}, u32[]{:S(2)}) copy-start(bf16[800,800]{1,0:T(8,128)(2,1)} %old_down.1) | copy-start | bytes 3840004
  18.7 33.1 %copy-start.1 = (bf16[4,256,896]{2,1,0:T(8,128)(2,1)}, bf16[4,256,896]{2,1,0:T(8,128)(2,1)S(1)}, u32[]{:S(2)}) copy-start(bf16[4,256,896]{2,1,0:T(8,128)(2,1)S(1)} %pad.87.w_down) | copy-start | bytes 5505028
  20.1 0.7 copy-start.7
  28.4 1.2 copy-start.4
  29.7 23.9 %copy-start.2 = (f32[4,512,256]{2,1,0:T(8,128)}, f32[4,512,256]{2,1,0:T(8,128)S(1)}, u32[]{:S(2)}) copy-start(f32[4,512,256]{2,1,0:T(8,128)S(1)} %get-tuple-element.71.h_zero) | copy-start | bytes 6291460
  29.7 23.9 %copy-start.3 = (f32[4,512,256]{2,1,0:T(8,128)}, f32[4,512,256]{2,1,0:T(8,128)S(1)}, u32[]{:S(2)}) copy-start(f32[4,512,256]{2,1,0:T(8,128)S(1)} %get-tuple-element.82.a_zero) | copy-start | bytes 6291460
  29.7 28.9 %copy-start.21 = (f32[8,128]{1,0:T(8,128)S(1)}, f32[8,128]{1,0:T(8,128)}, u32[]{:S(2)}) copy-start(f32[8,128]{1,0:T(8,128)} %param.24) | copy-start | bytes 12292
  29.7 28.9 %copy-start.22 = (s32[8,128]{1,0:T(8,128)S(1)}, s32[8,128]{1,0:T(8,128)}, u32[]{:S(2)}) copy-start(s32[8,128]{1,0:T(8,128)} %param.23) | copy-start | bytes 12292
  51.8 1.8 copy-start
  53.6 7.4 %copy-start.12 = (bf16[49,800]{1,0:T(8,128)(2,1)S(1)}, bf16[49,800]{1,0:T(8,128)(2,1)}, u32[]{:S(2)}) copy-start(bf16[49,800]{1,0:T(8,128)(2,1)} %param.30) | copy-start | bytes 235204
  53.6 9.4 %copy-start.6 = (bf16[800,800]{1,0:T(8,128)(2,1)S(1)}, bf16[800,800]{1,0:T(8,128)(2,1)}, u32[]{:S(2)}) copy-start(bf16[800,800]{1,0:T(8,128)(2,1)} %old_up.1) | copy-start | bytes 3840004
  53.6 8.1 %copy-start.20 = (bf16[200,77]{0,1:T(8,128)(2,1)S(1)}, bf16[200,77]{0,1:T(8,128)(2,1)}, u32[]{:S(2)}) copy-start(bf16[200,77]{0,1:T(8,128)(2,1)} %param.34) | copy-start | bytes 92404
  53.6 8.8 %copy-start.23 = (f32[200]{0:T(256)S(1)}, f32[200]{0:T(256)}, u32[]{:S(2)}) copy-start(f32[200]{0:T(256)} %get-tuple-element.124) | copy-start | bytes 2404
  64.4 2.3 copy-start.16
  67.9 39.7 %copy-start.19 = (s32[800]{0:T(1024)S(1)}, s32[800]{0:T(1024)}, u32[]{:S(2)}) copy-start(s32[800]{0:T(1024)} %param.26) | copy-start | bytes 9604
  67.9 40.7 %copy-start.17 = (s32[3200]{0:T(1024)S(1)}, s32[3200]{0:T(1024)}, u32[]{:S(2)}) copy-start(s32[3200]{0:T(1024)} %param.27) | copy-start | bytes 38404
  192.9 8.2 %copy-start.13 = (f32[7,56,128]{2,1,0:T(8,128)S(1)}, f32[7,56,128]{2,1,0:T(8,128)}, u32[]{:S(2)}) copy-start(f32[7,56,128]{2,1,0:T(8,128)} %get-tuple-element.86) | copy-start | bytes 602116
  199.5 2.5 copy-start.18
  441.1 33.2 %copy-start.11 = (f32[1096,128]{1,0:T(8,128)S(1)}, f32[1096,128]{1,0:T(8,128)}, u32[]{:S(2)}) copy-start(f32[1096,128]{1,0:T(8,128)} %get-tuple-element.91) | copy-start | bytes 1683460
  441.1 34.5 %copy-start.8 = (bf16[693,200]{1,0:T(8,128)(2,1)S(1)}, bf16[693,200]{1,0:T(8,128)(2,1)}, u32[]{:S(2)}) copy-start(bf16[693,200]{1,0:T(8,128)(2,1)} %copy-done.7) | copy-start | bytes 831604
  474.3 2.5 copy-start.14
  475.6 7.5 %copy-start.10 = (f32[1612,128]{1,0:T(8,128)S(1)}, f32[1612,128]{1,0:T(8,128)}, u32[]{:S(2)}) copy-start(f32[1612,128]{1,0:T(8,128)} %get-tuple-element.98) | copy-start | bytes 2476036
  475.7 8.3 %copy-start.9 = (f32[1612,128]{1,0:T(8,128)S(1)}, f32[1612,128]{1,0:T(8,128)}, u32[]{:S(2)}) copy-start(f32[1612,128]{1,0:T(8,128)} %get-tuple-element.99) | copy-start | bytes 2476036

commit v4 on v3

--- a/solution.py
+++ b/solution.py
@@ -275,42 +275,61 @@
     lax.fori_loop(1, nc, gather_far, 0)
 
     offset = lax.rem(share * me, 8)
+    low_end, high_end = share * me * LANES, share * (me + 1) * LANES
     for number, (shift_rows, shift_lanes, begin, end) in enumerate(SHIFTS):
         def turn(b, carry, number=number, shift_lanes=shift_lanes):
             at = pl.ds(pl.multiple_of(b * plan.block, plan.block), plan.block)
             rolled[number, at, :] = pltpu.roll(acc[mine, at, :], LANES - shift_lanes, 1)
             return carry
 
-        lax.fori_loop(0, 2 * plan.blocks, turn, 0)
-
-    def share_rows(start, length):
+        @pl.when((low_end < end) & (high_end > begin))
+        def _(turn=turn):
+            lax.fori_loop(0, 2 * plan.blocks, turn, 0)
+
+    def share_rows(start, length, chosen):
         lane = lax.broadcasted_iota(jnp.int32, (length, LANES), 1)
-        line = lax.broadcasted_iota(jnp.int32, (length, LANES), 0)
-        flat = (share * me + start + line) * LANES + lane
         out = jnp.zeros((length, LANES), jnp.float32)
-        for number, (shift_rows, shift_lanes, begin, end) in enumerate(SHIFTS):
+        if len(chosen) > 1:
+            line = lax.broadcasted_iota(jnp.int32, (length, LANES), 0)
+            flat = (share * me + start + line) * LANES + lane
+        for number in chosen:
+            shift_rows, shift_lanes, begin, end = SHIFTS[number]
             here = rolled[number, pl.ds(offset + start + shift_rows, length), :]
             after = rolled[number, pl.ds(offset + start + shift_rows + 1, length), :]
             value = jnp.where(lane < LANES - shift_lanes, here, after)
-            out = jnp.where((flat >= begin) & (flat < end), value, out)
+            if len(chosen) > 1:
+                value = jnp.where((flat >= begin) & (flat < end), value, out)
+            out = value
         return out
 
     chunk = 32
     whole, tail = share // chunk, share % chunk
-
-    def square(b, total):
-        start = pl.multiple_of(b * chunk, chunk)
-        value = share_rows(start, chunk)
-        step[pl.ds(start, chunk), :] = value
-        return total + jnp.sum((value * value).reshape(chunk // 8, 8, LANES), axis=0)
-
-    total = lax.fori_loop(0, whole, square, jnp.zeros((8, LANES), jnp.float32))
     stats[me, 8:16, :] = extra[...]
-    stats[me, 0:8, :] = total
-    if tail:
-        value = share_rows(whole * chunk, tail)
-        step[whole * chunk : share, :] = value
-        stats[me, 0:1, :] += jnp.sum(value * value, axis=0, keepdims=True)
+
+    def squares(chosen):
+        def square(b, total):
+            start = pl.multiple_of(b * chunk, chunk)
+            value = share_rows(start, chunk, chosen)
+            step[pl.ds(start, chunk), :] = value
+            return total + jnp.sum((value * value).reshape(chunk // 8, 8, LANES), axis=0)
+
+        total = lax.fori_loop(0, whole, square, jnp.zeros((8, LANES), jnp.float32))
+        stats[me, 0:8, :] = total
+        if tail:
+            value = share_rows(whole * chunk, tail, chosen)
+            step[whole * chunk : share, :] = value
+            stats[me, 0:1, :] += jnp.sum(value * value, axis=0, keepdims=True)
+
+    largest = max(range(len(SHIFTS)), key=lambda i: SHIFTS[i][3] - SHIFTS[i][2])
+    alone = (low_end >= SHIFTS[largest][2]) & (high_end <= SHIFTS[largest][3])
+
+    @pl.when(alone)
+    def _():
+        squares((largest,))
+
+    @pl.when(jnp.logical_not(alone))
+    def _():
+        squares(tuple(range(len(SHIFTS))))
 
     def stat_copy(target, source):
         return remote(
@@ -340,7 +359,9 @@
 
     sums = lax.fori_loop(0, n, add_stat, jnp.zeros((16, LANES), jnp.float32))
     norm = jnp.sqrt(jnp.sum(sums[0:8], keepdims=True))
-    totals[0:8, :] = sums[8:16]
+    totals[0:1, :] = jnp.broadcast_to(jnp.sum(sums[8:9], keepdims=True), (1, LANES))
+    totals[1:2, :] = jnp.broadcast_to(jnp.sum(sums[9:10], keepdims=True), (1, LANES))
+    totals[2:8, :] = jnp.zeros((6, LANES), jnp.float32)
     totals[8:16, :] = jnp.broadcast_to(norm, (8, LANES))
     clip = jnp.minimum(1.0, clip_limit / norm)
 
@@ -575,21 +596,30 @@
 KEPT = ((8, 1104), (6096, 6408), (51400, 51584))
 PLACES = tuple(divmod(FLAT_AT[i], LANES) for i in (3, 4, 5, 1))
 
-def unpack_kernel(plan, gathered, old_up, old_down, hidden, out, up, down, small_a, small_b, small_c, held, flat, woven, sems):
+SLOTS = 4
+HALF = WIDE // 2
+PITCH = 33
+
+
+def unpack_kernel(
+    plan, gathered, old_up, old_down, wide, hidden_out, rows_out, up_out, down_out, small_a, small_b, small_c,
+    held, flat, woven, hidden, by_row, rows_low, up, down, sems, sem_out,
+):
     n, share = plan.count, plan.share
     step = CH // LANES
 
     def fetch(k, slot):
         return pltpu.make_async_copy(gathered.at[k], held.at[slot], sems.at[slot])
 
-    fetch(0, 0).start()
+    for k in range(SLOTS - 1):
+        fetch(k, k).start()
 
     def widen(k, carry):
-        slot = lax.rem(k, 2)
-
-        @pl.when(k + 1 < n)
+        slot = lax.rem(k, SLOTS)
+
+        @pl.when(k + SLOTS - 1 < n)
         def _():
-            fetch(k + 1, 1 - slot).start()
+            fetch(k + SLOTS - 1, lax.rem(k + SLOTS - 1, SLOTS)).start()
 
         fetch(k, slot).wait()
 
@@ -603,52 +633,121 @@
 
     lax.fori_loop(0, n, widen, 0)
 
-    for ref, (row, lane) in zip((hidden, out), PLACES):
-        def column(t, carry, ref=ref, row=row):
+    copies = [
+        pltpu.make_async_copy(source, target, sem_out.at[i])
+        for i, (source, target) in enumerate(
+            (
+                (hidden, hidden_out.at[:, pl.ds(0, HALF)]), (rows_low, rows_out), (up, up_out),
+                (down, down_out), (hidden, hidden_out.at[:, pl.ds(HALF, HALF)]),
+            )
+        )
+    ]
+    row, lane = PLACES[0]
+
+    def columns(half):
+        def column(t, carry):
             for begin in range(0, C1, 160):
-                values = flat[pl.ds(row + begin * step + t, 160, stride=step), :]
-                ref[begin : begin + 160, pl.ds(pl.multiple_of(t * LANES, LANES), LANES)] = values.astype(
-                    jnp.bfloat16
-                )
+                at = row + begin * step + half * (HALF // LANES) + t
+                values = flat[pl.ds(at, 160, stride=step), :]
+                at = pl.ds(pl.multiple_of(t * LANES, LANES), LANES)
+                hidden[begin : begin + 160, at] = values.astype(jnp.bfloat16)
             return carry
 
-        lax.fori_loop(0, WIDE // LANES, column, 0)
+        lax.fori_loop(0, HALF // LANES, column, 0)
+
+    columns(0)
+    copies[0].start()
 
     quarter = C1 // 4
-    for ref, old, (row, lane) in zip((up, down), (old_up, old_down), PLACES[2:]):
+    for number, (ref, old, (line, begin)) in enumerate(zip((up, down), (old_up, old_down), PLACES[2:])):
         for u in range(-(-C1 // LANES)):
             width = min(LANES, C1 - u * LANES)
             place = lax.broadcasted_iota(jnp.int32, (quarter, LANES), 1)
             for b in range(4):
-                first, rest = divmod(C1 * b + lane, LANES)
-                here = flat[pl.ds(row + first + u, quarter, stride=step), :]
-                after = flat[pl.ds(row + first + u + 1, quarter, stride=step), :]
+                first, rest = divmod(C1 * b + begin, LANES)
+                here = flat[pl.ds(line + first + u, quarter, stride=step), :]
+                after = flat[pl.ds(line + first + u + 1, quarter, stride=step), :]
                 value = pltpu.roll(jnp.where(place >= rest, here, after), LANES - rest, 1)
                 woven[pl.ds(b, quarter, stride=4), :] = value
             at = slice(u * LANES, u * LANES + width)
             ref[:, at] = moved(old[:, at], woven[:, :width])
+        copies[2 + number].start()
+
     for ref, (begin, end) in zip((small_a, small_b, small_c), KEPT):
         ref[...] = flat[begin:end, :]
-
-
-def unpack(plan, gathered, old_up, old_down):
+    copies[0].wait()
+    columns(1)
+    copies[4].start()
+
+    row, lane = PLACES[1]
+
+    def align(part, carry):
+        place = lax.broadcasted_iota(jnp.int32, (40, LANES), 1)
+        for b in range(4):
+            first, rest = divmod(C1 * b + lane, LANES)
+            values = []
+            for u in range(-(-C1 // LANES)):
+                at = row + part * (40 * step) + first + u
+                here = flat[pl.ds(at, 40, stride=step), :]
+                after = flat[pl.ds(at + 1, 40, stride=step), :]
+                values.append(pltpu.roll(jnp.where(place >= rest, here, after), LANES - rest, 1))
+            for u, value in enumerate(values):
+                flat[pl.ds(part * (40 * PITCH) + b * 8 + u, 40, stride=PITCH), :] = value
+        return carry
+
+    lax.fori_loop(0, C1 // 40, align, 0)
+
+    def scatter(a, carry):
+        for b in range(4):
+            by_row[pl.ds(wide[a * 4 + b] * 9, 8), :] = flat[pl.ds(a * PITCH + b * 8, 8), :]
+        return carry
+
+    lax.fori_loop(0, CH // 4, scatter, 0, unroll=4)
+
+    def by_lane(part, carry):
+        for u in range(C1P // LANES):
+            values = by_row[pl.ds(part * (160 * 9) + u, 160, stride=9), :]
+            at = pl.ds(pl.multiple_of(part * 160, 160), 160)
+            rows_low[at, u * LANES : (u + 1) * LANES] = values.astype(jnp.bfloat16)
+        return carry
+
+    lax.fori_loop(0, CH // 160, by_lane, 0)
+    copies[1].start()
+    for copy in copies[1:]:
+        copy.wait()
+
+
+def unpack(plan, gathered, old_up, old_down, wide):
     lines = PADDED // LANES
     vmem = pl.BlockSpec(memory_space=pltpu.VMEM)
+    hbm = pl.BlockSpec(memory_space=pl.ANY)
+    dma = pltpu.SemaphoreType.DMA
+    f32, low = jnp.float32, jnp.bfloat16
     return pl.pallas_call(
         functools.partial(unpack_kernel, plan),
-        out_shape=tuple(jax.ShapeDtypeStruct((C1, WIDE), jnp.bfloat16) for _ in range(2))
-        + tuple(jax.ShapeDtypeStruct((C1, C1), jnp.float32) for _ in range(2))
-        + tuple(jax.ShapeDtypeStruct((end - begin, LANES), jnp.float32) for begin, end in KEPT),
-        in_specs=[pl.BlockSpec(memory_space=pl.ANY), vmem, vmem],
-        out_specs=tuple([vmem] * 7),
+        out_shape=(
+            jax.ShapeDtypeStruct((C1, WIDE), low),
+            jax.ShapeDtypeStruct((CH, C1P), low),
+            jax.ShapeDtypeStruct((C1, C1), f32),
+            jax.ShapeDtypeStruct((C1, C1), f32),
+        )
+        + tuple(jax.ShapeDtypeStruct((end - begin, LANES), f32) for begin, end in KEPT),
+        in_specs=[hbm, vmem, vmem, pl.BlockSpec(memory_space=pltpu.SMEM)],
+        out_specs=(hbm, hbm, hbm, hbm, vmem, vmem, vmem),
         scratch_shapes=[
-            pltpu.VMEM((2, plan.padded, LANES), jnp.bfloat16),
-            pltpu.VMEM((-(-lines // 8) * 8 + 16, LANES), jnp.float32),
-            pltpu.VMEM((C1, LANES), jnp.float32),
-            pltpu.SemaphoreType.DMA((2,)),
+            pltpu.VMEM((SLOTS, plan.padded, LANES), low),
+            pltpu.VMEM((-(-lines // 8) * 8 + 16, LANES), f32),
+            pltpu.VMEM((C1, LANES), f32),
+            pltpu.VMEM((C1, HALF), low),
+            pltpu.VMEM((CH * 9, LANES), f32),
+            pltpu.VMEM((CH, C1P), low),
+            pltpu.VMEM((C1, C1), f32),
+            pltpu.VMEM((C1, C1), f32),
+            dma((SLOTS,)),
+            dma((5,)),
         ],
-        compiler_params=pltpu.CompilerParams(vmem_limit_bytes=54 << 20),
-    )(gathered, old_up, old_down)
+        compiler_params=pltpu.CompilerParams(vmem_limit_bytes=63 << 20),
+    )(gathered, old_up, old_down, wide)
 
 
 def moved(old, direction):
@@ -696,23 +795,6 @@
     turn = one_hot(lax.broadcasted_iota(jnp.int32, (C1, C1), 0) == narrow[...])
     for begin in range(0, WIDE, 832):
         lines[:, begin : begin + 832] = product(turn, packed[:, begin : begin + 832]).astype(jnp.bfloat16)
-
-
-def quarter_spans(lane):
-    spans = []
-    for b in range(4):
-        begin = (C1 * b + lane) // LANES * LANES
-        end = -(-(C1 * b + lane + C1) // LANES) * LANES
-        spans.append((begin, end))
-    return spans
-
-
-def prepare_out(packed, narrow, lines):
-    for b, (begin, end) in enumerate(quarter_spans(PLACES[1][1])):
-        turn = one_hot(
-            lax.broadcasted_iota(jnp.int32, (C1, end - begin), 0) == narrow[b : b + 1, begin:end]
-        )
-        lines[:, b * C1 : (b + 1) * C1] = product_t(turn, packed[:, begin:end]).astype(jnp.bfloat16)
 
 
 def turn_back(prepare, packed, narrow, wide, old):
@@ -739,18 +821,28 @@
     return turn_back(prepare_hidden, packed, narrow[None, :], shifted, old)
 
 
-def rebuild_out(packed, narrow, wide, old):
-    lane = PLACES[1][1]
-    place = jnp.arange(WIDE)
-    lanes = jnp.full((WIDE,), -1, jnp.int32).at[lane : lane + CH].set(jnp.tile(narrow, 4))
-    table = jnp.stack(
-        [
-            jnp.where((place >= C1 * b + lane) & (place < C1 * (b + 1) + lane), lanes, -1)
-            for b in range(4)
-        ]
-    )
-    order = wide.reshape(C1, 4).T.reshape(-1)
-    return turn_back(prepare_out, packed, table, order, old.T).T
+def out_kernel(rows, narrow, old, new, turn):
+    @pl.when(pl.program_id(0) == 0)
+    def _():
+        turn[...] = one_hot(lax.broadcasted_iota(jnp.int32, (C1, C1), 0) == narrow[...])
+
+    new[...] = moved(old[...], product_t(turn[...], rows[:, :C1]))
+
+
+def rebuild_out(rows, narrow, old):
+    return pl.pallas_call(
+        out_kernel,
+        out_shape=jax.ShapeDtypeStruct((C1, CH), jnp.float32),
+        grid=(CH // TILE,),
+        in_specs=[
+            pl.BlockSpec((TILE, C1P), lambda i: (i, 0)),
+            pl.BlockSpec((1, C1), lambda i: (0, 0)),
+            pl.BlockSpec((C1, TILE), lambda i: (0, i)),
+        ],
+        out_specs=pl.BlockSpec((C1, TILE), lambda i: (0, i)),
+        scratch_shapes=[pltpu.VMEM((C1, C1), jnp.bfloat16)],
+        compiler_params=pltpu.CompilerParams(vmem_limit_bytes=48 << 20),
+    )(rows, narrow[None, :], old.T).T
 
 
 def weave(source, rows, put):
@@ -1056,7 +1148,7 @@
     )(cells)
 
 
-def input_kernel(state, w_in, b_in, w_down, b_down, taps, a_zero, h_zero, coarse, coarse_low, wide):
+def input_kernel(state, w_in, w_down, lines, taps, a_zero, h_zero, coarse, coarse_low, wide):
     batch, rows, breadth, _ = state.shape
     half_h, half_w = (rows - 2) // 2, (breadth - 2 * EDGE) // 2
     for m in range(batch):
@@ -1075,9 +1167,9 @@
                             begin = (m * half_h + i) * half_w
                             tap = (dy * 3 + dx) * CIP
                             taps[sy * 2 + f - dx, begin : begin + half_w, tap : tap + CIP] = line
-    coarse[...] = jnp.broadcast_to(b_down[...], coarse.shape)
+    coarse[...] = jnp.broadcast_to(lines[1:2, :C1P], coarse.shape)
     for s in range(4):
-        value = product(taps[s], w_in[...]) + b_in[...]
+        value = product(taps[s], w_in[...]) + lines[0:1, :C0P]
         a_zero[s] = value
         value = gelu(value)
         h_zero[s] = value
@@ -1085,7 +1177,7 @@
     coarse_low[...] = coarse[...].astype(jnp.bfloat16).reshape(coarse_low.shape)
 
 
-def input_part(state, w_in, b_in, w_down, b_down):
+def input_part(state, w_in, w_down, lines):
     batch, rows, breadth, _ = state.shape
     half_h, half_w = (rows - 2) // 2, (breadth - 2 * EDGE) // 2
     cells = batch * half_h * half_w
@@ -1099,11 +1191,11 @@
             jax.ShapeDtypeStruct((cells, C1P), jnp.float32),
             jax.ShapeDtypeStruct((batch, half_h, half_w, C1P), jnp.bfloat16),
         ),
-        in_specs=[vmem] * 5,
+        in_specs=[vmem] * 4,
         out_specs=tuple([vmem] * 5),
         scratch_shapes=[pltpu.VMEM(state.shape, jnp.float32)],
         compiler_params=pltpu.CompilerParams(vmem_limit_bytes=40 << 20),
-    )(state, w_in, b_in, w_down, b_down)
+    )(state, w_in, w_down, lines)
 
 
 def spread_lanes(padded, held):
@@ -1129,7 +1221,7 @@
                 for i in range(height):
                     if 0 <= y - i < 7:
                         tap = (6 - (y - i)) * 7 + 6 - x if back else (y - i) * 7 + x
-                        sums[i] = sums[i] + window * w_dw[u, pl.ds(tap, 1), :]
+                        sums[i] = sums[i] + window * w_dw[pl.ds(tap, 1), lanes_at(u)]
         for i in range(height):
             put(u, m, i, sums[i])
         return carry
@@ -1148,88 +1240,121 @@
 PART = 640
 
 
-def middle_kernel(
-    padded, coarse, h_zero, target, weight, w_dw, w_hidden, w_out_t, w_up, w_head,
-    b_dw, gain, shift, b_hidden, b_out, b_up, b_head,
-    normed, act, grad_pre, grad_mixed, grad_branch, grad_summed, grad_conv, d_up, d_head, sums,
-    conv, total,
-):
-    cells = coarse.shape[0]
-    batch, rows, breadth, _ = padded.shape
+LATE = ("coarse", "h_zero", "target", "weight", "w_hidden", "w_out_t", "w_up")
+EARLY = ("normed", "act", "grad_mixed", "grad_branch", "grad_summed", "d_up")
+
+
+def middle_kernel(names, *refs):
+    ref = dict(zip(names, refs))
+    batch, rows, breadth, _ = ref["padded"].shape
+    cells = ref["coarse"].shape[0]
     height, half_w = rows - 6, breadth - 2 * EDGE
+    fetch, store, held_in, held_out = {}, {}, {}, {}
+    for i, name in enumerate(LATE):
+        held_in[name] = ref["held_" + name]
+        fetch[name] = pltpu.make_async_copy(ref[name], held_in[name], ref["sem_in"].at[i])
+        fetch[name].start()
+    for i, name in enumerate(EARLY):
+        held_out[name] = ref["held_" + name]
+        store[name] = pltpu.make_async_copy(held_out[name], ref[name], ref["sem_out"].at[i])
+    conv = ref["conv"]
 
     def depthwise(held):
-        spread_lanes(padded, held)
+        spread_lanes(ref["padded"], held)
 
         def put(u, m, i, value):
             conv[rows_at(m, i, height, half_w), lanes_at(u)] = value
 
-        convolve(held, w_dw, put, False)
+        convolve(held, ref["w_dw"], put, False)
 
     pl.run_scoped(depthwise, pltpu.VMEM((C1P // LANES, batch, rows, breadth, LANES), jnp.float32))
     pl.run_scoped(
-        functools.partial(
-            pointwise_kernel, coarse, h_zero, target, weight, w_hidden, w_out_t, w_up, w_head,
-            b_dw, gain, shift, b_hidden, b_out, b_up, b_head,
-            normed, act, grad_pre, grad_mixed, grad_branch, grad_summed, grad_conv, d_up, d_head, sums,
-            conv, total,
-        ),
+        functools.partial(pointwise_part, ref, fetch, store, held_in, held_out),
         pltpu.VMEM((cells, CH), jnp.float32),
         pltpu.VMEM((cells, C1), jnp.bfloat16),
     )
-
-
-def pointwise_kernel(
-    coarse, h_zero, target, weight, w_hidden, w_out_t, w_up, w_head,
-    b_dw, gain, shift, b_hidden, b_out, b_up, b_head,
-    normed, act, grad_pre, grad_mixed, grad_branch, grad_summed, grad_conv, d_up, d_head, sums,
-    conv, total, pre, spread_all,
-):
+    for name in EARLY:
+        store[name].wait()
+
+
+def pointwise_part(ref, fetch, store, held_in, held_out, pre, spread_all):
+    conv, total, sums, extra = ref["conv"], ref["total"], ref["sums"], ref["extra"]
+    gain, w_head = ref["lines"].at[3:4, 0:C1P], ref["w_head"]
+    normed, act = held_out["normed"], held_out["act"]
+    grad_mixed, grad_branch, grad_summed = (
+        held_out[name] for name in ("grad_mixed", "grad_branch", "grad_summed")
+    )
+    w_hidden, w_out_t, w_up = (held_in[name] for name in ("w_hidden", "w_out_t", "w_up"))
+    target, weight, h_zero = (held_in[name] for name in ("target", "weight", "h_zero"))
+    batch, rows, breadth, _ = ref["padded"].shape
+    height, half_w = rows - 6, breadth - 2 * EDGE
+
     inside = lax.broadcasted_iota(jnp.int32, (1, C1P), 1) < C1
-    values = conv[...] + b_dw[...]
+    values = conv[...] + ref["lines"][2:3, :C1P]
     mean = jnp.sum(values, axis=1, keepdims=True) * (1.0 / C1)
     centered = jnp.where(inside, values - mean, 0.0)
     scale = lax.rsqrt(jnp.sum(centered * centered, axis=1, keepdims=True) * (1.0 / C1) + 1e-06)
     conv[...] = centered * scale
-    normed[...] = (conv[...] * gain[...] + shift[...]).astype(jnp.bfloat16)
-
-    total[...] = coarse[...]
+    normed[...] = (conv[...] * gain[...] + ref["lines"][4:5, :C1P]).astype(jnp.bfloat16)
+    store["normed"].start()
+
+    fetch["coarse"].wait()
+    fetch["w_hidden"].wait()
+    fetch["w_out_t"].wait()
+    total[...] = held_in["coarse"][...]
     for begin in range(0, CH, PART):
         span = slice(begin, begin + PART)
-        value = product(normed[:, :C1], w_hidden[:, span]) + b_hidden[:, span]
+        value = product(normed[:, :C1], w_hidden[:, span]) + ref["lines"][5:6, span]
         pre[:, span] = value
         act[:, span] = gelu(value).astype(jnp.bfloat16)
         total[:, :C1] += product_t(act[:, span], w_out_t[:, span])
-    mixed = (total[...] + b_out[...]).astype(jnp.bfloat16)
-
+    store["act"].start()
+    mixed = (total[...] + ref["lines"][6:7, :C1P]).astype(jnp.bfloat16)
+
+    for name in ("h_zero", "target", "weight", "w_up"):
+        fetch[name].wait()
     grad_mixed[...] = jnp.zeros_like(grad_mixed)
-    loss = jnp.zeros((1, CIP), jnp.float32)
-    head_sum = jnp.zeros((1, CIP), jnp.float32)
-    up_sum = jnp.zeros((1, C0P), jnp.float32)
+    loss = jnp.zeros((1, CI), jnp.float32)
+    head_sum = jnp.zeros((1, CI), jnp.float32)
+    up_sum = jnp.zeros((1, C0), jnp.float32)
     for s in range(4):
-        upper = product(mixed[:, :C1], w_up[s]) + b_up[...]
-        summed = (upper + h_zero[s]).astype(jnp.bfloat16)
-        error = product(summed, w_head[...]) + b_head[...] - target[s].astype(jnp.float32)
-        weighted = weight[s] * error
+        sub_y, sub_x = divmod(s, 2)
+        for m in range(batch):
+            for i in range(height):
+                at = rows_at(m, i, height, half_w)
+                line = pl.ds(sub_x, half_w, stride=2)
+                ref["goal"][at, :] = target[m, 2 * i + sub_y, line, :]
+                ref["load"][at, :] = weight[2 * i + sub_y, line, :]
+        w_up_s = w_up[:, s * C0 : (s + 1) * C0]
+        upper = product(mixed[:, :C1], w_up_s) + ref["lines"][7:8, :C0]
+        summed = (upper + h_zero[s, :, :C0]).astype(jnp.bfloat16)
+        error = product(summed, w_head[...]) + ref["lines"][8:9, :CI] - ref["goal"][:, :CI]
+        weighted = ref["load"][:, :CI] * error
         loss = loss + column_sum(weighted * error)
         grad_out = (2.0 * weighted).astype(jnp.bfloat16)
         head_sum = head_sum + column_sum(grad_out)
         if s == 0:
-            d_head[...] = inner_rows(summed, grad_out)
+            ref["d_head"][...] = inner_rows(summed, grad_out)
         else:
-            d_head[...] += inner_rows(summed, grad_out)
+            ref["d_head"][...] += inner_rows(summed, grad_out)
         spread = product_t(grad_out, w_head[...])
         grad_summed[s] = spread
         grad_upper = spread.astype(jnp.bfloat16)
         up_sum = up_sum + column_sum(grad_upper)
-        spread_all[:, s * C0 : (s + 1) * C0] = grad_upper[:, :C0]
-        grad_mixed[:, :C1] += product_t(grad_upper, w_up[s])
-    d_up[...] = inner_rows(mixed, spread_all[...])
+        spread_all[:, s * C0 : (s + 1) * C0] = grad_upper
+        grad_mixed[:, :C1] += product_t(grad_upper, w_up_s)
+    store["grad_summed"].start()
+    store["grad_mixed"].start()
+    held_out["d_up"][...] = inner_rows(mixed[:, :C1], spread_all[...])
+    store["d_up"].start()
     grad_branch[...] = grad_mixed[...].astype(jnp.bfloat16)
+    store["grad_branch"].start()
     sums[...] = jnp.zeros_like(sums)
-    sums[0:1, 0:CIP] = loss
-    sums[1:2, 0:CIP] = head_sum
-    sums[2:3, 0:C0P] = up_sum
+    extra[...] = jnp.zeros_like(extra)
+    extra[0:1, 0:CI] = loss
+    extra[1:2, :] = column_sum(ref["weight_map"][...])
+    sums[1:2, 0:CI] = head_sum
+    sums[2:3, 0:C0] = up_sum
     sums[3:4, 0:C1P] = column_sum(grad_branch[...])
 
     total[...] = jnp.zeros_like(total)
@@ -1237,7 +1362,7 @@
         span = slice(begin, begin + PART)
         value = product(grad_branch[:, :C1], w_out_t[:, span]) * gelu_slope(pre[:, span])
         low = value.astype(jnp.bfloat16)
-        grad_pre[:, span] = low
+        ref["grad_pre"][:, span] = low
         sums[4:5, span] = column_sum(low)
         total[:, :C1] += product_t(low, w_hidden[:, span])
 
@@ -1250,45 +1375,67 @@
     value = scale * jnp.where(inside, inward - first - conv[...] * second, 0.0)
     low = value.astype(jnp.bfloat16)
     sums[7:8, 0:C1P] = column_sum(low)
-    grad_conv[...] = low.reshape(grad_conv.shape)
-
-
-def middle_part(padded, coarse, h_zero, target, weight, *rest):
-    cells = coarse.shape[0]
-    batch, rows, breadth, _ = padded.shape
+    ref["grad_conv"][...] = low.reshape(ref["grad_conv"].shape)
+
+
+def middle_part(**given):
+    cells = given["coarse"].shape[0]
+    batch, rows, breadth, _ = given["padded"].shape
     half_h, half_w = rows - 6, breadth - 2 * EDGE
     vmem = pl.BlockSpec(memory_space=pltpu.VMEM)
+    hbm = pl.BlockSpec(memory_space=pl.ANY)
     f32, low = jnp.float32, jnp.bfloat16
-    return pl.pallas_call(
-        middle_kernel,
-        out_shape=(
-            jax.ShapeDtypeStruct((cells, C1P), low),
-            jax.ShapeDtypeStruct((cells, CH), low),
-            jax.ShapeDtypeStruct((cells, CH), low),
-            jax.ShapeDtypeStruct((cells, C1P), f32),
-            jax.ShapeDtypeStruct((cells, C1P), low),
-            jax.ShapeDtypeStruct((4, cells, C0P), f32),
-            jax.ShapeDtypeStruct((batch, half_h, half_w, C1P), low),
-            jax.ShapeDtypeStruct((C1P, C1), f32),
-            jax.ShapeDtypeStruct((C0P, CIP), f32),
-            jax.ShapeDtypeStruct((8, CH), f32),
-        ),
-        in_specs=[vmem] * 17,
-        out_specs=tuple([vmem] * 10),
-        scratch_shapes=[
-            pltpu.VMEM((cells, C1P), f32),
-            pltpu.VMEM((cells, C1P), f32),
-        ],
+    outs = {
+        "normed": ((cells, C1P), low),
+        "act": ((cells, CH), low),
+        "grad_pre": ((cells, CH), low),
+        "grad_mixed": ((cells, C1P), f32),
+        "grad_branch": ((cells, C1P), low),
+        "grad_summed": ((4, cells, C0), f32),
+        "grad_conv": ((batch, half_h, half_w, C1P), low),
+        "d_up": ((C1, C1), f32),
+        "d_head": ((C0, CI), f32),
+        "sums": ((8, CH), f32),
+        "extra": ((8, LANES), f32),
+    }
+    scratch = {
+        "conv": pltpu.VMEM((cells, C1P), f32),
+        "total": pltpu.VMEM((cells, C1P), f32),
+        "goal": pltpu.VMEM((cells, LANES), f32),
+        "load": pltpu.VMEM((cells, LANES), f32),
+        "sem_in": pltpu.SemaphoreType.DMA((len(LATE),)),
+        "sem_out": pltpu.SemaphoreType.DMA((len(EARLY),)),
+    }
+    for name in LATE:
+        scratch["held_" + name] = pltpu.VMEM(given[name].shape, given[name].dtype)
+    for name in EARLY:
+        scratch["held_" + name] = pltpu.VMEM(*outs[name])
+    found = pl.pallas_call(
+        functools.partial(middle_kernel, tuple(given) + tuple(outs) + tuple(scratch)),
+        out_shape=tuple(jax.ShapeDtypeStruct(*out) for out in outs.values()),
+        in_specs=[hbm if name in LATE else vmem for name in given],
+        out_specs=tuple(hbm if name in EARLY else vmem for name in outs),
+        scratch_shapes=list(scratch.values()),
         compiler_params=pltpu.CompilerParams(vmem_limit_bytes=62 << 20),
-    )(padded, coarse, h_zero, target, weight, *rest)
-
-
-def outer_kernel(
-    padded, grad_padded, grad_conv, grad_mixed, grad_summed, a_zero, h_zero, taps, w_dw, w_down,
-    d_dw, d_down, d_in, sums, held, conv,
-):
+    )(*given.values())
+    return dict(zip(outs, found))
+
+
+AFTER = ("grad_mixed", "grad_summed", "a_zero", "h_zero", "taps", "w_down")
+
+
+def outer_kernel(names, *refs):
+    ref = dict(zip(names, refs))
+    fetch = {}
+    for i, name in enumerate(AFTER):
+        fetch[name] = pltpu.make_async_copy(ref[name], ref["held_" + name], ref["sem_in"].at[i])
+        fetch[name].start()
+    grad_mixed, grad_summed, a_zero, h_zero, taps, w_down = (ref["held_" + name] for name in AFTER)
+    held, conv, sums, d_dw, d_in = (ref[name] for name in ("held", "conv", "sums", "d_dw", "d_in"))
+    vector = ref["vector"]
+    grad_conv = ref["grad_conv"]
     batch, height, half_w, _ = grad_conv.shape
-    spread_lanes(padded, held)
+    spread_lanes(ref["padded"], held)
     tiles = C1P // LANES
     d_dw[...] = jnp.zeros_like(d_dw)
 
@@ -1304,53 +1451,69 @@
                         term = (window * grads[i]).reshape(half_w // 8, 8, LANES)
                         found[y - i] = found[y - i] + jnp.sum(term, axis=0)
             for dy in range(7):
-                d_dw[u, pl.ds(dy * 7 + x, 1), :] += jnp.sum(found[dy], axis=0, keepdims=True)
+                d_dw[pl.ds(dy * 7 + x, 1), lanes_at(u)] += jnp.sum(found[dy], axis=0, keepdims=True)
         return carry
 
     lax.fori_loop(0, tiles * batch, taps_of, 0)
-    spread_lanes(grad_padded, held)
+    spread_lanes(ref["grad_padded"], held)
 
     def put(u, m, i, value):
         conv[rows_at(m, i, height, half_w), lanes_at(u)] = value
 
-    convolve(held, w_dw, put, True)
+    convolve(held, ref["w_dw"], put, True)
+    for name in AFTER:
+        fetch[name].wait()
     grad_coarse = (conv[...] + grad_mixed[...]).astype(jnp.bfloat16)
-    sums[...] = jnp.zeros_like(sums)
-    sums[0:1, 0:C1P] = column_sum(grad_coarse)
-    in_sum = jnp.zeros((1, C0P), jnp.float32)
+    vector[...] = jnp.zeros_like(vector)
+    pieces = [(column_sum(grad_coarse), C1)] + [(sums[i : i + 1, :], C1) for i in (7, 5, 6)]
+    pieces += [(sums[4:5, :], CH), (sums[3:4, :], C1), (sums[2:3, :], C0), (sums[1:2, :], CI)]
+    start = C0
+    for piece, size in pieces:
+        vector[:, start : start + size] = piece[:, :size]
+        start = start + size
+    in_sum = jnp.zeros((1, C0), jnp.float32)
     for s in range(4):
-        d_down[s * C0 : (s + 1) * C0, :] = inner_rows(h_zero[s].astype(jnp.bfloat16), grad_coarse)[:C0]
-        grad_h = product_t(grad_coarse, w_down[s]) + grad_summed[s]
-        grad_a = (gelu_slope(a_zero[s]) * grad_h).astype(jnp.bfloat16)
+        ref["d_down"][s * C0 : (s + 1) * C0, :] = inner_rows(
+            h_zero[s].astype(jnp.bfloat16), grad_coarse
+        )[:C0]
+        grad_h = product_t(grad_coarse, w_down[s])[:, :C0] + grad_summed[s]
+        grad_a = (gelu_slope(a_zero[s, :, :C0]) * grad_h).astype(jnp.bfloat16)
         in_sum = in_sum + column_sum(grad_a)
         if s == 0:
             d_in[...] = inner_rows(taps[s], grad_a)
         else:
             d_in[...] += inner_rows(taps[s], grad_a)
-    sums[1:2, 0:C0P] = in_sum
-
-
-def outer_part(padded, grad_padded, grad_conv, grad_mixed, grad_summed, a_zero, h_zero, taps, w_dw, w_down):
-    cells = grad_mixed.shape[0]
-    batch, rows, breadth, _ = padded.shape
+    vector[:, 0:C0] = in_sum
+
+
+def outer_part(length, **given):
+    cells = given["grad_mixed"].shape[0]
+    batch, rows, breadth, _ = given["padded"].shape
     vmem = pl.BlockSpec(memory_space=pltpu.VMEM)
+    hbm = pl.BlockSpec(memory_space=pl.ANY)
     f32 = jnp.float32
-    return pl.pallas_call(
-        outer_kernel,
-        out_shape=(
-            jax.ShapeDtypeStruct((C1P // LANES, 56, LANES), f32),
-            jax.ShapeDtypeStruct((C1, C1P), f32),
-            jax.ShapeDtypeStruct((9 * CIP, C0P), f32),
-            jax.ShapeDtypeStruct((8, C1P), f32),
-        ),
-        in_specs=[vmem] * 10,
-        out_specs=tuple([vmem] * 4),
-        scratch_shapes=[
-            pltpu.VMEM((C1P // LANES, batch, rows, breadth, LANES), f32),
-            pltpu.VMEM((cells, C1P), f32),
-        ],
-        compiler_params=pltpu.CompilerParams(vmem_limit_bytes=62 << 20),
-    )(padded, grad_padded, grad_conv, grad_mixed, grad_summed, a_zero, h_zero, taps, w_dw, w_down)
+    outs = {
+        "d_dw": ((56, C1P), f32),
+        "d_down": ((C1, C1P), f32),
+        "d_in": ((9 * CIP, C0), f32),
+        "vector": ((1, length), f32),
+    }
+    scratch = {
+        "held": pltpu.VMEM((C1P // LANES, batch, rows, breadth, LANES), f32),
+        "conv": pltpu.VMEM((cells, C1P), f32),
+        "sem_in": pltpu.SemaphoreType.DMA((len(AFTER),)),
+    }
+    for name in AFTER:
+        scratch["held_" + name] = pltpu.VMEM(given[name].shape, given[name].dtype)
+    found = pl.pallas_call(
+        functools.partial(outer_kernel, tuple(given) + tuple(outs) + tuple(scratch)),
+        out_shape=tuple(jax.ShapeDtypeStruct(*out) for out in outs.values()),
+        in_specs=[hbm if name in AFTER else vmem for name in given],
+        out_specs=tuple([vmem] * len(outs)),
+        scratch_shapes=list(scratch.values()),
+        compiler_params=pltpu.CompilerParams(vmem_limit_bytes=60 << 20),
+    )(*given.values())
+    return dict(zip(outs, found))
 
 
 def split_vector(vector):
@@ -1392,7 +1555,6 @@
     moment_second,
 ):
     rows, cols = lax.axis_size("rows"), lax.axis_size("cols")
-    b_in, b_down, b_dw, gain, shift, b_hidden, b_out, b_up, b_head = split_vector(biases_gains)
     weight = land_mask.astype(jnp.float32) * volume
     height, breadth = weight.shape
     half_h, half_w = (height // 2, breadth // 2)
@@ -1405,72 +1567,50 @@
         )
         return widened(picked, MB, height, breadth, CIP)
 
-    def by_subcell(field):
-        chans = field.shape[-1]
-        return (
-            field.reshape(MB, half_h, 2, half_w, 2, chans)
-            .transpose(2, 4, 0, 1, 3, 5)
-            .reshape(4, cells, chans)
-        )
-
-    def line(vector, size):
-        return widened(vector[None, :], 1, size)
-
+    lines = jnp.stack([widened(piece, CH) for piece in split_vector(biases_gains)])
     w_in_p = widened(w_in.reshape(9, CI, C0), 9, CIP, C0P).reshape(9 * CIP, C0P)
     w_down_p = widened(w_down.reshape(4, C0, C1), 4, C0P, C1P)
-    w_up_p = widened(w_up.reshape(C1, 4, C0).transpose(1, 0, 2), 4, C1, C0P)
-    w_dw_p = widened(w_dw.astype(jnp.float32), 56, C1P).reshape(56, C1P // LANES, LANES).transpose(1, 0, 2)
-    target = by_subcell(dates(targets))
-    weight_col = jnp.broadcast_to(weight[None, :, :, None], (MB, height, breadth, 1))
-    weight_col = jnp.broadcast_to(by_subcell(weight_col), (4, cells, CIP))
+    w_dw_p = widened(w_dw.astype(jnp.float32), 56, C1P)
+    weight_map = jnp.broadcast_to(weight[:, :, None], (height, breadth, LANES))
 
     state = halo(rows, cols, 1, dates(inputs), 1)
     taps, a_zero, h_zero, coarse, coarse_low = input_part(
-        state, w_in_p, line(b_in, C0P), w_down_p, line(b_down, C1P)
+        state, w_in_p, w_down_p, lines
     )
     padded = halo(rows, cols, 3, coarse_low, 2)
-    (
-        normed, act, grad_pre, grad_mixed, grad_branch, grad_summed, grad_conv, d_up, d_head, sums
-    ) = middle_part(
-        padded, coarse, h_zero, target, weight_col, w_dw_p, w_hidden, w_out.T, w_up_p,
-        widened(w_head, C0P, CIP), line(b_dw, C1P), line(gain, C1P), line(shift, C1P),
-        line(b_hidden, CH), line(b_out, C1P), line(b_up, C0P), line(b_head, CIP),
+    mid = middle_part(
+        padded=padded, coarse=coarse, h_zero=h_zero, target=dates(targets).astype(jnp.float32),
+        weight=weight_map, weight_map=weight, w_dw=w_dw_p, w_hidden=w_hidden, w_out_t=w_out.T,
+        w_up=w_up, w_head=w_head, lines=lines,
     )
     space = Plan(rows, cols, PADDED).space
     grad, grad_padded = place_gradients(
-        rows, cols, space, normed, grad_branch, grad_pre, act, perm_narrow, perm_wide, d_up, grad_conv
+        rows, cols, space, mid["normed"], mid["grad_branch"], mid["grad_pre"], mid["act"],
+        perm_narrow, perm_wide, mid["d_up"], mid["grad_conv"],
     )
-    d_dw, d_down, d_in, sums_out = outer_part(
-        padded, grad_padded, grad_conv, grad_mixed, grad_summed, a_zero, h_zero, taps, w_dw_p, w_down_p
+    out = outer_part(
+        (space - ROW_AT[7]) * LANES,
+        padded=padded, grad_padded=grad_padded, grad_conv=mid["grad_conv"],
+        grad_mixed=mid["grad_mixed"], grad_summed=mid["grad_summed"], a_zero=a_zero, h_zero=h_zero,
+        taps=taps, w_dw=w_dw_p, w_down=w_down_p, sums=mid["sums"],
     )
-    d_in = d_in.reshape(9, CIP, C0P)[:, :CI, :C0].reshape(9 * CI, C0)
-    d_dw = d_dw[:, :49].transpose(1, 0, 2).reshape(49, C1P)[:, :C1]
-    d_vector = jnp.concatenate(
-        [
-            sums_out[1, :C0], sums_out[0, :C1], sums[7, :C1], sums[5, :C1], sums[6, :C1],
-            sums[4], sums[3, :C1], sums[2, :C0], sums[1, :CI],
-        ]
-    )
-    loss_local = jnp.sum(sums[0, :CIP])
+    d_in = out["d_in"].reshape(9, CIP, C0)[:, :CI].reshape(9 * CI, C0)
     pieces = (
         jnp.pad(as_rows(d_in, ROW_AT[1] - ROW_AT[0]), ((ROW_AT[0], 0), (0, 0))),
-        as_rows(d_dw, ROW_AT[3] - ROW_AT[2]),
-        as_rows(d_head[:C0, :CI], ROW_AT[7] - ROW_AT[6]),
-        as_rows(d_vector, space - ROW_AT[7]),
+        as_rows(out["d_dw"][:49, :C1], ROW_AT[3] - ROW_AT[2]),
+        as_rows(mid["d_head"], ROW_AT[7] - ROW_AT[6]),
+        out["vector"].reshape(-1, LANES),
     )
-    grad = complete_gradients(grad, d_down, pieces)
-    lead = jnp.arange(8)[:, None]
-    extra = jnp.where(lead == 0, loss_local, jnp.where(lead == 1, jnp.sum(weight), 0.0))
-    extra = jnp.where(jnp.arange(LANES)[None, :] == 0, extra, 0.0)
+    grad = complete_gradients(grad, out["d_down"], pieces)
     plan, (gathered, first, second, totals) = exchange(
-        rows, cols, grad, moment_first, moment_second, extra
+        rows, cols, grad, moment_first, moment_second, mid["extra"]
     )
-    hidden_p, out_p, new_up, new_down, small_a, small_b, small_c = unpack(plan, gathered, w_up, w_down)
+    hidden_p, out_p, new_up, new_down, small_a, small_b, small_c = unpack(plan, gathered, w_up, w_down, perm_wide)
     small = {0: (small_a, 0), 2: (small_b, 1), 6: (small_c, 2), 7: (small_c, 2)}
     whole = {
         1: new_down,
         3: rebuild_hidden(hidden_p, perm_narrow, perm_wide, w_hidden),
-        4: rebuild_out(out_p, perm_narrow, perm_wide, w_out),
+        4: rebuild_out(out_p, perm_narrow, w_out),
         5: new_up,
     }
     olds = matrices + (biases_gains,)

time: 494 us -> 442 us (0.89)
  Pallas kernels: 426 us -> 396 us
  local copies, waits for them, and re-layouts: 45.2 us -> 28 us
    pallas_call x2 -> x1, Pallas kernels: 66.4 us -> 33.4 us  [turn_back(): pl.pallas_call(functools.partial(turn_kernel, prepare), out_shape=jax.Sha...]
    pallas_call x3 -> x4, Pallas kernels: 98.3 us -> 107 us  [the longest x1 36.8 us: middle_part(): pl.pallas_call(functools.partial(middle_kernel, tuple(given) + tuple(outs...]
    pallas_call x1, Pallas kernels: 164 us -> 159 us  [exchange(): pl.pallas_call(functools.partial(exchange_kernel, plan), out_shape=(jax.S...]
    unnamed x61 -> x72, local copies, waits for them, and re-layouts: 12.4 us -> 9.89 us
where the time goes in v4:
time: 442 us; the launch traced here: 436 us
  Pallas kernels  396 us (90%)
  local copies, waits for them, and re-layouts  28 us (6%)
  between operations  7.33 us (2%)
    pallas_call x1, Pallas kernels, exchange(): pl.pallas_call(functools.partial(exchange_kernel, plan), out_shape=(jax.S...  159 us
    pallas_call x1, Pallas kernels, place_gradients(): pl.pallas_call(functools.partial(place_kernel, nr, nc), out_shape=(jax.Sh...  55.3 us
    pallas_call x1, Pallas kernels, middle_part(): pl.pallas_call(functools.partial(middle_kernel, tuple(given) + tuple(outs...  36.8 us
    pallas_call x1, Pallas kernels, unpack(): pl.pallas_call(functools.partial(unpack_kernel, plan), out_shape=(jax.Sha...  34.3 us
    pallas_call x1, Pallas kernels, turn_back(): pl.pallas_call(functools.partial(turn_kernel, prepare), out_shape=jax.Sha...  33.4 us
    pallas_call x2, Pallas kernels, halo(): pl.pallas_call(functools.partial(halo_kernel, nr, nc, width), out_shape=j...  32.2 us
    pallas_call x1, Pallas kernels, outer_part(): pl.pallas_call(functools.partial(outer_kernel, tuple(given) + tuple(outs)...  24.7 us
    pallas_call x1, Pallas kernels, rebuild_out(): pl.pallas_call(out_kernel, out_shape=jax.ShapeDtypeStruct((C1, CH), jnp.f...  11.2 us

profile of v4, /device:TPU:0, one launch (start us, length us, event | category | flops | bytes accessed | tf_op | source)
XLA Modules:
  0.0 435.6 jit_solution(5952772810851828271)
XLA Ops:
  0.6 0.0 copy-start.28
  0.7 0.0 copy-start.15
  0.7 1.3 fusion.11
  5.9 1.9 constant_dynamic-slice_fusion.1
  7.7 0.2 copy.47
  8.0 0.2 copy.48
  8.2 0.2 fusion.4.cells
  8.4 10.0 %shard_map.264.state = bf16[2,10,160,128]{3,2,1,0:T(8,128)(2,1)S(1)} custom-call(bf16[2,8,128,128]{3,2,1,0:T(8,128)(2,1)S(1)} %fusion.4.cells), custom_call_target="tpu_custom_call" | custom-call | tf_op jit(solution)/shard_map/pallas_call | solution.py:1137
  18.5 0.1 fusion.8
  18.7 0.1 fusion.9
  18.8 0.1 slice.83
  18.9 0.1 slice.84
  19.0 1.5 stack.39.lines.refs_11_
  20.4 1.5 pad.71.w_down.refs_9_
  22.0 0.2 copy.37
  22.2 0.1 reshape.119
  22.3 0.1 pad.70
  22.4 1.2 copy-done.4
  23.6 5.0 %shard_map.265 = (bf16[4,512,1152]{2,1,0:T(8,128)(2,1)}, f32[4,512,256]{2,1,0:T(8,128)S(1)}, f32[4,512,256]{2,1,0:T(8,128)S(1)}, f32[512,896]{1,0:T(8,128)S(1)}, bf16[2,4,64,896]{3,2,1,0:T(8,128)(2,1)S(1)}) custom-call(bf16[2,10,160,128]{3,2,1,0:T(8,128)(2,1)S(1)} %shard_map.264.state, bf16[1152,256]{1,0:T(8,128)(2,1)S(1)} %bitcast.29, ...), custom_call_target="tpu_custom_call" | custom-call | tf_op jit(solution)/shard_map/pallas_call | solution.py:1185
  28.6 1.3 copy-done.5
  29.9 22.2 %shard_map.266.refs_0_ = bf16[2,10,96,896]{3,2,1,0:T(8,128)(2,1)S(1)} custom-call(bf16[2,4,64,896]{3,2,1,0:T(8,128)(2,1)S(1)} %get-tuple-element.58.cells), custom_call_target="tpu_custom_call" | custom-call | tf_op jit(solution)/shard_map/pallas_call | solution.py:1137
  52.1 1.8 copy-done
  53.9 0.2 copy.49
  54.1 0.2 copy.50
  54.3 1.2 fusion.6.refs_3_
  55.5 1.0 broadcast_in_dim.12.refs_4_
  56.5 0.7 pad.81.refs_6_.refs_8_
  57.2 0.7 copy.43.refs_10_
  58.0 36.8 %shard_map.267 = (bf16[512,896]{1,0:T(8,128)(2,1)}, bf16[512,3200]{1,0:T(8,128)(2,1)}, bf16[512,3200]{1,0:T(8,128)(2,1)}, f32[512,896]{1,0:T(8,128)}, bf16[512,8...) custom-call(bf16[2,10,96,896]{3,2,1,0:T(8,128)(2,1)} %copy-done, ...), custom_call_target="tpu_custom_call" | custom-call | tf_op jit(solution)/shard_map/pallas_call | solution.py:1413
  94.8 0.9 broadcast_in_dim.14.narrow_col
  95.7 0.6 broadcast_in_dim.15.wide
  96.3 0.6 broadcast_in_dim.13.narrow_row
  96.9 55.3 %shard_map.268 = (f32[51632,128]{1,0:T(8,128)}, bf16[2,10,96,896]{3,2,1,0:T(8,128)(2,1)}) custom-call(bf16[512,896]{1,0:T(8,128)(2,1)} %get-tuple-element.61.normed, bf16[512,896]{1,0:T(8,128)(2,1)} %get-tuple-element.62.branch, bf16[512,3200]{1,0:T(8,128)(2,1)} %get-tuple-element.63.pre, bf16[512,3200]{1,0:T(8,128)(2,1)} %get-tuple-element.64.act, ...), custom_call_target="tpu_custom_call" | custom-call | tf_op jit(solution)/shard_map/pallas_call | solution.py:957
  152.2 24.7 %shard_map.269 = (f32[56,896]{1,0:T(8,128)}, f32[800,896]{1,0:T(8,128)}, f32[1152,200]{1,0:T(8,128)}, f32[1,11264]{1,0:T(1,128)}) custom-call(bf16[2,10,96,896]{3,2,1,0:T(8,128)(2,1)} %copy-done, bf16[2,10,96,896]{3,2,1,0:T(8,128)(2,1)} %get-tuple-element.68.refs_1_, bf16[2,4,64,896]{3,2,1,0:T(8,128)(2,1)} %get-tuple-element.66.cells.refs_2_, ...), custom_call_target="tpu_custom_call" | custom-call | tf_op jit(solution)/shard_map/pallas_call | solution.py:1508
  176.9 1.2 slice.94
  178.2 0.6 reshape_reshape.3
  178.8 0.8 pad.84.piece_in
  179.7 0.1 reshape.124
  179.8 0.7 pad_bitcast_fusion.1.piece_dw
  180.5 0.2 reshape.126
  180.7 0.6 pad_bitcast_fusion.2.piece_head
  181.3 4.3 shard_map.270.grad
  185.6 158.8 %shard_map.271 = (bf16[32,1616,128]{2,1,0:T(8,128)(2,1)}, f32[1612,128]{1,0:T(8,128)}, f32[1612,128]{1,0:T(8,128)}, f32[16,128]{1,0:T(8,128)}) custom-call(f32[51632,128]{1,0:T(8,128)} %shard_map.270.grad, f32[1612,128]{1,0:T(8,128)} %bitcast.34, f32[1612,128]{1,0:T(8,128)} %bitcast.35, f32[8,128]{1,0:T(8,128)} %get-tuple-element.79.extra), custom_call_target="tpu_custom_call" | custom-call | tf_op jit(solution)/shard_map/pallas_call | solution.py:556
  344.4 0.0 slice-start
  344.4 34.3 %shard_map.272 = (bf16[800,3328]{1,0:T(8,128)(2,1)}, bf16[3200,896]{1,0:T(8,128)(2,1)}, f32[800,800]{1,0:T(8,128)}, f32[800,800]{1,0:T(8,128)}, f32[1096,128]{1,...) custom-call(bf16[32,1616,128]{2,1,0:T(8,128)(2,1)} %get-tuple-element.80.gathered, bf16[800,800]{1,0:T(8,128)(2,1)} %old_up.1, ...), custom_call_target="tpu_custom_call" | custom-call | tf_op jit(solution)/shard_map/pallas_call | solution.py:726
  378.7 0.1 scatter.4
  378.8 0.5 broadcast_in_dim.34.wide
  379.3 0.0 slice-start.1
  379.3 33.4 %shard_map.273 = f32[800,3200]{1,0:T(8,128)} custom-call(bf16[800,3328]{1,0:T(8,128)(2,1)} %get-tuple-element.84.packed, s32[1,800]{1,0:T(1,128)S(1)} %broadcast_in_dim.16.narrow, s32[3328,128]{1,0:T(8,128)S(1)} %broadcast_in_dim.34.wide, bf16[800,3200]{1,0:T(8,128)(2,1)} %old.1), custom_call_target="tpu_custom_call" | custom-call | tf_op jit(solution)/shard_map/pallas_call | solution.py:802
  412.7 11.2 %shard_map.274 = f32[800,3200]{1,0:T(8,128)} custom-call(bf16[3200,896]{1,0:T(8,128)(2,1)} %get-tuple-element.85.rows, s32[1,800]{1,0:T(1,128)S(1)} %broadcast_in_dim.16.narrow, bf16[800,3200]{1,0:T(8,128)(2,1)S(1)} %bitcast.28), custom_call_target="tpu_custom_call" | custom-call | tf_op jit(solution)/shard_map/pallas_call | solution.py:833
  423.9 0.2 slice_multiply_fusion
  424.2 1.0 mul.59
  425.2 1.1 multiply_subtract_fusion
  426.4 1.1 copy.45
  427.5 0.1 slice_multiply_fusion.1
  427.6 0.1 mul.64
  427.7 0.7 multiply_subtract_fusion.1
  428.5 0.1 slice_multiply_fusion.2
  428.5 0.2 mul.69
  428.8 0.7 copy.46
  429.5 0.7 fusion.7
  430.2 1.3 fusion.10
  432.2 0.9 copy.54
  433.1 0.9 copy.55
  (77 shorter events, 0.3 us)
Async XLA Ops:
  0.6 18.0 %copy-start.28 = (pred[3200]{0:T(1024)(128)(4,1)S(1)}, pred[3200]{0:T(1024)(128)(4,1)}, u32[]{:S(2)}) copy-start(pred[3200]{0:T(1024)(128)(4,1)} %constant.46.clone.1) | copy-start | bytes 9604
  0.7 17.8 %copy-start.15 = (f32[7677]{0:T(1024)S(1)}, f32[7677]{0:T(1024)}, u32[]{:S(2)}) copy-start(f32[7677]{0:T(1024)} %param.33) | copy-start | bytes 92128
  8.4 13.6 %copy-start.14 = (bf16[693,200]{0,1:T(8,128)(2,1)S(1)}, bf16[693,200]{0,1:T(8,128)(2,1)}, u32[]{:S(2)}) copy-start(bf16[693,200]{0,1:T(8,128)(2,1)} %param.26) | copy-start | bytes 831604
  22.0 6.6 %copy-start.1 = (bf16[4,256,896]{2,1,0:T(8,128)(2,1)}, bf16[4,256,896]{2,1,0:T(8,128)(2,1)S(1)}, u32[]{:S(2)}) copy-start(bf16[4,256,896]{2,1,0:T(8,128)(2,1)S(1)} %pad.71.w_down.refs_9_) | copy-start | bytes 5505028
  22.1 29.9 %copy-start.6 = (bf16[693,200]{1,0:T(8,128)(2,1)}, bf16[693,200]{1,0:T(8,128)(2,1)S(1)}, u32[]{:S(2)}) copy-start(bf16[693,200]{1,0:T(8,128)(2,1)S(1)} %copy.37) | copy-start | bytes 831604
  22.4 1.2 copy-start.4
  28.6 1.3 copy-start.5
  29.8 22.2 %copy-start.2 = (f32[4,512,256]{2,1,0:T(8,128)}, f32[4,512,256]{2,1,0:T(8,128)S(1)}, u32[]{:S(2)}) copy-start(f32[4,512,256]{2,1,0:T(8,128)S(1)} %get-tuple-element.60.refs_2_.refs_6_) | copy-start | bytes 6291460
  29.8 24.0 %copy-start.3 = (f32[4,512,256]{2,1,0:T(8,128)}, f32[4,512,256]{2,1,0:T(8,128)S(1)}, u32[]{:S(2)}) copy-start(f32[4,512,256]{2,1,0:T(8,128)S(1)} %get-tuple-element.71.refs_5_) | copy-start | bytes 6291460
  29.8 24.0 %copy-start.9 = (bf16[1,8,128,77]{2,1,3,0:T(8,128)(2,1)S(1)}, bf16[1,8,128,77]{2,1,3,0:T(8,128)(2,1)}, u32[]{:S(2)}) copy-start(bf16[1,8,128,77]{2,1,3,0:T(8,128)(2,1)} %get-tuple-element.104) | copy-start | bytes 473092
  29.8 25.7 %copy-start.26 = (f32[8,128]{1,0:T(8,128)S(1)}, f32[8,128]{1,0:T(8,128)}, u32[]{:S(2)}) copy-start(f32[8,128]{1,0:T(8,128)} %param.22) | copy-start | bytes 12292
  29.9 25.7 %copy-start.27 = (s32[8,128]{1,0:T(8,128)S(1)}, s32[8,128]{1,0:T(8,128)}, u32[]{:S(2)}) copy-start(s32[8,128]{1,0:T(8,128)} %param.21) | copy-start | bytes 12292
  29.9 26.7 %copy-start.12 = (bf16[49,800]{1,0:T(8,128)(2,1)S(1)}, bf16[49,800]{1,0:T(8,128)(2,1)}, u32[]{:S(2)}) copy-start(bf16[49,800]{1,0:T(8,128)(2,1)} %param.28) | copy-start | bytes 235204
  29.9 27.3 %copy-start.23 = (bf16[200,77]{0,1:T(8,128)(2,1)S(1)}, bf16[200,77]{0,1:T(8,128)(2,1)}, u32[]{:S(2)}) copy-start(bf16[200,77]{0,1:T(8,128)(2,1)} %param.32) | copy-start | bytes 92404
  52.1 1.8 copy-start
  55.5 2.4 copy-start.24
  58.0 36.8 %copy-start.25 = (s32[800]{0:T(1024)S(1)}, s32[800]{0:T(1024)}, u32[]{:S(2)}) copy-start(s32[800]{0:T(1024)} %param.24) | copy-start | bytes 9604
  58.0 37.7 %copy-start.19 = (s32[3200]{0:T(1024)S(1)}, s32[3200]{0:T(1024)}, u32[]{:S(2)}) copy-start(s32[3200]{0:T(1024)} %wide.1) | copy-start | bytes 38404
  176.9 2.7 copy-start.17
  176.9 3.6 copy-start.22
  344.4 34.3 %copy-start.20 = (s32[3200]{0:T(1024)S(1)}, s32[3200]{0:T(1024)}, u32[]{:S(2)}) copy-start(s32[3200]{0:T(1024)} %wide.1) | copy-start | bytes 38404
  344.4 68.3 %slice-start = ((s8[5120000]{0:T(1024)(128)(4,1)}), s8[925696]{0:T(1024)(128)(4,1)S(1)}, s32[]{:S(2)}) async-start(s8[5120000]{0:T(1024)(128)(4,1)} %bitcast.26), calls=%async_computation | async-start | bytes 1851392
  379.3 33.4 %slice-start.1 = ((s8[5120000]{0:T(1024)(128)(4,1)}), s8[4194304]{0:T(1024)(128)(4,1)S(1)}, s32[]{:S(2)}) async-start(s8[5120000]{0:T(1024)(128)(4,1)} %bitcast.26), calls=%async_computation.1 | async-start | bytes 8388608
  412.7 11.2 %copy-start.10 = (f32[1096,128]{1,0:T(8,128)S(1)}, f32[1096,128]{1,0:T(8,128)}, u32[]{:S(2)}) copy-start(f32[1096,128]{1,0:T(8,128)} %get-tuple-element.81) | copy-start | bytes 1683460
  423.9 3.5 copy-start.18
  423.9 3.8 copy-start.13
  424.2 4.3 copy-start.21
  424.2 4.6 %copy-start.11 = (bf16[200,77]{1,0:T(8,128)(2,1)S(1)}, bf16[200,77]{1,0:T(8,128)(2,1)}, u32[]{:S(2)}) copy-start(bf16[200,77]{1,0:T(8,128)(2,1)} %copy.43.refs_10_) | copy-start | bytes 92404
  424.2 5.3 %copy-start.16 = (f32[7677]{0:T(1024)S(1)}, f32[7677]{0:T(1024)}, u32[]{:S(2)}) copy-start(f32[7677]{0:T(1024)} %param.33) | copy-start | bytes 92128
  425.2 6.9 %copy-start.8 = (f32[1612,128]{1,0:T(8,128)S(1)}, f32[1612,128]{1,0:T(8,128)}, u32[]{:S(2)}) copy-start(f32[1612,128]{1,0:T(8,128)} %get-tuple-element.88) | copy-start | bytes 2476036
  426.4 6.7 %copy-start.7 = (f32[1612,128]{1,0:T(8,128)S(1)}, f32[1612,128]{1,0:T(8,128)}, u32[]{:S(2)}) copy-start(f32[1612,128]{1,0:T(8,128)} %get-tuple-element.89) | copy-start | bytes 2476036
